TPU v7x, 512 devices: a whole 4x4x16 slice. The times are simulated.
512 devices in a mesh: dp: 32 (over z, y_hi), fsdp: 16 (over x, y_lo, core).
Axes of the slice: x: 4, y: 4 (y_hi: 2, y_lo: 2; y = y_hi * 2 + y_lo), z: 16, core: 2. Of those that a mesh axis runs over, the one named last changes fastest.
Arguments:
- hidden: bfloat16 [65536, 8192], P(('dp', 'fsdp')), may hold values from -6 to 6
- target: bfloat16 [65536, 512], P(('dp', 'fsdp')), may hold values from -6 to 6
- base_weight: bfloat16 [8192, 512], P('fsdp'), may hold values from -0.0625 to 0.0625
- v_factor: float32 [8192, 128], P('fsdp'), may hold values from -0.0625 to 0.0625
- u_factor: float32 [512, 128], replicated, may hold values from -0.25 to 0.25
- sigma: float32 [128], replicated, may hold values from 0.5 to 4
- bits: int32 [128], replicated, may hold values from 2 to 8, as said below
- v_exps: int32 [128], replicated, may hold values from 6 to 9
- u_exps: int32 [128], replicated, may hold values from 4 to 7
Outputs:
- grad_v: float32 [8192, 128], P('fsdp')
- grad_u: float32 [512, 128], replicated
Inputs may be any that keep to these rules, and one draw needn't show every extreme that they name: bits holds 8 for the first few singular vectors, then 3, then 2; it never rises along the vectors and all three widths occur.
All inputs are finite; a program needn't handle non-finite values.
Results may differ from a plain program's by a relative error of at most 0.003.
Values may be sent and summed in bfloat16 or wider, within the bound.
No kernel may reach another device: no remote copies, remote signals or barrier semaphores. Data moves between devices by JAX's collectives and lax.ppermute only.
A program may use at most 64 MiB of HBM per device.

v0:
```python
import math

import jax
import jax.numpy as jnp
from jax import lax
from jax.sharding import PartitionSpec as P


def fake_quantize(factor, bits, scale_exps):
    step = jnp.exp2(-scale_exps.astype(jnp.float32))
    upper = jnp.exp2(bits.astype(jnp.float32) - 1.0)
    ratio = factor / step
    smooth = ratio - jnp.sin(2.0 * math.pi * ratio) / (2.0 * math.pi)
    return step * jnp.clip(smooth, -upper, upper - 1.0)


def shards(hidden, target, base_weight, v_factor, u_factor, sigma, bits, v_exps, u_exps):
    v_quant = fake_quantize(v_factor, bits, v_exps).astype(jnp.bfloat16)
    u_quant = fake_quantize(u_factor, bits, u_exps).astype(jnp.bfloat16)
    tok_rows = hidden.shape[0]

    def add_rows(piece):
        return jnp.dot(hidden, piece, preferred_element_type=jnp.float32)

    low_rank = add_rows(lax.all_gather(v_quant, "fsdp", axis=0, tiled=True))
    base_out = add_rows(lax.all_gather(base_weight, "fsdp", axis=0, tiled=True))
    scaled = (low_rank * sigma).astype(jnp.bfloat16)
    residual = (
        base_out
        + jnp.dot(scaled, u_quant.T, preferred_element_type=jnp.float32)
        - target.astype(jnp.float32)
    )
    tokens_all = tok_rows * lax.axis_size("dp") * lax.axis_size("fsdp")
    out_grad = (residual * (1.0 / math.sqrt(tokens_all))).astype(jnp.bfloat16)
    grad_u_part = jnp.einsum("tk,tr->kr", out_grad, scaled, preferred_element_type=jnp.float32)
    rank_grad = (jnp.dot(out_grad, u_quant, preferred_element_type=jnp.float32) * sigma).astype(
        jnp.bfloat16
    )
    grad_v_part = lax.psum_scatter(
        jnp.einsum("td,tr->dr", hidden, rank_grad, preferred_element_type=jnp.float32),
        "fsdp",
        scatter_dimension=0,
        tiled=True,
    )
    grad_u = lax.psum(grad_u_part, ("dp", "fsdp"))
    grad_v = lax.psum(grad_v_part, "dp")
    return (grad_v, grad_u)


def solution(mesh):
    in_specs = (
        P(("dp", "fsdp"), None),
        P(("dp", "fsdp"), None),
        P("fsdp", None),
        P("fsdp", None),
        P(),
        P(),
        P(),
        P(),
        P(),
    )
    out_specs = (P("fsdp", None), P())
    return jax.shard_map(shards, mesh=mesh, in_specs=in_specs, out_specs=out_specs, check_vma=False)
```

profile of v0, /device:TPU:1, one launch (start us, length us, event | category | flops | bytes accessed | tf_op | source)
XLA Modules:
  0.0 980.1 jit_solution(3150472659456650991)
XLA Ops:
  7.2 0.0 copy-start
  7.2 0.0 all-gather.5.cloned.1.call-start
  7.2 0.8 multiply_exponential_fusion.2
  8.0 0.7 broadcast_add_fusion
  8.7 2.5 multiply_convert_fusion.1
  11.2 0.0 all-gather.5.cloned.1.call-update
  11.3 0.0 all-gather.3.cloned.1.call-start
  11.3 0.7 all-gather.3.cloned.1.call-update
  12.0 0.0 reduce-scatter.2.cloned.1.call-start
  12.1 0.7 multiply_exponential_fusion
  12.7 46.1 %all-gather.5.cloned.1.call-done = bf16[8192,128]{1,0:T(8,128)(2,1)} async-done(((bf16[512,128]{1,0:T(8,128)(2,1)}), bf16[8192,128]{1,0:T(8,128)(2,1)}) %all-gather.5.cloned.1.call-update) | async-done | bytes 2097168 | tf_op jit(solution)/shard_map/all_gather | solution.py:25
  58.8 0.0 copy-done
  58.8 2.3 fusion.3
  61.1 0.0 copy-start.1
  61.1 0.0 copy-start.3
  61.2 0.0 copy-start.2
  61.2 59.7 %all-gather.3.cloned.1.call-done = bf16[8192,512]{1,0:T(8,128)(2,1)} async-done(((bf16[512,512]{1,0:T(8,128)(2,1)}), bf16[8192,512]{1,0:T(8,128)(2,1)}) %all-gather.3.cloned.1.call-update) | async-done | bytes 8388624 | tf_op jit(solution)/shard_map/all_gather | solution.py:26
  120.9 4.6 fusion.7
  125.5 0.0 copy-done.1
  125.5 0.0 copy-done.3
  125.5 1.1 fusion.2
  126.6 0.0 copy-done.2
  126.6 3.7 convolution_bitcast_fusion
  130.4 0.0 reduce-scatter.2.cloned.1.call-update
  130.4 0.0 all-reduce.3.cloned.1.call-start
  130.4 73.0 %reduce-scatter.2.cloned.1.call-done = f32[512,128]{0,1:T(8,128)} async-done(((f32[8192,128]{0,1:T(8,128)}), f32[512,128]{0,1:T(8,128)}) %reduce-scatter.2.cloned.1.call-update) | async-done | bytes 262160 | tf_op jit(solution)/shard_map/reduce_scatter | solution.py:39
  203.5 0.0 all-reduce.3.cloned.1.call-update
  203.5 0.0 all-reduce.5.cloned.1.call-start
  203.6 0.9 fusion.8
  204.5 0.0 all-reduce.5.cloned.1.call-update
  204.5 289.4 %all-reduce.3.cloned.1.call-done = f32[512,128]{0,1:T(8,128)} async-done(((f32[512,128]{0,1:T(8,128)}), f32[512,128]{0,1:T(8,128)}) %all-reduce.3.cloned.1.call-update) | async-done | bytes 262160 | tf_op jit(solution)/shard_map/psum | solution.py:46
  493.9 1.8 copy.11
  495.7 476.2 %all-reduce.5.cloned.1.call-done = f32[512,128]{1,0:T(8,128)} async-done(((f32[512,128]{1,0:T(8,128)}), f32[512,128]{1,0:T(8,128)}) %all-reduce.5.cloned.1.call-update) | async-done | bytes 262160 | tf_op jit(solution)/shard_map/psum | solution.py:45
  971.9 1.7 copy.14
Async XLA Ops:
  7.2 51.6 %copy-start = (bf16[128,8192]{1,0:T(8,128)(2,1)S(1)}, bf16[128,8192]{1,0:T(8,128)(2,1)}, u32[]{:S(2)}) copy-start(bf16[128,8192]{1,0:T(8,128)(2,1)} %param.9) | copy-start | bytes 6291460
  7.2 51.6 %all-gather.5.cloned.1.call-start = ((), (), s32[]{:S(2)}) async-start(), calls=%async_computation.2 | async-start | bytes 2228224 | tf_op jit(solution)/shard_map/all_gather | solution.py:25
  11.3 109.6 %all-gather.3.cloned.1.call-start = ((), (), s32[]{:S(2)}) async-start(), calls=%async_computation.1 | async-start | bytes 8912896 | tf_op jit(solution)/shard_map/all_gather | solution.py:26
  12.0 191.5 %reduce-scatter.2.cloned.1.call-start = ((), (), s32[]{:S(2)}) async-start(), calls=%async_computation.3 | async-start | bytes 4456448 | tf_op jit(solution)/shard_map/reduce_scatter | solution.py:39
  61.1 64.4 %copy-start.1 = (f32[512,128]{1,0:T(8,128)S(1)}, f32[512,128]{1,0:T(8,128)}, u32[]{:S(2)}) copy-start(f32[512,128]{1,0:T(8,128)} %param.13) | copy-start | bytes 786436
  61.1 64.4 %copy-start.3 = (bf16[128,512]{1,0:T(8,128)(2,1)S(1)}, bf16[128,512]{1,0:T(8,128)(2,1)}, u32[]{:S(2)}) copy-start(bf16[128,512]{1,0:T(8,128)(2,1)} %param.10) | copy-start | bytes 393220
  61.2 65.5 %copy-start.2 = (f32[128]{0:T(128)S(1)}, f32[128]{0:T(128)}, u32[]{:S(2)}) copy-start(f32[128]{0:T(128)} %param.14) | copy-start | bytes 1540
  130.4 363.5 %all-reduce.3.cloned.1.call-start = ((), (), s32[]{:S(2)}) async-start(), calls=%async_computation.4 | async-start | bytes 524288 | tf_op jit(solution)/shard_map/psum | solution.py:46
  203.5 768.4 %all-reduce.5.cloned.1.call-start = ((), (), s32[]{:S(2)}) async-start(), calls=%async_computation.5 | async-start | bytes 524288 | tf_op jit(solution)/shard_map/psum | solution.py:45
Sparse Core Ops, SparseCore 0:
  11.4 47.3 all-gather.4
  60.9 59.8 all-gather.2
  130.5 72.9 reduce-scatter.1
  206.2 287.6 all-reduce.2
  500.7 471.1 all-reduce.4
where the time goes:
time: 981 us; the launch traced here: 980 us
  waiting for transfers between devices  945 us (96%)
  between operations  13.9 us (1%)
  matrix products  12.7 us (1%)
    psum x1, waiting for transfers between devices, shards(): grad_u = lax.psum(grad_u_part, ('dp', 'fsdp'))  476 us
    psum x1, waiting for transfers between devices, shards(): grad_v = lax.psum(grad_v_part, 'dp')  289 us
    reduce_scatter x1, waiting for transfers between devices, shards(): lax.psum_scatter(jnp.einsum('td,tr->dr', hidden, rank_grad, preferred_ele...  73 us
    all_gather x1, waiting for transfers between devices, shards(): base_out = add_rows(lax.all_gather(base_weight, 'fsdp', axis=0, tiled=True))  59.7 us
    all_gather x1, waiting for transfers between devices, shards(): low_rank = add_rows(lax.all_gather(v_quant, 'fsdp', axis=0, tiled=True))  46.1 us
  transfers between devices with their start and end apart: 5, of which 5 were waited for; matrix products, arithmetic and copies ran while one was open for 1% of the time, Pallas kernels for 0%

commit v1 on v0

v1 whole, which is shorter than its diff:
```python
import math

import jax
import jax.numpy as jnp
from jax import lax
from jax.sharding import PartitionSpec as P


def fake_quantize(factor, bits, scale_exps):
    step = jnp.exp2(-scale_exps.astype(jnp.float32))
    upper = jnp.exp2(bits.astype(jnp.float32) - 1.0)
    ratio = factor / step
    smooth = ratio - jnp.sin(2.0 * math.pi * ratio) / (2.0 * math.pi)
    return step * jnp.clip(smooth, -upper, upper - 1.0)


def scatter_sum(parts, axis):
    return jnp.sum(lax.all_to_all(parts, axis, 0, 0, tiled=True), axis=0)


def spread(rows, axis):
    n = lax.axis_size(axis)
    return lax.all_to_all(jnp.broadcast_to(rows, (n, *rows.shape)), axis, 0, 0, tiled=True)


def shards(hidden, target, base_weight, v_factor, u_factor, sigma, bits, v_exps, u_exps):
    n_fsdp, n_dp = lax.axis_size("fsdp"), lax.axis_size("dp")
    v_quant = fake_quantize(v_factor, bits, v_exps).astype(jnp.bfloat16)
    u_quant = fake_quantize(u_factor, bits, u_exps).astype(jnp.bfloat16)
    tok_rows = hidden.shape[0]
    kvw, rank = u_factor.shape

    both = lax.all_gather(jnp.concatenate([base_weight, v_quant], axis=1), "fsdp", axis=0, tiled=True)
    out = jnp.dot(hidden, both, preferred_element_type=jnp.float32)
    base_out, low_rank = out[:, :kvw], out[:, kvw:]
    scaled = (low_rank * sigma).astype(jnp.bfloat16)
    residual = (
        base_out
        + jnp.dot(scaled, u_quant.T, preferred_element_type=jnp.float32)
        - target.astype(jnp.float32)
    )
    tokens_all = tok_rows * n_dp * n_fsdp
    out_grad = (residual * (1.0 / math.sqrt(tokens_all))).astype(jnp.bfloat16)
    grad_u_part = jnp.einsum("tk,tr->kr", out_grad, scaled, preferred_element_type=jnp.float32)
    rank_grad = (jnp.dot(out_grad, u_quant, preferred_element_type=jnp.float32) * sigma).astype(
        jnp.bfloat16
    )
    grad_v_part = jnp.einsum("td,tr->dr", hidden, rank_grad, preferred_element_type=jnp.float32)

    parts = jnp.concatenate(
        [grad_v_part.reshape(n_fsdp, -1, rank), grad_u_part.reshape(n_fsdp, -1, rank)], axis=1
    )
    mine = scatter_sum(parts, "fsdp")
    rows_v = v_factor.shape[0]
    parts = jnp.concatenate(
        [mine[:rows_v].reshape(n_dp, -1, rank), mine[rows_v:].reshape(n_dp, -1, rank)], axis=1
    )
    mine = scatter_sum(parts, "dp")
    whole = spread(mine, "dp")
    per_v = rows_v // n_dp
    grad_v = whole[:, :per_v].reshape(rows_v, rank)
    grad_u = spread(whole[:, per_v:].reshape(-1, rank), "fsdp").reshape(kvw, rank)
    return (grad_v, grad_u)


def solution(mesh):
    in_specs = (
        P(("dp", "fsdp"), None),
        P(("dp", "fsdp"), None),
        P("fsdp", None),
        P("fsdp", None),
        P(),
        P(),
        P(),
        P(),
        P(),
    )
    out_specs = (P("fsdp", None), P())
    return jax.shard_map(shards, mesh=mesh, in_specs=in_specs, out_specs=out_specs, check_vma=False)
```

time: 981 us -> 260 us (0.27)
  waiting for transfers between devices: 945 us -> 80.6 us
  blocking collectives: 0 us -> 129 us
    psum x2 -> x0, waiting for transfers between devices: 766 us -> none  [the longest x1 476 us: shards(): grad_u = lax.psum(grad_u_part, ('dp', 'fsdp'))]
    all_to_all x0 -> x3, blocking collectives: none -> 129 us  [the longest x2 97.9 us: scatter_sum(): return jnp.sum(lax.all_to_all(parts, axis, 0, 0, tiled=True), axis=0)]
    reduce_scatter x1 -> x0, waiting for transfers between devices: 73 us -> none  [shards(): lax.psum_scatter(jnp.einsum('td,tr->dr', hidden, rank_grad, preferred_ele...]
    all_gather x2 -> x1, waiting for transfers between devices: 106 us -> 73.8 us  [shards(): lax.all_gather(jnp.concatenate([base_weight, v_quant], axis=1), 'fsdp', a...]
  transfers between devices with their start and end apart: 5 -> 2, of which waited for: 5 -> 2; matrix products, arithmetic and copies ran while one was open for 1% -> 1% of each run, Pallas kernels for 0% -> 0%
where the time goes in v1:
time: 260 us
  blocking collectives  129 us (50%)
  waiting for transfers between devices  80.6 us (31%)
  between operations  14.1 us (5%)
  matrix products  10.7 us (4%)
  other arithmetic  10.4 us (4%)
  local copies, waits for them, and re-layouts  8.99 us (3%)
  starting transfers between devices  5.89 us (2%)
    all_to_all x2, blocking collectives, scatter_sum(): return jnp.sum(lax.all_to_all(parts, axis, 0, 0, tiled=True), axis=0)  97.9 us
    all_gather x1, waiting for transfers between devices, shards(): lax.all_gather(jnp.concatenate([base_weight, v_quant], axis=1), 'fsdp', a...  73.8 us
    all_to_all x1, blocking collectives, spread(): lax.all_to_all(jnp.broadcast_to(rows, (n, *rows.shape)), axis, 0, 0, tile...  31.1 us
    all_to_all x1, waiting for transfers between devices, spread(): lax.all_to_all(jnp.broadcast_to(rows, (n, *rows.shape)), axis, 0, 0, tile...  6.74 us
    all_to_all x1, starting transfers between devices, spread(): lax.all_to_all(jnp.broadcast_to(rows, (n, *rows.shape)), axis, 0, 0, tile...  5.85 us
    dot_general x1, matrix products, shards(): out = jnp.dot(hidden, both, preferred_element_type=jnp.float32)  5.62 us
    reshape x1, local copies, waits for them, and re-layouts, shards(): grad_v_part.reshape(n_fsdp, -1, rank)  5.58 us
  transfers between devices with their start and end apart: 2, of which 2 were waited for; matrix products, arithmetic and copies ran while one was open for 1% of the time, Pallas kernels for 0%

profile of v1, /device:TPU:1, one launch (start us, length us, event | category | flops | bytes accessed | tf_op | source)
XLA Modules:
  0.0 259.7 jit_solution(11769970991505728804)
XLA Ops:
  7.2 0.0 copy-start
  7.2 0.0 all-gather.2.cloned.1.call-start
  7.2 0.8 broadcast_add_fusion
  8.0 1.9 multiply_convert_fusion.1
  9.9 1.9 pad_maximum_fusion.1
  11.9 0.0 all-gather.2.cloned.1.call-update
  11.9 1.0 copy.21
  12.9 0.7 multiply_exponential_fusion
  13.6 0.0 copy-start.1
  13.6 0.0 copy-start.2
  13.6 73.8 %all-gather.2.cloned.1.call-done = bf16[8192,640]{1,0:T(8,128)(2,1)} async-done(((bf16[512,640]{1,0:T(8,128)(2,1)}), bf16[8192,640]{1,0:T(8,128)(2,1)}) %all-gather.2.cloned.1.call-update) | async-done | bytes 10485776 | tf_op jit(solution)/shard_map/all_gather | solution.py:33
  87.4 0.0 copy-done
  87.4 5.6 %convolution_bitcast_fusion.1 = f32[128,640]{0,1:T(8,128)S(1)} fusion(bf16[8192,640]{1,0:T(8,128)(2,1)} %all-gather.2.cloned.1.call-done, bf16[128,8192]{1,0:T(8,128)(2,1)S(1)} %copy-done), kind=kOutput, calls=%fused_computation.2 | convolution fusion | flops 1342177280 | bytes 12910592 | tf_op jit(solution)/shard_map/dot_general | solution.py:34
  93.1 0.0 copy-done.1
  93.1 0.0 copy-done.2
  93.1 1.1 fusion.2
  94.1 0.3 fusion.7
  94.4 3.7 %convolution_bitcast_fusion = f32[8192,128]{0,1:T(8,128)} fusion(bf16[128,8192]{1,0:T(8,128)(2,1)S(1)} %copy-done, bf16[128,512]{0,1:T(8,128)(2,1)S(1)} %fusion.2, f32[128]{0:T(128)S(1)} %copy-done.2, f32[512,128]{1,0:T(8,128)S(1)} %copy-done.1, f32[128]{0:T(128)S(1)} %multiply_exponential_fusion, f32[128]{0:T(128)S(1)} %get-tuple-element.3, ...), kind=kOutput, calls=%fused_computation | convolution fusion | flops 285769728 | bytes 6686720 | tf_op jit(solution)/shard_map/td,tr->dr/dot_general | solution.py:48
  98.1 5.6 %copy.29 = f32[8192,128]{1,0:T(8,128)} copy(f32[8192,128]{0,1:T(8,128)} %convolution_bitcast_fusion) | data formatting | bytes 8388608 | tf_op jit(solution)/shard_map/reshape | solution.py:51
  103.7 2.5 pad_maximum_fusion
  106.3 57.4 %all_to_all.20 = f32[16,544,128]{2,1,0:T(8,128)} all-to-all(f32[16,544,128]{2,1,0:T(8,128)S(1)} %pad_maximum_fusion), channel_id=1, replica_groups=mesh['dp'=32,'fsdp'=16] {'fsdp'}, dimensions={0} | all-to-all | bytes 8912896 | tf_op jit(solution)/shard_map/all_to_all | solution.py:18
  163.6 2.5 reduce_sum.18
  166.2 0.1 copy.32
  166.3 0.1 copy.26
  166.3 0.1 pad_maximum_fusion.2
  166.4 40.5 %all_to_all.21 = f32[32,17,128]{2,1,0:T(8,128)S(1)} all-to-all(f32[32,17,128]{2,1,0:T(8,128)S(1)} %pad_maximum_fusion.2), channel_id=1, replica_groups=mesh['dp'=32,'fsdp'=16] {'dp'}, dimensions={0} | all-to-all | bytes 557056 | tf_op jit(solution)/shard_map/all_to_all | solution.py:18
  207.0 31.1 %all_to_all.22 = f32[32,17,128]{2,1,0:T(8,128)S(1)} all-to-all(f32[32,17,128]{2,1,0:T(8,128)S(1)} %broadcast_in_dim.10), channel_id=1, replica_groups=mesh['dp'=32,'fsdp'=16] {'dp'}, dimensions={0} | all-to-all | bytes 557056 | tf_op jit(solution)/shard_map/all_to_all | solution.py:23
  238.1 0.7 broadcast_in_dim.11
  238.8 5.8 %all-to-all-start.3 = ((f32[16,32,128]{2,1,0:T(8,128)}), f32[16,32,128]{2,1,0:T(8,128)S(1)}, u32[]{:S(2)}, u32[]{:S(2)}) async-start(f32[16,32,128]{2,1,0:T(8,128)} %broadcast_in_dim.11), calls=%async_computation.3 | async-start | bytes 524288 | tf_op jit(solution)/shard_map/all_to_all | solution.py:23
  244.7 0.7 slice.28
  245.4 6.7 %all-to-all-done.3 = f32[16,32,128]{2,1,0:T(8,128)S(1)} async-done(((f32[16,32,128]{2,1,0:T(8,128)}), f32[16,32,128]{2,1,0:T(8,128)S(1)}, u32[]{:S(2)}, u32[]{:S(2)}) %all-to-all-start.3) | async-done | bytes 262176 | tf_op jit(solution)/shard_map/all_to_all | solution.py:23
  252.2 0.7 copy.34
  (5 shorter events, 0.1 us)
Async XLA Ops:
  7.2 80.3 %copy-start = (bf16[128,8192]{1,0:T(8,128)(2,1)S(1)}, bf16[128,8192]{1,0:T(8,128)(2,1)}, u32[]{:S(2)}) copy-start(bf16[128,8192]{1,0:T(8,128)(2,1)} %param.9) | copy-start | bytes 6291460
  7.2 80.2 %all-gather.2.cloned.1.call-start = ((), (), s32[]{:S(2)}) async-start(), calls=%async_computation.4 | async-start | bytes 11141120 | tf_op jit(solution)/shard_map/all_gather | solution.py:33
  13.6 79.5 %copy-start.1 = (f32[512,128]{1,0:T(8,128)S(1)}, f32[512,128]{1,0:T(8,128)}, u32[]{:S(2)}) copy-start(f32[512,128]{1,0:T(8,128)} %param.13) | copy-start | bytes 786436
  13.6 79.5 %copy-start.2 = (f32[128]{0:T(128)S(1)}, f32[128]{0:T(128)}, u32[]{:S(2)}) copy-start(f32[128]{0:T(128)} %param.14) | copy-start | bytes 1540
  238.8 13.3 %all-to-all-start.3 = ((f32[16,32,128]{2,1,0:T(8,128)}), f32[16,32,128]{2,1,0:T(8,128)S(1)}, u32[]{:S(2)}, u32[]{:S(2)}) async-start(f32[16,32,128]{2,1,0:T(8,128)} %broadcast_in_dim.11), calls=%async_computation.3 | async-start | bytes 524288 | tf_op jit(solution)/shard_map/all_to_all | solution.py:23
Sparse Core Ops, SparseCore 0:
  12.0 75.3 all-gather.1

commit v2 on v0

v2 whole, which is shorter than its diff:
```python
import math

import jax
import jax.numpy as jnp
from jax import lax
from jax.sharding import Mesh, PartitionSpec as P

AXES = {"z": 16, "yh": 2, "x": 4, "yl": 2, "core": 2}
DP, FSDP, CHIPS = ("z", "yh"), ("x", "yl", "core"), ("x", "yl")


def fake_quantize(factor, bits, scale_exps):
    step = jnp.exp2(-scale_exps.astype(jnp.float32))
    upper = jnp.exp2(bits.astype(jnp.float32) - 1.0)
    ratio = factor / step
    smooth = ratio - jnp.sin(2.0 * math.pi * ratio) / (2.0 * math.pi)
    return step * jnp.clip(smooth, -upper, upper - 1.0)


def exchange(parts, axes):
    return lax.all_to_all(parts, axes, 0, 0, tiled=True)


def spread(rows, axes):
    return exchange(jnp.broadcast_to(rows, (lax.axis_size(axes), *rows.shape)), axes)


def shards(hidden, target, base_weight, v_factor, u_factor, sigma, bits, v_exps, u_exps):
    n_z, n_yh, n_chips = lax.axis_size("z"), lax.axis_size("yh"), lax.axis_size(CHIPS)
    tok, _ = hidden.shape
    kvw, rank = u_factor.shape
    rows = v_factor.shape[0]

    v_quant = fake_quantize(v_factor, bits, v_exps).astype(jnp.bfloat16)
    weights = lax.all_gather(
        jnp.concatenate([base_weight, v_quant], axis=1), CHIPS, axis=0, tiled=True
    )
    by_core = hidden.reshape(tok, n_chips, 2, rows).transpose(2, 0, 1, 3).reshape(2, tok, -1)
    pair = exchange(by_core, "core").reshape(2 * tok, -1)
    u_quant = fake_quantize(u_factor, bits, u_exps).astype(jnp.bfloat16)

    part = jnp.dot(pair, weights, preferred_element_type=jnp.float32)
    out = jnp.sum(exchange(part.reshape(2, tok, -1), "core"), axis=0)
    base_out, low_rank = out[:, :kvw], out[:, kvw:]
    scaled = (low_rank * sigma).astype(jnp.bfloat16)
    residual = (
        base_out
        + jnp.dot(scaled, u_quant.T, preferred_element_type=jnp.float32)
        - target.astype(jnp.float32)
    )
    tokens_all = tok * n_z * n_yh * n_chips * 2
    out_grad = (residual * (1.0 / math.sqrt(tokens_all))).astype(jnp.bfloat16)
    rank_grad = jnp.dot(out_grad, u_quant, preferred_element_type=jnp.float32) * sigma
    rank_pair = spread(rank_grad.astype(jnp.bfloat16), "core").reshape(2 * tok, rank)
    grad_u_part = jnp.einsum("tk,tr->kr", out_grad, scaled, preferred_element_type=jnp.float32)
    u_half = grad_u_part.reshape(n_chips, 2, -1, rank).transpose(1, 0, 2, 3)
    u_half = jnp.sum(exchange(u_half, "core"), axis=0)
    grad_v_part = jnp.einsum("td,tr->dr", pair, rank_pair, preferred_element_type=jnp.float32)

    half = rows // n_yh
    u_parts = jnp.broadcast_to(u_half[:, None], (n_chips, n_yh, *u_half.shape[1:]))
    parts = jnp.concatenate(
        [grad_v_part.reshape(n_chips * n_yh, half, rank), u_parts.reshape(n_chips * n_yh, -1, rank)],
        axis=1,
    )
    mine = jnp.sum(exchange(parts, (*CHIPS, "yh")), axis=0)
    mine = jnp.concatenate(
        [mine[:half].reshape(n_z, -1, rank), mine[half:].reshape(n_z, -1, rank)], axis=1
    )
    mine = jnp.sum(exchange(mine, "z"), axis=0)
    whole = spread(mine, "z")
    per_z = half // n_z
    v_mine = whole[:, :per_z].reshape(-1, rank)
    v_other = lax.ppermute(v_mine, "yh", [(0, 1), (1, 0)])
    low = lax.axis_index("yh") == 0
    grad_v = jnp.concatenate(
        [jnp.where(low, v_mine, v_other), jnp.where(low, v_other, v_mine)], axis=0
    )
    grad_u = spread(whole[:, per_z:].reshape(-1, rank), FSDP).reshape(kvw, rank)
    return (grad_v, grad_u)


def solution(mesh):
    fine = Mesh(mesh.devices.reshape(tuple(AXES.values())), tuple(AXES))
    in_specs = (
        P((*DP, *FSDP), None),
        P((*DP, *FSDP), None),
        P(FSDP, None),
        P(FSDP, None),
        P(),
        P(),
        P(),
        P(),
        P(),
    )
    out_specs = (P(FSDP, None), P())
    return jax.shard_map(shards, mesh=fine, in_specs=in_specs, out_specs=out_specs, check_vma=False)
```

time: 981 us -> 269 us (0.27)
  waiting for transfers between devices: 945 us -> 111 us
  blocking collectives: 0 us -> 89.3 us
  starting transfers between devices: 0.2 us -> 27.8 us
    psum x2 -> x0, waiting for transfers between devices: 766 us -> none  [the longest x1 476 us: shards(): grad_u = lax.psum(grad_u_part, ('dp', 'fsdp'))]
    all_to_all x0 -> x5, blocking collectives: none -> 89.3 us  [exchange(): return lax.all_to_all(parts, axes, 0, 0, tiled=True)]
    reduce_scatter x1 -> x0, waiting for transfers between devices: 73 us -> none  [shards(): lax.psum_scatter(jnp.einsum('td,tr->dr', hidden, rank_grad, preferred_ele...]
    all_to_all x0 -> x3, starting transfers between devices: none -> 25.4 us  [exchange(): return lax.all_to_all(parts, axes, 0, 0, tiled=True)]
    all_gather x2 -> x1, waiting for transfers between devices: 106 us -> 102 us  [shards(): lax.all_gather(jnp.concatenate([base_weight, v_quant], axis=1), CHIPS, ax...]
  transfers between devices with their start and end apart: 5 -> 5, of which waited for: 5 -> 3; matrix products, arithmetic and copies ran while one was open for 1% -> 5% of each run, Pallas kernels for 0% -> 0%
where the time goes in v2:
time: 269 us; the launch traced here: 268 us
  waiting for transfers between devices  111 us (41%)
  blocking collectives  89.3 us (33%)
  starting transfers between devices  27.8 us (10%)
  between operations  14.3 us (5%)
  local copies, waits for them, and re-layouts  11.3 us (4%)
  matrix products  8.46 us (3%)
  other arithmetic  5.77 us (2%)
    all_gather x1, waiting for transfers between devices, shards(): lax.all_gather(jnp.concatenate([base_weight, v_quant], axis=1), CHIPS, ax...  102 us
    all_to_all x5, blocking collectives, exchange(): return lax.all_to_all(parts, axes, 0, 0, tiled=True)  89.3 us
    all_to_all x3, starting transfers between devices, exchange(): return lax.all_to_all(parts, axes, 0, 0, tiled=True)  25.4 us
    all_to_all x3, waiting for transfers between devices, exchange(): return lax.all_to_all(parts, axes, 0, 0, tiled=True)  9.13 us
    reshape x3, local copies, waits for them, and re-layouts, shards(): hidden.reshape(tok, n_chips, 2, rows).transpose(2, 0, 1, 3)  7.06 us
  transfers between devices with their start and end apart: 5, of which 3 were waited for; matrix products, arithmetic and copies ran while one was open for 5% of the time, Pallas kernels for 0%

profile of v2, /device:TPU:1, one launch (start us, length us, event | category | flops | bytes accessed | tf_op | source)
XLA Modules:
  0.0 268.3 jit_solution(3721792675189735775)
XLA Ops:
  7.2 0.0 copy-start
  7.2 0.0 all-gather.2.cloned.1.call-start
  7.2 0.8 broadcast_add_fusion
  8.0 1.9 multiply_convert_fusion.1
  9.9 1.9 pad_maximum_fusion.1
  11.8 0.0 all-gather.2.cloned.1.call-update
  11.9 0.0 copy-done
  11.9 2.8 %reshape.47 = bf16[128,8,2,512]{3,2,1,0:T(2,128)(2,1)} reshape(bf16[128,8192]{1,0:T(8,128)(2,1)S(1)} %copy-done) | data formatting | bytes 4194304 | tf_op jit(solution)/shard_map/reshape | solution.py:38
  14.7 1.9 copy.34
  16.6 2.4 reshape.48
  18.9 0.0 copy-start.4
  18.9 10.8 %all-to-all-start = ((bf16[2,128,4096]{2,1,0:T(8,128)(2,1)}), bf16[2,128,4096]{2,1,0:T(8,128)(2,1)S(1)}, u32[]{:S(2)}, u32[]{:S(2)}) async-start(bf16[2,128,4096]{2,1,0:T(8,128)(2,1)} %reshape.48), calls=%async_computation | async-start | bytes 4194304 | tf_op jit(solution)/shard_map/all_to_all | solution.py:21
  29.7 0.0 copy-done.4
  29.7 2.5 all-to-all-done
  32.2 102.1 %all-gather.2.cloned.1.call-done = bf16[4096,640]{1,0:T(8,128)(2,1)} async-done(((bf16[512,640]{1,0:T(8,128)(2,1)}), bf16[4096,640]{1,0:T(8,128)(2,1)}) %all-gather.2.cloned.1.call-update) | async-done | bytes 5242896 | tf_op jit(solution)/shard_map/all_gather | solution.py:35
  134.4 4.3 %fusion.9 = f32[640,256]{0,1:T(8,128)S(1)} fusion(bf16[256,4096]{1,0:T(8,128)(2,1)S(1)} %bitcast.32, bf16[4096,640]{1,0:T(8,128)(2,1)} %all-gather.2.cloned.1.call-done), kind=kOutput, calls=%fused_computation.25 | convolution fusion | flops 1342177280 | bytes 7995392 | tf_op jit(solution)/shard_map/dot_general | solution.py:42
  138.7 0.0 copy-start.1
  138.7 0.0 copy-start.2
  138.7 0.0 copy-start.3
  138.7 4.7 %all_to_all.40 = f32[2,128,640]{2,1,0:T(8,128)S(1)} all-to-all(f32[2,128,640]{2,1,0:T(8,128)S(1)} %bitcast.38), channel_id=1, replica_groups=mesh['z'=16,'yh'=2,'x'=4,'yl'=2,'core'=2] {'core'}, dimensions={0} | all-to-all | bytes 1310720 | tf_op jit(solution)/shard_map/all_to_all | solution.py:21
  143.5 0.0 copy-done.1
  143.5 0.0 copy-done.2
  143.5 0.0 copy-done.3
  143.5 1.1 fusion.2
  144.6 0.2 fusion.5
  144.8 1.1 fusion.3
  145.9 0.7 copy.35
  146.6 0.1 copy.20
  146.8 3.8 %all_to_all.41 = bf16[2,128,128]{1,2,0:T(8,128)(2,1)S(1)} all-to-all(bf16[2,128,128]{1,2,0:T(8,128)(2,1)S(1)} %broadcast_in_dim.14), channel_id=1, replica_groups=mesh['z'=16,'yh'=2,'x'=4,'yl'=2,'core'=2] {'core'}, dimensions={0} | all-to-all | bytes 131072 | tf_op jit(solution)/shard_map/all_to_all | solution.py:21
  150.6 3.8 %all-to-all-start.3 = ((f32[2,8,32,128]{3,2,1,0:T(8,128)}), f32[2,8,32,128]{3,2,1,0:T(8,128)S(1)}, u32[]{:S(2)}, u32[]{:S(2)}) async-start(f32[2,8,32,128]{3,2,1,0:T(8,128)} %bitcast.31), calls=%async_computation.3 | async-start | bytes 524288 | tf_op jit(solution)/shard_map/all_to_all | solution.py:21
  154.3 1.8 convolution_bitcast_fusion
  156.1 1.9 copy.27
  158.1 0.0 all-to-all-done.3
  158.1 0.2 pad_maximum_fusion
  158.3 36.7 %all_to_all.42 = f32[16,288,128]{2,1,0:T(8,128)S(1)} all-to-all(f32[16,288,128]{2,1,0:T(8,128)S(1)} %pad_maximum_fusion), channel_id=1, replica_groups=mesh['z'=16,'yh'=2,'x'=4,'yl'=2,'core'=2] {'x','yl','yh'}, dimensions={0} | all-to-all | bytes 4718592 | tf_op jit(solution)/shard_map/all_to_all | solution.py:21
  195.0 0.1 reduce_sum.38
  195.1 24.1 %all_to_all.43 = f32[16,18,128]{2,1,0:T(8,128)S(1)} all-to-all(f32[16,18,128]{2,1,0:T(8,128)S(1)} %pad_maximum_fusion.3), channel_id=1, replica_groups=mesh['z'=16,'yh'=2,'x'=4,'yl'=2,'core'=2] {'z'}, dimensions={0} | all-to-all | bytes 294912 | tf_op jit(solution)/shard_map/all_to_all | solution.py:21
  219.3 19.9 %all_to_all.44 = f32[16,18,128]{2,1,0:T(8,128)S(1)} all-to-all(f32[16,18,128]{2,1,0:T(8,128)S(1)} %broadcast_in_dim.16), channel_id=1, replica_groups=mesh['z'=16,'yh'=2,'x'=4,'yl'=2,'core'=2] {'z'}, dimensions={0} | all-to-all | bytes 294912 | tf_op jit(solution)/shard_map/all_to_all | solution.py:21
  239.3 2.4 collective-permute-start
  241.7 0.7 broadcast_in_dim.30
  242.4 10.9 %all-to-all-start.7 = ((f32[16,32,128]{2,1,0:T(8,128)}), f32[16,32,128]{2,1,0:T(8,128)S(1)}, u32[]{:S(2)}, u32[]{:S(2)}) async-start(f32[16,32,128]{2,1,0:T(8,128)} %broadcast_in_dim.30), calls=%async_computation.7 | async-start | bytes 524288 | tf_op jit(solution)/shard_map/all_to_all | solution.py:21
  253.3 0.0 collective-permute-done
  253.3 0.7 pad_maximum_fusion.2
  254.1 6.6 %all-to-all-done.7 = f32[16,32,128]{2,1,0:T(8,128)S(1)} async-done(((f32[16,32,128]{2,1,0:T(8,128)}), f32[16,32,128]{2,1,0:T(8,128)S(1)}, u32[]{:S(2)}, u32[]{:S(2)}) %all-to-all-start.7) | async-done | bytes 262176 | tf_op jit(solution)/shard_map/all_to_all | solution.py:21
  260.7 0.7 copy.37
  (13 shorter events, 0.2 us)
Async XLA Ops:
  7.2 4.7 %copy-start = (bf16[128,8192]{1,0:T(8,128)(2,1)S(1)}, bf16[128,8192]{1,0:T(8,128)(2,1)}, u32[]{:S(2)}) copy-start(bf16[128,8192]{1,0:T(8,128)(2,1)} %param.9) | copy-start | bytes 6291460
  7.2 127.2 %all-gather.2.cloned.1.call-start = ((), (), s32[]{:S(2)}) async-start(), calls=%async_computation.8 | async-start | bytes 5898240 | tf_op jit(solution)/shard_map/all_gather | solution.py:35
  18.9 10.8 %copy-start.4 = (s32[128]{0:T(128)S(1)}, s32[128]{0:T(128)}, u32[]{:S(2)}) copy-start(s32[128]{0:T(128)} %param.17) | copy-start | bytes 1540
  18.9 13.3 %all-to-all-start = ((bf16[2,128,4096]{2,1,0:T(8,128)(2,1)}), bf16[2,128,4096]{2,1,0:T(8,128)(2,1)S(1)}, u32[]{:S(2)}, u32[]{:S(2)}) async-start(bf16[2,128,4096]{2,1,0:T(8,128)(2,1)} %reshape.48), calls=%async_computation | async-start | bytes 4194304 | tf_op jit(solution)/shard_map/all_to_all | solution.py:21
  138.7 4.8 %copy-start.1 = (f32[128]{0:T(128)S(1)}, f32[128]{0:T(128)}, u32[]{:S(2)}) copy-start(f32[128]{0:T(128)} %param.14) | copy-start | bytes 1540
  138.7 4.8 %copy-start.2 = (f32[512,128]{1,0:T(8,128)S(1)}, f32[512,128]{1,0:T(8,128)}, u32[]{:S(2)}) copy-start(f32[512,128]{1,0:T(8,128)} %param.13) | copy-start | bytes 786436
  138.7 4.8 %copy-start.3 = (bf16[128,512]{1,0:T(8,128)(2,1)S(1)}, bf16[128,512]{1,0:T(8,128)(2,1)}, u32[]{:S(2)}) copy-start(bf16[128,512]{1,0:T(8,128)(2,1)} %param.10) | copy-start | bytes 393220
  150.6 7.5 %all-to-all-start.3 = ((f32[2,8,32,128]{3,2,1,0:T(8,128)}), f32[2,8,32,128]{3,2,1,0:T(8,128)S(1)}, u32[]{:S(2)}, u32[]{:S(2)}) async-start(f32[2,8,32,128]{3,2,1,0:T(8,128)} %bitcast.31), calls=%async_computation.3 | async-start | bytes 524288 | tf_op jit(solution)/shard_map/all_to_all | solution.py:21
  239.3 14.0 %collective-permute-start = (f32[256,128]{1,0:T(8,128)S(1)}, f32[256,128]{1,0:T(8,128)S(1)}, u32[]{:S(2)}, u32[]{:S(2)}) collective-permute-start(f32[256,128]{1,0:T(8,128)S(1)} %bitcast.39), channel_id=1, source_target_pairs={{0,16},{16,0},{1,17},{17,1},{2,18},{18,2},{3,19},{19,3},{4,20},{20... | collective-permute-start | bytes 393224 | tf_op jit(solution)/shard_map/ppermute | solution.py:74
  242.4 18.3 %all-to-all-start.7 = ((f32[16,32,128]{2,1,0:T(8,128)}), f32[16,32,128]{2,1,0:T(8,128)S(1)}, u32[]{:S(2)}, u32[]{:S(2)}) async-start(f32[16,32,128]{2,1,0:T(8,128)} %broadcast_in_dim.30), calls=%async_computation.7 | async-start | bytes 524288 | tf_op jit(solution)/shard_map/all_to_all | solution.py:21
Sparse Core Ops, SparseCore 0:
  12.0 122.3 all-gather.1

commit v3 on v2

--- a/solution.py
+++ b/solution.py
@@ -6,7 +6,7 @@
 from jax.sharding import Mesh, PartitionSpec as P
 
 AXES = {"z": 16, "yh": 2, "x": 4, "yl": 2, "core": 2}
-DP, FSDP, CHIPS = ("z", "yh"), ("x", "yl", "core"), ("x", "yl")
+DP, FSDP, NEAR = ("z", "yh"), ("x", "yl", "core"), ("yl", "core")
 
 
 def fake_quantize(factor, bits, scale_exps):
@@ -26,21 +26,31 @@
 
 
 def shards(hidden, target, base_weight, v_factor, u_factor, sigma, bits, v_exps, u_exps):
-    n_z, n_yh, n_chips = lax.axis_size("z"), lax.axis_size("yh"), lax.axis_size(CHIPS)
+    n_x, n_z, n_yh = lax.axis_size("x"), lax.axis_size("z"), lax.axis_size("yh")
+    n_near = lax.axis_size(NEAR)
     tok, _ = hidden.shape
     kvw, rank = u_factor.shape
     rows = v_factor.shape[0]
+    me = lax.axis_index(NEAR)
 
     v_quant = fake_quantize(v_factor, bits, v_exps).astype(jnp.bfloat16)
-    weights = lax.all_gather(
-        jnp.concatenate([base_weight, v_quant], axis=1), CHIPS, axis=0, tiled=True
-    )
-    by_core = hidden.reshape(tok, n_chips, 2, rows).transpose(2, 0, 1, 3).reshape(2, tok, -1)
-    pair = exchange(by_core, "core").reshape(2 * tok, -1)
+    weights = [jnp.concatenate([base_weight, v_quant], axis=1)]
+    for k in range(1, n_near):
+        weights.append(lax.ppermute(weights[0], NEAR, [(j, j ^ k) for j in range(n_near)]))
+    wide = n_near * rows
+    columns = jnp.stack([hidden[:, i * wide : (i + 1) * wide] for i in range(n_x)])
+    tokens = exchange(columns, "x").reshape(n_x * tok, wide)
     u_quant = fake_quantize(u_factor, bits, u_exps).astype(jnp.bfloat16)
 
-    part = jnp.dot(pair, weights, preferred_element_type=jnp.float32)
-    out = jnp.sum(exchange(part.reshape(2, tok, -1), "core"), axis=0)
+    part = sum(
+        jnp.dot(
+            lax.dynamic_slice_in_dim(tokens, (me ^ k) * rows, rows, 1),
+            weights[k],
+            preferred_element_type=jnp.float32,
+        )
+        for k in range(n_near)
+    )
+    out = jnp.sum(exchange(part.reshape(n_x, tok, -1), "x"), axis=0)
     base_out, low_rank = out[:, :kvw], out[:, kvw:]
     scaled = (low_rank * sigma).astype(jnp.bfloat16)
     residual = (
@@ -48,22 +58,20 @@
         + jnp.dot(scaled, u_quant.T, preferred_element_type=jnp.float32)
         - target.astype(jnp.float32)
     )
-    tokens_all = tok * n_z * n_yh * n_chips * 2
+    tokens_all = tok * n_z * n_yh * n_x * n_near
     out_grad = (residual * (1.0 / math.sqrt(tokens_all))).astype(jnp.bfloat16)
     rank_grad = jnp.dot(out_grad, u_quant, preferred_element_type=jnp.float32) * sigma
-    rank_pair = spread(rank_grad.astype(jnp.bfloat16), "core").reshape(2 * tok, rank)
+    rank_all = spread(rank_grad.astype(jnp.bfloat16), "x").reshape(n_x * tok, rank)
     grad_u_part = jnp.einsum("tk,tr->kr", out_grad, scaled, preferred_element_type=jnp.float32)
-    u_half = grad_u_part.reshape(n_chips, 2, -1, rank).transpose(1, 0, 2, 3)
-    u_half = jnp.sum(exchange(u_half, "core"), axis=0)
-    grad_v_part = jnp.einsum("td,tr->dr", pair, rank_pair, preferred_element_type=jnp.float32)
+    u_rows = jnp.sum(exchange(grad_u_part.reshape(n_x, -1, rank), "x"), axis=0)
+    grad_v_part = jnp.einsum("td,tr->dr", tokens, rank_all, preferred_element_type=jnp.float32)
 
     half = rows // n_yh
-    u_parts = jnp.broadcast_to(u_half[:, None], (n_chips, n_yh, *u_half.shape[1:]))
-    parts = jnp.concatenate(
-        [grad_v_part.reshape(n_chips * n_yh, half, rank), u_parts.reshape(n_chips * n_yh, -1, rank)],
-        axis=1,
-    )
-    mine = jnp.sum(exchange(parts, (*CHIPS, "yh")), axis=0)
+    v_parts = grad_v_part.reshape(n_near * n_yh, half, rank)
+    u_parts = u_rows.reshape(n_near, 1, -1, rank)
+    u_parts = jnp.broadcast_to(u_parts, (n_near, n_yh, *u_parts.shape[2:]))
+    parts = jnp.concatenate([v_parts, u_parts.reshape(n_near * n_yh, -1, rank)], axis=1)
+    mine = jnp.sum(exchange(parts, (*NEAR, "yh")), axis=0)
     mine = jnp.concatenate(
         [mine[:half].reshape(n_z, -1, rank), mine[half:].reshape(n_z, -1, rank)], axis=1
     )

time: 269 us -> 183 us (0.68)
  waiting for transfers between devices: 111 us -> 46.9 us
  blocking collectives: 89.3 us -> 72 us
  between operations: 14.3 us -> 0.94 us
  starting transfers between devices: 27.8 us -> 40.2 us
  local copies, waits for them, and re-layouts: 11.3 us -> 7.12 us
  matrix products: 8.46 us -> 11.2 us
    all_gather x1 -> x0, waiting for transfers between devices: 102 us -> none  [shards(): lax.all_gather(jnp.concatenate([base_weight, v_quant], axis=1), CHIPS, ax...]
    all_to_all x3 -> x5, waiting for transfers between devices: 9.13 us -> 36.7 us  [exchange(): return lax.all_to_all(parts, axes, 0, 0, tiled=True)]
    all_to_all x5 -> x3, blocking collectives: 89.3 us -> 72 us  [exchange(): return lax.all_to_all(parts, axes, 0, 0, tiled=True)]
    ppermute x0 -> x3, starting transfers between devices: none -> 12.8 us  [shards(): lax.ppermute(weights[0], NEAR, [(j, j ^ k) for j in range(n_near)])]
    ppermute x0 -> x3, waiting for transfers between devices: none -> 10.1 us  [shards(): lax.ppermute(weights[0], NEAR, [(j, j ^ k) for j in range(n_near)])]
    reshape x5 -> x1, local copies, waits for them, and re-layouts: 9.69 us -> 2.56 us  [shards(): tokens = exchange(columns, 'x').reshape(n_x * tok, wide)]
    dot_general x2 -> x5, matrix products: 6.11 us -> 7.35 us  [the longest x4 6.64 us: shards(): jnp.dot(lax.dynamic_slice_in_dim(tokens, (me ^ k) * rows, rows, 1), weigh...]
    all_to_all x3 -> x5, starting transfers between devices: 25.4 us -> 24.8 us  [exchange(): return lax.all_to_all(parts, axes, 0, 0, tiled=True)]
  transfers between devices with their start and end apart: 5 -> 9, of which waited for: 3 -> 6; matrix products, arithmetic and copies ran while one was open for 5% -> 6% of each run, Pallas kernels for 0% -> 0%
where the time goes in v3:
time: 183 us; the launch traced here: 182 us
  blocking collectives  72 us (39%)
  waiting for transfers between devices  46.9 us (26%)
  starting transfers between devices  40.2 us (22%)
  matrix products  11.2 us (6%)
  local copies, waits for them, and re-layouts  7.12 us (4%)
  other arithmetic  3.63 us (2%)
    all_to_all x3, blocking collectives, exchange(): return lax.all_to_all(parts, axes, 0, 0, tiled=True)  72 us
    all_to_all x5, waiting for transfers between devices, exchange(): return lax.all_to_all(parts, axes, 0, 0, tiled=True)  36.7 us
    all_to_all x5, starting transfers between devices, exchange(): return lax.all_to_all(parts, axes, 0, 0, tiled=True)  24.8 us
    ppermute x3, starting transfers between devices, shards(): lax.ppermute(weights[0], NEAR, [(j, j ^ k) for j in range(n_near)])  12.8 us
    ppermute x3, waiting for transfers between devices, shards(): lax.ppermute(weights[0], NEAR, [(j, j ^ k) for j in range(n_near)])  10.1 us
    dot_general x4, matrix products, shards(): jnp.dot(lax.dynamic_slice_in_dim(tokens, (me ^ k) * rows, rows, 1), weigh...  6.64 us
  transfers between devices with their start and end apart: 9, of which 6 were waited for; matrix products, arithmetic and copies ran while one was open for 6% of the time, Pallas kernels for 0%

profile of v3, /device:TPU:1, one launch (start us, length us, event | category | flops | bytes accessed | tf_op | source)
XLA Modules:
  0.0 182.0 jit_solution(13311551073655061528)
XLA Ops:
  0.6 1.7 slice_bitcast_fusion.3
  2.3 1.6 pad_maximum_fusion
  3.9 0.0 copy-start.8
  3.9 0.0 copy-start.9
  3.9 0.0 copy-start.3
  3.9 0.0 copy-start.1
  3.9 5.0 %all-to-all-start = ((bf16[4,128,2048]{2,1,0:T(8,128)(2,1)}), bf16[4,128,2048]{2,1,0:T(8,128)(2,1)S(1)}, u32[]{:S(2)}, u32[]{:S(2)}) async-start(bf16[4,128,2048]{2,1,0:T(8,128)(2,1)} %pad_maximum_fusion), calls=%async_computation | async-start | bytes 4194304 | tf_op jit(solution)/shard_map/all_to_all | solution.py:21
  8.9 0.0 copy-done.8
  8.9 0.0 copy-done.9
  8.9 0.0 copy-done.3
  8.9 0.9 multiply_convert_fusion.1
  9.9 0.0 copy-done.1
  9.9 0.1 pad_maximum_fusion.2
  9.9 4.0 %collective-permute-start.2 = (bf16[512,640]{1,0:T(8,128)(2,1)S(1)}, bf16[512,640]{1,0:T(8,128)(2,1)}, u32[]{:S(2)}, u32[]{:S(2)}) collective-permute-start(bf16[512,640]{1,0:T(8,128)(2,1)S(1)} %pad_maximum_fusion.2), channel_id=1, source_target_pairs={{0,3},{1,2},{2,1},{3,0},{4,7},{5,6},{6,5},{7,4},{8,11},{9,10},{10,... | collective-permute-start | bytes 1966088 | tf_op jit(solution)/shard_map/ppermute | solution.py:39
  14.0 5.4 %collective-permute-start = (bf16[512,640]{1,0:T(8,128)(2,1)S(1)}, bf16[512,640]{1,0:T(8,128)(2,1)}, u32[]{:S(2)}, u32[]{:S(2)}) collective-permute-start(bf16[512,640]{1,0:T(8,128)(2,1)S(1)} %pad_maximum_fusion.2), channel_id=1, source_target_pairs={{0,1},{1,0},{2,3},{3,2},{4,5},{5,4},{6,7},{7,6},{8,9},{9,8},{10,11... | collective-permute-start | bytes 1966088 | tf_op jit(solution)/shard_map/ppermute | solution.py:39
  19.4 3.3 %collective-permute-start.1 = (bf16[512,640]{1,0:T(8,128)(2,1)S(1)}, bf16[512,640]{1,0:T(8,128)(2,1)}, u32[]{:S(2)}, u32[]{:S(2)}) collective-permute-start(bf16[512,640]{1,0:T(8,128)(2,1)S(1)} %pad_maximum_fusion.2), channel_id=1, source_target_pairs={{0,2},{1,3},{2,0},{3,1},{4,6},{5,7},{6,4},{7,5},{8,10},{9,11},{10,... | collective-permute-start | bytes 1966088 | tf_op jit(solution)/shard_map/ppermute | solution.py:39
  22.7 6.6 %all-to-all-done = bf16[4,128,2048]{2,1,0:T(8,128)(2,1)S(1)} async-done(((bf16[4,128,2048]{2,1,0:T(8,128)(2,1)}), bf16[4,128,2048]{2,1,0:T(8,128)(2,1)S(1)}, u32[]{:S(2)}, u32[]{:S(2)}) %all-to-all-start) | async-done | bytes 2097184 | tf_op jit(solution)/shard_map/all_to_all | solution.py:21
  29.3 0.6 fusion.6
  29.9 0.0 collective-permute-done.2
  29.9 1.7 fusion.2
  31.6 0.0 collective-permute-done
  31.6 1.7 convolution_add_fusion.1
  33.3 10.1 %collective-permute-done.1 = bf16[512,640]{1,0:T(8,128)(2,1)} collective-permute-done((bf16[512,640]{1,0:T(8,128)(2,1)S(1)}, bf16[512,640]{1,0:T(8,128)(2,1)}, u32[]{:S(2)}, u32[]{:S(2)}) %collective-permute-start.1) | collective-permute-done | bytes 655392 | tf_op jit(solution)/shard_map/ppermute | solution.py:39
  43.4 2.7 %fusion = f32[512,640]{1,0:T(8,128)} fusion(f32[512,640]{1,0:T(8,128)S(1)} %fusion.2, f32[512,640]{1,0:T(8,128)S(1)} %convolution_add_fusion.1, bf16[512,640]{1,0:T(8,128)(2,1)} %collective-permute-done.1, bf16[512,2048]{1,0:T(8,128)(2,1)S(1)} %bitcast.36, s32[]{:T(128)S(6)} %select_n.27), kind=kOutput, calls=%fused_computation.2 | convolution fusion | flops 336199680 | bytes 5111812 | tf_op jit(solution)/shard_map/dot_general | solution.py:46
  46.1 0.0 copy-start.10
  46.2 4.6 %all-to-all-start.1 = ((f32[4,128,640]{2,1,0:T(8,128)}), f32[4,128,640]{2,1,0:T(8,128)S(1)}, u32[]{:S(2)}, u32[]{:S(2)}) async-start(f32[4,128,640]{2,1,0:T(8,128)} %bitcast.39), calls=%async_computation.1 | async-start | bytes 2621440 | tf_op jit(solution)/shard_map/all_to_all | solution.py:21
  50.8 0.0 copy-done.10
  50.8 2.6 %copy.13 = bf16[512,2048]{0,1:T(8,128)(2,1)} copy(bf16[512,2048]{1,0:T(8,128)(2,1)S(1)} %bitcast.37) | data formatting | bytes 4194304 | tf_op jit(solution)/shard_map/reshape | solution.py:42
  53.4 0.0 copy-start.4
  53.4 0.0 copy-start.5
  53.4 0.0 copy-start.7
  53.4 15.6 %all-to-all-done.1 = f32[4,128,640]{2,1,0:T(8,128)S(1)} async-done(((f32[4,128,640]{2,1,0:T(8,128)}), f32[4,128,640]{2,1,0:T(8,128)S(1)}, u32[]{:S(2)}, u32[]{:S(2)}) %all-to-all-start.1) | async-done | bytes 1310752 | tf_op jit(solution)/shard_map/all_to_all | solution.py:21
  69.0 0.1 reduce_sum.36
  69.1 0.0 copy-start.2
  69.1 0.7 copy-done.2
  69.8 0.0 copy-done.4
  69.8 0.0 copy-done.5
  69.8 0.0 copy-done.7
  69.8 0.0 copy-start.6
  69.8 1.1 fusion.10
  70.9 0.0 copy-done.6
  70.9 0.0 copy-start
  70.9 1.1 fusion.1
  72.0 0.7 broadcast_in_dim.28
  72.7 3.3 %all-to-all-start.2 = ((bf16[4,128,128]{2,1,0:T(8,128)(2,1)}), bf16[4,128,128]{2,1,0:T(8,128)(2,1)S(1)}, u32[]{:S(2)}, u32[]{:S(2)}) async-start(bf16[4,128,128]{2,1,0:T(8,128)(2,1)} %broadcast_in_dim.28), calls=%async_computation.2 | async-start | bytes 262144 | tf_op jit(solution)/shard_map/all_to_all | solution.py:21
  76.0 1.8 fusion.12
  77.7 3.0 %all-to-all-done.2 = bf16[4,128,128]{2,1,0:T(8,128)(2,1)S(1)} async-done(((bf16[4,128,128]{2,1,0:T(8,128)(2,1)}), bf16[4,128,128]{2,1,0:T(8,128)(2,1)S(1)}, u32[]{:S(2)}, u32[]{:S(2)}) %all-to-all-start.2) | async-done | bytes 131104 | tf_op jit(solution)/shard_map/all_to_all | solution.py:21
  80.8 3.4 %all-to-all-start.3 = ((f32[4,128,128]{2,1,0:T(8,128)}), f32[4,128,128]{2,1,0:T(8,128)S(1)}, u32[]{:S(2)}, u32[]{:S(2)}) async-start(f32[4,128,128]{2,1,0:T(8,128)} %bitcast.10), calls=%async_computation.3 | async-start | bytes 524288 | tf_op jit(solution)/shard_map/all_to_all | solution.py:21
  84.2 0.0 copy-done
  84.2 0.7 fusion.23
  84.9 4.8 %all-to-all-done.3 = f32[4,128,128]{2,1,0:T(8,128)S(1)} async-done(((f32[4,128,128]{2,1,0:T(8,128)}), f32[4,128,128]{2,1,0:T(8,128)S(1)}, u32[]{:S(2)}, u32[]{:S(2)}) %all-to-all-start.3) | async-done | bytes 262176 | tf_op jit(solution)/shard_map/all_to_all | solution.py:21
  89.7 0.1 pad_maximum_fusion.1
  89.8 23.6 %all_to_all.40 = f32[8,288,128]{2,1,0:T(8,128)S(1)} all-to-all(f32[8,288,128]{2,1,0:T(8,128)S(1)} %pad_maximum_fusion.1), channel_id=1, replica_groups=mesh['z'=16,'yh'=2,'x'=4,'yl'=2,'core'=2] {'yl','core','yh'}, dimensions={0} | all-to-all | bytes 2359296 | tf_op jit(solution)/shard_map/all_to_all | solution.py:21
  113.4 0.1 reduce_sum.38
  113.5 27.7 %all_to_all.41 = f32[16,18,128]{2,1,0:T(8,128)S(1)} all-to-all(f32[16,18,128]{2,1,0:T(8,128)S(1)} %pad_maximum_fusion.4), channel_id=1, replica_groups=mesh['z'=16,'yh'=2,'x'=4,'yl'=2,'core'=2] {'z'}, dimensions={0} | all-to-all | bytes 294912 | tf_op jit(solution)/shard_map/all_to_all | solution.py:21
  141.3 20.7 %all_to_all.42 = f32[16,18,128]{2,1,0:T(8,128)S(1)} all-to-all(f32[16,18,128]{2,1,0:T(8,128)S(1)} %broadcast_in_dim.31), channel_id=1, replica_groups=mesh['z'=16,'yh'=2,'x'=4,'yl'=2,'core'=2] {'z'}, dimensions={0} | all-to-all | bytes 294912 | tf_op jit(solution)/shard_map/all_to_all | solution.py:21
  162.0 2.6 %collective-permute-start.3 = (f32[256,128]{1,0:T(8,128)S(1)}, f32[256,128]{1,0:T(8,128)S(1)}, u32[]{:S(2)}, u32[]{:S(2)}) collective-permute-start(f32[256,128]{1,0:T(8,128)S(1)} %bitcast.41), channel_id=1, source_target_pairs={{0,16},{16,0},{1,17},{17,1},{2,18},{18,2},{3,19},{19,3},{4,20},{20... | collective-permute-start | bytes 393224 | tf_op jit(solution)/shard_map/ppermute | solution.py:82
  164.7 0.7 broadcast_in_dim.32
  165.4 8.4 %all-to-all-start.7 = ((f32[16,32,128]{2,1,0:T(8,128)}), f32[16,32,128]{2,1,0:T(8,128)S(1)}, u32[]{:S(2)}, u32[]{:S(2)}) async-start(f32[16,32,128]{2,1,0:T(8,128)} %broadcast_in_dim.32), calls=%async_computation.7 | async-start | bytes 524288 | tf_op jit(solution)/shard_map/all_to_all | solution.py:21
  173.8 0.0 collective-permute-done.3
  173.9 0.7 pad_maximum_fusion.3
  174.6 6.7 %all-to-all-done.7 = f32[16,32,128]{2,1,0:T(8,128)S(1)} async-done(((f32[16,32,128]{2,1,0:T(8,128)}), f32[16,32,128]{2,1,0:T(8,128)S(1)}, u32[]{:S(2)}, u32[]{:S(2)}) %all-to-all-start.7) | async-done | bytes 262176 | tf_op jit(solution)/shard_map/all_to_all | solution.py:21
  181.3 0.7 copy.17
  (13 shorter events, 0.2 us)
Async XLA Ops:
  3.9 5.0 %copy-start.8 = (s32[128]{0:T(128)S(1)}, s32[128]{0:T(128)}, u32[]{:S(2)}) copy-start(s32[128]{0:T(128)} %param.16) | copy-start | bytes 1540
  3.9 5.0 %copy-start.9 = (s32[128]{0:T(128)S(1)}, s32[128]{0:T(128)}, u32[]{:S(2)}) copy-start(s32[128]{0:T(128)} %param.15) | copy-start | bytes 1540
  3.9 5.0 %copy-start.3 = (f32[512,128]{1,0:T(8,128)S(1)}, f32[512,128]{1,0:T(8,128)}, u32[]{:S(2)}) copy-start(f32[512,128]{1,0:T(8,128)} %param.12) | copy-start | bytes 786436
  3.9 6.0 %copy-start.1 = (bf16[512,512]{1,0:T(8,128)(2,1)S(1)}, bf16[512,512]{1,0:T(8,128)(2,1)}, u32[]{:S(2)}) copy-start(bf16[512,512]{1,0:T(8,128)(2,1)} %param.11) | copy-start | bytes 1572868
  3.9 25.4 %all-to-all-start = ((bf16[4,128,2048]{2,1,0:T(8,128)(2,1)}), bf16[4,128,2048]{2,1,0:T(8,128)(2,1)S(1)}, u32[]{:S(2)}, u32[]{:S(2)}) async-start(bf16[4,128,2048]{2,1,0:T(8,128)(2,1)} %pad_maximum_fusion), calls=%async_computation | async-start | bytes 4194304 | tf_op jit(solution)/shard_map/all_to_all | solution.py:21
  9.9 20.0 %collective-permute-start.2 = (bf16[512,640]{1,0:T(8,128)(2,1)S(1)}, bf16[512,640]{1,0:T(8,128)(2,1)}, u32[]{:S(2)}, u32[]{:S(2)}) collective-permute-start(bf16[512,640]{1,0:T(8,128)(2,1)S(1)} %pad_maximum_fusion.2), channel_id=1, source_target_pairs={{0,3},{1,2},{2,1},{3,0},{4,7},{5,6},{6,5},{7,4},{8,11},{9,10},{10,... | collective-permute-start | bytes 1966088 | tf_op jit(solution)/shard_map/ppermute | solution.py:39
  14.0 17.6 %collective-permute-start = (bf16[512,640]{1,0:T(8,128)(2,1)S(1)}, bf16[512,640]{1,0:T(8,128)(2,1)}, u32[]{:S(2)}, u32[]{:S(2)}) collective-permute-start(bf16[512,640]{1,0:T(8,128)(2,1)S(1)} %pad_maximum_fusion.2), channel_id=1, source_target_pairs={{0,1},{1,0},{2,3},{3,2},{4,5},{5,4},{6,7},{7,6},{8,9},{9,8},{10,11... | collective-permute-start | bytes 1966088 | tf_op jit(solution)/shard_map/ppermute | solution.py:39
  19.4 24.0 %collective-permute-start.1 = (bf16[512,640]{1,0:T(8,128)(2,1)S(1)}, bf16[512,640]{1,0:T(8,128)(2,1)}, u32[]{:S(2)}, u32[]{:S(2)}) collective-permute-start(bf16[512,640]{1,0:T(8,128)(2,1)S(1)} %pad_maximum_fusion.2), channel_id=1, source_target_pairs={{0,2},{1,3},{2,0},{3,1},{4,6},{5,7},{6,4},{7,5},{8,10},{9,11},{10,... | collective-permute-start | bytes 1966088 | tf_op jit(solution)/shard_map/ppermute | solution.py:39
  46.1 4.7 %copy-start.10 = (s32[128]{0:T(128)S(1)}, s32[128]{0:T(128)}, u32[]{:S(2)}) copy-start(s32[128]{0:T(128)} %param.17) | copy-start | bytes 1540
  46.2 22.8 %all-to-all-start.1 = ((f32[4,128,640]{2,1,0:T(8,128)}), f32[4,128,640]{2,1,0:T(8,128)S(1)}, u32[]{:S(2)}, u32[]{:S(2)}) async-start(f32[4,128,640]{2,1,0:T(8,128)} %bitcast.39), calls=%async_computation.1 | async-start | bytes 2621440 | tf_op jit(solution)/shard_map/all_to_all | solution.py:21
  53.4 16.4 %copy-start.4 = (f32[128]{0:T(128)S(1)}, f32[128]{0:T(128)}, u32[]{:S(2)}) copy-start(f32[128]{0:T(128)} %param.14) | copy-start | bytes 1540
  53.4 16.4 %copy-start.5 = (f32[512,128]{1,0:T(8,128)S(1)}, f32[512,128]{1,0:T(8,128)}, u32[]{:S(2)}) copy-start(f32[512,128]{1,0:T(8,128)} %param.13) | copy-start | bytes 786436
  53.4 16.4 %copy-start.7 = (bf16[128,512]{1,0:T(8,128)(2,1)S(1)}, bf16[128,512]{1,0:T(8,128)(2,1)}, u32[]{:S(2)}) copy-start(bf16[128,512]{1,0:T(8,128)(2,1)} %param.10) | copy-start | bytes 393220
  69.1 0.7 copy-start.2
  69.8 1.1 copy-start.6
  70.9 13.3 %copy-start = (bf16[512,2048]{0,1:T(8,128)(2,1)S(1)}, bf16[512,2048]{0,1:T(8,128)(2,1)}, u32[]{:S(2)}) copy-start(bf16[512,2048]{0,1:T(8,128)(2,1)} %copy.13) | copy-start | bytes 6291460
  72.7 8.1 %all-to-all-start.2 = ((bf16[4,128,128]{2,1,0:T(8,128)(2,1)}), bf16[4,128,128]{2,1,0:T(8,128)(2,1)S(1)}, u32[]{:S(2)}, u32[]{:S(2)}) async-start(bf16[4,128,128]{2,1,0:T(8,128)(2,1)} %broadcast_in_dim.28), calls=%async_computation.2 | async-start | bytes 262144 | tf_op jit(solution)/shard_map/all_to_all | solution.py:21
  80.8 8.9 %all-to-all-start.3 = ((f32[4,128,128]{2,1,0:T(8,128)}), f32[4,128,128]{2,1,0:T(8,128)S(1)}, u32[]{:S(2)}, u32[]{:S(2)}) async-start(f32[4,128,128]{2,1,0:T(8,128)} %bitcast.10), calls=%async_computation.3 | async-start | bytes 524288 | tf_op jit(solution)/shard_map/all_to_all | solution.py:21
  162.0 11.8 %collective-permute-start.3 = (f32[256,128]{1,0:T(8,128)S(1)}, f32[256,128]{1,0:T(8,128)S(1)}, u32[]{:S(2)}, u32[]{:S(2)}) collective-permute-start(f32[256,128]{1,0:T(8,128)S(1)} %bitcast.41), channel_id=1, source_target_pairs={{0,16},{16,0},{1,17},{17,1},{2,18},{18,2},{3,19},{19,3},{4,20},{20... | collective-permute-start | bytes 393224 | tf_op jit(solution)/shard_map/ppermute | solution.py:82
  165.4 15.9 %all-to-all-start.7 = ((f32[16,32,128]{2,1,0:T(8,128)}), f32[16,32,128]{2,1,0:T(8,128)S(1)}, u32[]{:S(2)}, u32[]{:S(2)}) async-start(f32[16,32,128]{2,1,0:T(8,128)} %broadcast_in_dim.32), calls=%async_computation.7 | async-start | bytes 524288 | tf_op jit(solution)/shard_map/all_to_all | solution.py:21

commit v4 on v3

v4 whole, which is shorter than its diff:
```python
import functools
import math

import jax
import jax.numpy as jnp
from jax import lax
from jax.experimental import pallas as pl
from jax.experimental.pallas import tpu as pltpu
from jax.sharding import Mesh, PartitionSpec as P

AXES = {"z": 16, "yh": 2, "x": 4, "yl": 2, "core": 2}
DP, FSDP, NEAR = ("z", "yh"), ("x", "yl", "core"), ("yl", "core")


def fake_quantize(factor, bits, scale_exps):
    step = jnp.exp2(-scale_exps.astype(jnp.float32))
    upper = jnp.exp2(bits.astype(jnp.float32) - 1.0)
    ratio = factor / step
    smooth = ratio - jnp.sin(2.0 * math.pi * ratio) / (2.0 * math.pi)
    return step * jnp.clip(smooth, -upper, upper - 1.0)


def exchange(parts, axes):
    return lax.all_to_all(parts, axes, 0, 0, tiled=True)


def spread(rows, axes):
    return exchange(jnp.broadcast_to(rows, (lax.axis_size(axes), *rows.shape)), axes)


IN_VMEM = pl.BlockSpec(memory_space=pltpu.VMEM)
IN_SMEM = pl.BlockSpec(memory_space=pltpu.SMEM)
PARAMS = pltpu.CompilerParams(vmem_limit_bytes=40 * 1024 * 1024)


def dot32(a, b, dims=((1,), (0,))):
    return lax.dot_general(a, b, (dims, ((), ())), preferred_element_type=jnp.float32)


def partial_kernel(order_ref, tokens_ref, *refs):
    *piece_refs, out_ref = refs
    n_x, tok, _ = out_ref.shape
    rows = piece_refs[0].shape[0]
    for i in range(n_x):
        total = None
        for k, piece in enumerate(piece_refs):
            start = pl.multiple_of(order_ref[k] * rows, rows)
            term = dot32(tokens_ref[i * tok : (i + 1) * tok, pl.ds(start, rows)], piece[...])
            total = term if total is None else total + term
        out_ref[i] = total


def middle_kernel(scale, parts_ref, target_ref, u_ref, sigma_ref, out_ref):
    n_x, tok, _ = parts_ref.shape
    kvw, rank = u_ref.shape
    out = parts_ref[0]
    for i in range(1, n_x):
        out = out + parts_ref[i]
    sigma = sigma_ref[...]
    u_quant = u_ref[...]
    scaled = (out[:, kvw:] * sigma).astype(jnp.bfloat16)
    residual = out[:, :kvw] + dot32(scaled, u_quant, ((1,), (1,))) - target_ref[...].astype(jnp.float32)
    out_grad = (residual * scale).astype(jnp.bfloat16)
    rank_grad = (dot32(out_grad, u_quant) * sigma).astype(jnp.bfloat16).astype(jnp.float32)
    each = kvw // n_x
    for i in range(n_x):
        out_ref[i, :tok] = rank_grad
        out_ref[i, tok:] = dot32(out_grad[:, i * each : (i + 1) * each], scaled, ((0,), (0,)))


def grads_kernel(tokens_ref, arrived_ref, out_ref):
    n_x, both, rank = arrived_ref.shape
    n_to, packed, _ = out_ref.shape
    tok = tokens_ref.shape[0] // n_x
    half = tokens_ref.shape[1] // n_to
    rank_all = jnp.concatenate([arrived_ref[i, :tok] for i in range(n_x)], axis=0)
    rank_all = rank_all.astype(jnp.bfloat16)
    u_rows = arrived_ref[0, tok:]
    for i in range(1, n_x):
        u_rows = u_rows + arrived_ref[i, tok:]
    u_rows = u_rows.astype(jnp.bfloat16)
    each = packed - half
    n_near = (both - tok) // each
    for i in range(n_to):
        v_rows = dot32(tokens_ref[:, i * half : (i + 1) * half], rank_all, ((0,), (0,)))
        out_ref[i, :half] = v_rows.astype(jnp.bfloat16)
        near = i * n_near // n_to
        out_ref[i, half:] = u_rows[near * each : (near + 1) * each]


def shards(hidden, target, base_weight, v_factor, u_factor, sigma, bits, v_exps, u_exps):
    n_x, n_z, n_yh = lax.axis_size("x"), lax.axis_size("z"), lax.axis_size("yh")
    n_near = lax.axis_size(NEAR)
    tok, _ = hidden.shape
    kvw, rank = u_factor.shape
    rows = v_factor.shape[0]
    me = lax.axis_index(NEAR)
    swap = [(0, 1), (1, 0)]

    v_quant = fake_quantize(v_factor, bits, v_exps).astype(jnp.bfloat16)
    own = jnp.concatenate([base_weight, v_quant], axis=1)
    across = lax.ppermute(own, "yl", swap)
    pieces = [own, lax.ppermute(own, "core", swap), across, lax.ppermute(across, "core", swap)]
    wide = n_near * rows
    columns = jnp.stack([hidden[:, i * wide : (i + 1) * wide] for i in range(n_x)])
    tokens = exchange(columns, "x").reshape(n_x * tok, wide)
    u_quant = fake_quantize(u_factor, bits, u_exps).astype(jnp.bfloat16)

    f32, order = jnp.float32, jnp.bitwise_xor(me, jnp.arange(n_near, dtype=jnp.int32))
    part = pl.pallas_call(
        partial_kernel,
        out_shape=jax.ShapeDtypeStruct((n_x, tok, kvw + rank), f32),
        in_specs=[IN_SMEM] + [IN_VMEM] * (1 + n_near),
        out_specs=IN_VMEM,
        compiler_params=PARAMS,
        name="partial_products",
    )(order, tokens, *pieces)
    scale = 1.0 / math.sqrt(tok * n_z * n_yh * n_x * n_near)
    ranks = pl.pallas_call(
        functools.partial(middle_kernel, scale),
        out_shape=jax.ShapeDtypeStruct((n_x, tok + kvw // n_x, rank), f32),
        in_specs=[IN_VMEM] * 4,
        out_specs=IN_VMEM,
        compiler_params=PARAMS,
        name="residual_and_grad_u",
    )(exchange(part, "x"), target, u_quant, sigma.reshape(1, rank))
    half = rows // n_yh
    parts = pl.pallas_call(
        grads_kernel,
        out_shape=jax.ShapeDtypeStruct((n_near * n_yh, half + kvw // (n_x * n_near), rank), jnp.bfloat16),
        in_specs=[IN_VMEM] * 2,
        out_specs=IN_VMEM,
        compiler_params=PARAMS,
        name="grad_v_packed",
    )(tokens, exchange(ranks, "x"))
    mine = jnp.sum(exchange(parts, (*NEAR, "yh")).astype(f32), axis=0)
    mine = jnp.concatenate(
        [mine[:half].reshape(n_z, -1, rank), mine[half:].reshape(n_z, -1, rank)], axis=1
    )
    mine = jnp.sum(exchange(mine, "z"), axis=0)
    whole = spread(mine, "z")
    per_z = half // n_z
    v_mine = whole[:, :per_z].reshape(-1, rank)
    v_other = lax.ppermute(v_mine, "yh", swap)
    low = lax.axis_index("yh") == 0
    grad_v = jnp.concatenate(
        [jnp.where(low, v_mine, v_other), jnp.where(low, v_other, v_mine)], axis=0
    )
    grad_u = spread(whole[:, per_z:].reshape(-1, rank), FSDP).reshape(kvw, rank)
    return (grad_v, grad_u)


def solution(mesh):
    fine = Mesh(mesh.devices.reshape(tuple(AXES.values())), tuple(AXES))
    in_specs = (
        P((*DP, *FSDP), None),
        P((*DP, *FSDP), None),
        P(FSDP, None),
        P(FSDP, None),
        P(),
        P(),
        P(),
        P(),
        P(),
    )
    out_specs = (P(FSDP, None), P())
    return jax.shard_map(shards, mesh=fine, in_specs=in_specs, out_specs=out_specs, check_vma=False)
```

time: 183 us -> 156 us (0.85)
  waiting for transfers between devices: 46.9 us -> 12.1 us
  blocking collectives: 72 us -> 97.1 us
  matrix products: 11.2 us -> 0 us
  starting transfers between devices: 40.2 us -> 33.5 us
  Pallas kernels: 0 us -> 4.32 us
  local copies, waits for them, and re-layouts: 7.12 us -> 3.17 us
    all_to_all x5 -> x2, waiting for transfers between devices: 36.7 us -> 6.7 us  [exchange(): return lax.all_to_all(parts, axes, 0, 0, tiled=True)]
    all_to_all x3 -> x5, blocking collectives: 72 us -> 97.1 us  [exchange(): return lax.all_to_all(parts, axes, 0, 0, tiled=True)]
    all_to_all x5 -> x2, starting transfers between devices: 24.8 us -> 13.4 us  [exchange(): return lax.all_to_all(parts, axes, 0, 0, tiled=True)]
    dot_general x8 -> x0, matrix products: 11.2 us -> none  [the longest x4 6.64 us: shards(): jnp.dot(lax.dynamic_slice_in_dim(tokens, (me ^ k) * rows, rows, 1), weigh...]
    ppermute x4, waiting for transfers between devices: 10.1 us -> 5.41 us  [the longest x1 3.6 us: shards(): across = lax.ppermute(own, 'yl', swap)]
    ppermute x4, starting transfers between devices: 15.4 us -> 20 us  [the longest x1 7.83 us: shards(): lax.ppermute(across, 'core', swap)]
    pallas_call x0 -> x3, Pallas kernels: none -> 4.32 us  [the longest x1 3.11 us: shards(): pl.pallas_call(partial_kernel, out_shape=jax.ShapeDtypeStruct((n_x, tok,...]
    reshape x1 -> x0, local copies, waits for them, and re-layouts: 2.56 us -> none  [shards(): tokens = exchange(columns, 'x').reshape(n_x * tok, wide)]
  transfers between devices with their start and end apart: 9 -> 6, of which waited for: 6 -> 3; matrix products, arithmetic and copies ran while one was open for 6% -> 2% of each run, Pallas kernels for 0% -> 0%
where the time goes in v4:
time: 156 us; the launch traced here: 155 us
  blocking collectives  97.1 us (62%)
  starting transfers between devices  33.5 us (21%)
  waiting for transfers between devices  12.1 us (8%)
  other arithmetic  4.41 us (3%)
  Pallas kernels  4.32 us (3%)
  local copies, waits for them, and re-layouts  3.17 us (2%)
    all_to_all x5, blocking collectives, exchange(): return lax.all_to_all(parts, axes, 0, 0, tiled=True)  97.1 us
    all_to_all x2, starting transfers between devices, exchange(): return lax.all_to_all(parts, axes, 0, 0, tiled=True)  13.4 us
    ppermute x1, starting transfers between devices, shards(): lax.ppermute(across, 'core', swap)  7.83 us
    all_to_all x2, waiting for transfers between devices, exchange(): return lax.all_to_all(parts, axes, 0, 0, tiled=True)  6.7 us
    ppermute x1, starting transfers between devices, shards(): lax.ppermute(own, 'core', swap)  6.29 us
    ppermute x1, waiting for transfers between devices, shards(): across = lax.ppermute(own, 'yl', swap)  3.6 us
    ppermute x1, starting transfers between devices, shards(): across = lax.ppermute(own, 'yl', swap)  3.2 us
  transfers between devices with their start and end apart: 6, of which 3 were waited for; matrix products, arithmetic and copies ran while one was open for 2% of the time, Pallas kernels for 0%

profile of v4, /device:TPU:1, one launch (start us, length us, event | category | flops | bytes accessed | tf_op | source)
XLA Modules:
  0.0 155.5 jit_solution(1945252465310356265)
XLA Ops:
  0.6 1.7 %slice_bitcast_fusion.3 = (bf16[1,128,2048]{2,1,0:T(8,128)(2,1)S(1)}, bf16[1,128,2048]{2,1,0:T(8,128)(2,1)S(1)}, bf16[1,128,2048]{2,1,0:T(8,128)(2,1)S(1)}, bf16[1,128,2048]{2,1,0:T(8,128)(2,1)S(1)}) fusion(bf16[128,8192]{1,0:T(8,128)(2,1)} %param.9), kind=kLoop, calls=%fused_computation.6 | loop fusion | bytes 4194304 | tf_op jit(solution)/shard_map/stack | solution.py:105
  2.3 1.6 %pad_maximum_fusion = bf16[4,128,2048]{2,1,0:T(8,128)(2,1)} fusion(bf16[1,128,2048]{2,1,0:T(8,128)(2,1)S(1)} %get-tuple-element.4, bf16[1,128,2048]{2,1,0:T(8,128)(2,1)S(1)} %get-tuple-element.5, bf16[1,128,2048]{2,1,0:T(8,128)(2,1)S(1)} %get-tuple-element.3, bf16[1,128,2048]{2,1,0:T(8,128)(2,1)S(1)} %get-tuple-element.2), kind=kLoop, calls=%fused_computation | loop fusion | flops 3145728 | bytes 4194304 | tf_op jit(solution)/shard_map/stack | solution.py:105
  3.9 0.0 copy-start.7
  3.9 0.0 copy-start.5
  3.9 0.0 copy-start.6
  3.9 0.0 copy-start.3
  3.9 0.0 copy-start.4
  3.9 0.0 copy-start.2
  3.9 5.0 %all-to-all-start = ((bf16[4,128,2048]{2,1,0:T(8,128)(2,1)}), bf16[4,128,2048]{2,1,0:T(8,128)(2,1)S(1)}, u32[]{:S(2)}, u32[]{:S(2)}) async-start(bf16[4,128,2048]{2,1,0:T(8,128)(2,1)} %pad_maximum_fusion), calls=%async_computation | async-start | bytes 4194304 | tf_op jit(solution)/shard_map/all_to_all | solution.py:24
  8.9 0.0 copy-done.7
  8.9 0.0 copy-done.5
  8.9 0.0 copy-done.6
  9.0 0.0 copy-done.3
  9.0 0.0 copy-done.4
  9.0 1.9 %multiply_convert_fusion = (bf16[512,128]{1,0:T(8,128)(2,1)S(1)}, bf16[512,128]{1,0:T(8,128)(2,1)S(1)}) fusion(f32[512,128]{1,0:T(8,128)S(1)} %copy-done.3, f32[128]{0:T(128)S(1)} %get-tuple-element.12, f32[128]{0:T(128)S(1)} %get-tuple-element.11, f32[128]{0:T(128)S(1)} %get-tuple-element.10, f32[512,128]{1,0:T(8,128)S(1)} %copy-done.4, ...), kind=kLoop, calls=%fused_computation.8 | loop fusion | flops 1048576 | bytes 788480 | tf_op jit(solution)/shard_map/convert_element_type | solution.py:107
  10.9 0.0 copy-done.2
  10.9 0.1 pad_maximum_fusion.1.refs_0_
  10.9 3.2 %collective-permute-start.1 = (bf16[512,640]{1,0:T(8,128)(2,1)S(1)}, bf16[512,640]{1,0:T(8,128)(2,1)S(1)}, u32[]{:S(2)}, u32[]{:S(2)}) collective-permute-start(bf16[512,640]{1,0:T(8,128)(2,1)S(1)} %pad_maximum_fusion.1.refs_0_), channel_id=1, source_target_pairs={{0,2},{2,0},{1,3},{3,1},{4,6},{6,4},{5,7},{7,5},{8,10},{10,8},{9,1... | collective-permute-start | bytes 1966088 | tf_op jit(solution)/shard_map/ppermute | solution.py:102
  14.2 6.3 %collective-permute-start = (bf16[512,640]{1,0:T(8,128)(2,1)S(1)}, bf16[512,640]{1,0:T(8,128)(2,1)}, u32[]{:S(2)}, u32[]{:S(2)}) collective-permute-start(bf16[512,640]{1,0:T(8,128)(2,1)S(1)} %pad_maximum_fusion.1.refs_0_), channel_id=1, source_target_pairs={{0,1},{1,0},{2,3},{3,2},{4,5},{5,4},{6,7},{7,6},{8,9},{9,8},{10,11... | collective-permute-start | bytes 1966088 | tf_op jit(solution)/shard_map/ppermute | solution.py:103
  20.4 3.6 %collective-permute-done.1.refs_2_ = bf16[512,640]{1,0:T(8,128)(2,1)S(1)} collective-permute-done((bf16[512,640]{1,0:T(8,128)(2,1)S(1)}, bf16[512,640]{1,0:T(8,128)(2,1)S(1)}, u32[]{:S(2)}, u32[]{:S(2)}) %collective-permute-start.1) | collective-permute-done | bytes 655392 | tf_op jit(solution)/shard_map/ppermute | solution.py:102
  24.1 7.8 %collective-permute-start.2 = (bf16[512,640]{1,0:T(8,128)(2,1)S(1)}, bf16[512,640]{1,0:T(8,128)(2,1)}, u32[]{:S(2)}, u32[]{:S(2)}) collective-permute-start(bf16[512,640]{1,0:T(8,128)(2,1)S(1)} %collective-permute-done.1.refs_2_), channel_id=1, source_target_pairs={{0,1},{1,0},{2,3},{3,2},{4,5},{5,4},{6,7},{7,6},{8,9},{9,8},{10,11... | collective-permute-start | bytes 1966088 | tf_op jit(solution)/shard_map/ppermute | solution.py:103
  31.9 0.0 collective-permute-done.refs_1_
  31.9 1.8 %collective-permute-done.2.refs_3_ = bf16[512,640]{1,0:T(8,128)(2,1)} collective-permute-done((bf16[512,640]{1,0:T(8,128)(2,1)S(1)}, bf16[512,640]{1,0:T(8,128)(2,1)}, u32[]{:S(2)}, u32[]{:S(2)}) %collective-permute-start.2) | collective-permute-done | bytes 655392 | tf_op jit(solution)/shard_map/ppermute | solution.py:103
  33.7 0.0 all-to-all-done
  33.7 3.1 %partial_products.1 = f32[4,128,640]{2,1,0:T(8,128)S(1)} custom-call(s32[4]{0:T(128)S(1)} %iota_xor_fusion.order_ref, bf16[512,2048]{1,0:T(8,128)(2,1)S(1)} %bitcast.17, bf16[512,640]{1,0:T(8,128)(2,1)S(1)} %pad_maximum_fusion.1.refs_0_, bf16[512,640]{1,0:T(8,128)(2,1)} %collective-permute-done.refs_1_, bf16[512,640]{1,0:T(8,128)(2,1)S(1)} %collective-permute-done.1.refs_2_, ...), custom_call_target="tpu_custom_call" | custom-call | tf_op jit(solution)/shard_map/partial_products/pallas_call | solution.py:110
  36.8 0.0 copy-start
  36.9 0.0 copy-start.1
  36.9 21.2 %all_to_all.35.parts_ref = f32[4,128,640]{2,1,0:T(8,128)S(1)} all-to-all(f32[4,128,640]{2,1,0:T(8,128)S(1)} %partial_products.1), channel_id=1, replica_groups=mesh['z'=16,'yh'=2,'x'=4,'yl'=2,'core'=2] {'x'}, dimensions={0} | all-to-all | bytes 2621440 | tf_op jit(solution)/shard_map/all_to_all | solution.py:24
  58.1 0.0 copy-done
  58.1 0.0 copy-done.1
  58.1 0.4 residual_and_grad_u.1
  58.5 10.1 %all_to_all.36.arrived_ref = f32[4,256,128]{2,1,0:T(8,128)S(1)} all-to-all(f32[4,256,128]{2,1,0:T(8,128)S(1)} %residual_and_grad_u.1), channel_id=1, replica_groups=mesh['z'=16,'yh'=2,'x'=4,'yl'=2,'core'=2] {'x'}, dimensions={0} | all-to-all | bytes 1048576 | tf_op jit(solution)/shard_map/all_to_all | solution.py:24
  68.6 0.8 grad_v_packed.1
  69.4 17.4 %all_to_all.37 = bf16[8,288,128]{2,1,0:T(8,128)(2,1)S(1)} all-to-all(bf16[8,288,128]{2,1,0:T(8,128)(2,1)S(1)} %grad_v_packed.1), channel_id=1, replica_groups=mesh['z'=16,'yh'=2,'x'=4,'yl'=2,'core'=2] {'yl','core','yh'}, dimensions={0} | all-to-all | bytes 1179648 | tf_op jit(solution)/shard_map/all_to_all | solution.py:24
  86.8 0.1 convert_reduce_fusion
  86.9 27.6 %all_to_all.38 = f32[16,18,128]{2,1,0:T(8,128)S(1)} all-to-all(f32[16,18,128]{2,1,0:T(8,128)S(1)} %pad_maximum_fusion.3), channel_id=1, replica_groups=mesh['z'=16,'yh'=2,'x'=4,'yl'=2,'core'=2] {'z'}, dimensions={0} | all-to-all | bytes 294912 | tf_op jit(solution)/shard_map/all_to_all | solution.py:24
  114.5 20.9 %all_to_all.39 = f32[16,18,128]{2,1,0:T(8,128)S(1)} all-to-all(f32[16,18,128]{2,1,0:T(8,128)S(1)} %broadcast_in_dim.16), channel_id=1, replica_groups=mesh['z'=16,'yh'=2,'x'=4,'yl'=2,'core'=2] {'z'}, dimensions={0} | all-to-all | bytes 294912 | tf_op jit(solution)/shard_map/all_to_all | solution.py:24
  135.4 2.7 %collective-permute-start.3 = (f32[256,128]{1,0:T(8,128)S(1)}, f32[256,128]{1,0:T(8,128)S(1)}, u32[]{:S(2)}, u32[]{:S(2)}) collective-permute-start(f32[256,128]{1,0:T(8,128)S(1)} %bitcast.21), channel_id=1, source_target_pairs={{0,16},{16,0},{1,17},{17,1},{2,18},{18,2},{3,19},{19,3},{4,20},{20... | collective-permute-start | bytes 393224 | tf_op jit(solution)/shard_map/ppermute | solution.py:144
  138.1 0.7 broadcast_in_dim.17
  138.9 8.4 %all-to-all-start.6 = ((f32[16,32,128]{2,1,0:T(8,128)}), f32[16,32,128]{2,1,0:T(8,128)S(1)}, u32[]{:S(2)}, u32[]{:S(2)}) async-start(f32[16,32,128]{2,1,0:T(8,128)} %broadcast_in_dim.17), calls=%async_computation.6 | async-start | bytes 524288 | tf_op jit(solution)/shard_map/all_to_all | solution.py:24
  147.3 0.0 collective-permute-done.3
  147.3 0.7 pad_maximum_fusion.2
  148.1 6.7 %all-to-all-done.6 = f32[16,32,128]{2,1,0:T(8,128)S(1)} async-done(((f32[16,32,128]{2,1,0:T(8,128)}), f32[16,32,128]{2,1,0:T(8,128)S(1)}, u32[]{:S(2)}, u32[]{:S(2)}) %all-to-all-start.6) | async-done | bytes 262176 | tf_op jit(solution)/shard_map/all_to_all | solution.py:24
  154.8 0.7 copy.14
  (11 shorter events, 0.1 us)
Async XLA Ops:
  3.9 5.0 %copy-start.7 = (s32[128]{0:T(128)S(1)}, s32[128]{0:T(128)}, u32[]{:S(2)}) copy-start(s32[128]{0:T(128)} %param.15) | copy-start | bytes 1540
  3.9 5.0 %copy-start.5 = (s32[128]{0:T(128)S(1)}, s32[128]{0:T(128)}, u32[]{:S(2)}) copy-start(s32[128]{0:T(128)} %param.17) | copy-start | bytes 1540
  3.9 5.0 %copy-start.6 = (s32[128]{0:T(128)S(1)}, s32[128]{0:T(128)}, u32[]{:S(2)}) copy-start(s32[128]{0:T(128)} %param.16) | copy-start | bytes 1540
  3.9 5.1 %copy-start.3 = (f32[512,128]{1,0:T(8,128)S(1)}, f32[512,128]{1,0:T(8,128)}, u32[]{:S(2)}) copy-start(f32[512,128]{1,0:T(8,128)} %param.13) | copy-start | bytes 786436
  3.9 5.1 %copy-start.4 = (f32[512,128]{1,0:T(8,128)S(1)}, f32[512,128]{1,0:T(8,128)}, u32[]{:S(2)}) copy-start(f32[512,128]{1,0:T(8,128)} %param.12) | copy-start | bytes 786436
  3.9 7.0 %copy-start.2 = (bf16[512,512]{1,0:T(8,128)(2,1)S(1)}, bf16[512,512]{1,0:T(8,128)(2,1)}, u32[]{:S(2)}) copy-start(bf16[512,512]{1,0:T(8,128)(2,1)} %param.11) | copy-start | bytes 1572868
  3.9 29.8 %all-to-all-start = ((bf16[4,128,2048]{2,1,0:T(8,128)(2,1)}), bf16[4,128,2048]{2,1,0:T(8,128)(2,1)S(1)}, u32[]{:S(2)}, u32[]{:S(2)}) async-start(bf16[4,128,2048]{2,1,0:T(8,128)(2,1)} %pad_maximum_fusion), calls=%async_computation | async-start | bytes 4194304 | tf_op jit(solution)/shard_map/all_to_all | solution.py:24
  10.9 13.1 %collective-permute-start.1 = (bf16[512,640]{1,0:T(8,128)(2,1)S(1)}, bf16[512,640]{1,0:T(8,128)(2,1)S(1)}, u32[]{:S(2)}, u32[]{:S(2)}) collective-permute-start(bf16[512,640]{1,0:T(8,128)(2,1)S(1)} %pad_maximum_fusion.1.refs_0_), channel_id=1, source_target_pairs={{0,2},{2,0},{1,3},{3,1},{4,6},{6,4},{5,7},{7,5},{8,10},{10,8},{9,1... | collective-permute-start | bytes 1966088 | tf_op jit(solution)/shard_map/ppermute | solution.py:102
  14.2 17.8 %collective-permute-start = (bf16[512,640]{1,0:T(8,128)(2,1)S(1)}, bf16[512,640]{1,0:T(8,128)(2,1)}, u32[]{:S(2)}, u32[]{:S(2)}) collective-permute-start(bf16[512,640]{1,0:T(8,128)(2,1)S(1)} %pad_maximum_fusion.1.refs_0_), channel_id=1, source_target_pairs={{0,1},{1,0},{2,3},{3,2},{4,5},{5,4},{6,7},{7,6},{8,9},{9,8},{10,11... | collective-permute-start | bytes 1966088 | tf_op jit(solution)/shard_map/ppermute | solution.py:103
  24.1 9.7 %collective-permute-start.2 = (bf16[512,640]{1,0:T(8,128)(2,1)S(1)}, bf16[512,640]{1,0:T(8,128)(2,1)}, u32[]{:S(2)}, u32[]{:S(2)}) collective-permute-start(bf16[512,640]{1,0:T(8,128)(2,1)S(1)} %collective-permute-done.1.refs_2_), channel_id=1, source_target_pairs={{0,1},{1,0},{2,3},{3,2},{4,5},{5,4},{6,7},{7,6},{8,9},{9,8},{10,11... | collective-permute-start | bytes 1966088 | tf_op jit(solution)/shard_map/ppermute | solution.py:103
  36.8 21.2 %copy-start = (bf16[128,512]{1,0:T(8,128)(2,1)S(1)}, bf16[128,512]{1,0:T(8,128)(2,1)}, u32[]{:S(2)}) copy-start(bf16[128,512]{1,0:T(8,128)(2,1)} %target_ref.1) | copy-start | bytes 393220
  36.9 21.2 %copy-start.1 = (f32[128]{0:T(128)S(1)}, f32[128]{0:T(128)}, u32[]{:S(2)}) copy-start(f32[128]{0:T(128)} %param.14) | copy-start | bytes 1540
  135.4 11.9 %collective-permute-start.3 = (f32[256,128]{1,0:T(8,128)S(1)}, f32[256,128]{1,0:T(8,128)S(1)}, u32[]{:S(2)}, u32[]{:S(2)}) collective-permute-start(f32[256,128]{1,0:T(8,128)S(1)} %bitcast.21), channel_id=1, source_target_pairs={{0,16},{16,0},{1,17},{17,1},{2,18},{18,2},{3,19},{19,3},{4,20},{20... | collective-permute-start | bytes 393224 | tf_op jit(solution)/shard_map/ppermute | solution.py:144
  138.9 15.9 %all-to-all-start.6 = ((f32[16,32,128]{2,1,0:T(8,128)}), f32[16,32,128]{2,1,0:T(8,128)S(1)}, u32[]{:S(2)}, u32[]{:S(2)}) async-start(f32[16,32,128]{2,1,0:T(8,128)} %broadcast_in_dim.17), calls=%async_computation.6 | async-start | bytes 524288 | tf_op jit(solution)/shard_map/all_to_all | solution.py:24

commit v5 on v4

v5 whole, which is shorter than its diff:
```python
import functools
import math

import jax
import jax.numpy as jnp
from jax import lax
from jax.experimental import pallas as pl
from jax.experimental.pallas import tpu as pltpu
from jax.sharding import Mesh, PartitionSpec as P

AXES = {"z1": 4, "z0": 4, "yh": 2, "x": 4, "yl": 2, "core": 2}
DP, FSDP, NEAR = ("z1", "z0", "yh"), ("x", "yl", "core"), ("yl", "core")
CLOSE, FAR = (*NEAR, "yh", "z0"), ("z1", "yh")


def fake_quantize(factor, bits, scale_exps):
    step = jnp.exp2(-scale_exps.astype(jnp.float32))
    upper = jnp.exp2(bits.astype(jnp.float32) - 1.0)
    ratio = factor / step
    smooth = ratio - jnp.sin(2.0 * math.pi * ratio) / (2.0 * math.pi)
    return step * jnp.clip(smooth, -upper, upper - 1.0)


def exchange(parts, axes):
    return lax.all_to_all(parts, axes, 0, 0, tiled=True)


IN_VMEM = pl.BlockSpec(memory_space=pltpu.VMEM)
IN_SMEM = pl.BlockSpec(memory_space=pltpu.SMEM)
PARAMS = pltpu.CompilerParams(vmem_limit_bytes=40 * 1024 * 1024)


def dot32(a, b, dims=((1,), (0,))):
    return lax.dot_general(a, b, (dims, ((), ())), preferred_element_type=jnp.float32)


def partial_kernel(order_ref, tokens_ref, *refs):
    *piece_refs, out_ref = refs
    n_x, tok, _ = out_ref.shape
    rows = piece_refs[0].shape[0]
    for i in range(n_x):
        total = None
        for k, piece in enumerate(piece_refs):
            start = pl.multiple_of(order_ref[k] * rows, rows)
            term = dot32(tokens_ref[i * tok : (i + 1) * tok, pl.ds(start, rows)], piece[...])
            total = term if total is None else total + term
        out_ref[i] = total


def middle_kernel(scale, parts_ref, target_ref, u_ref, sigma_ref, out_ref):
    n_x, tok, _ = parts_ref.shape
    kvw, rank = u_ref.shape
    out = parts_ref[0]
    for i in range(1, n_x):
        out = out + parts_ref[i]
    sigma = sigma_ref[...]
    u_quant = u_ref[...]
    scaled = (out[:, kvw:] * sigma).astype(jnp.bfloat16)
    residual = out[:, :kvw] + dot32(scaled, u_quant, ((1,), (1,))) - target_ref[...].astype(jnp.float32)
    out_grad = (residual * scale).astype(jnp.bfloat16)
    rank_grad = (dot32(out_grad, u_quant) * sigma).astype(jnp.bfloat16).astype(jnp.float32)
    each = kvw // n_x
    for i in range(n_x):
        out_ref[i, :tok] = rank_grad
        out_ref[i, tok:] = dot32(out_grad[:, i * each : (i + 1) * each], scaled, ((0,), (0,)))


def grads_kernel(tokens_ref, arrived_ref, out_ref):
    n_x, _, rank = arrived_ref.shape
    n_to, packed, _ = out_ref.shape
    tok = tokens_ref.shape[0] // n_x
    v_rows = tokens_ref.shape[1] // n_to
    u_rows = packed - v_rows
    rank_all = jnp.concatenate([arrived_ref[i, :tok] for i in range(n_x)], axis=0)
    rank_all = rank_all.astype(jnp.bfloat16)
    u_sum = arrived_ref[0, tok:]
    for i in range(1, n_x):
        u_sum = u_sum + arrived_ref[i, tok:]
    u_sum = u_sum.astype(jnp.bfloat16)
    repeat = n_to * u_rows // u_sum.shape[0]
    wide = repeat * v_rows
    for j in range(n_to // repeat):
        v_part = dot32(tokens_ref[:, j * wide : (j + 1) * wide], rank_all, ((0,), (0,)))
        v_part = v_part.astype(jnp.bfloat16)
        for i in range(repeat):
            out_ref[j * repeat + i, :v_rows] = v_part[i * v_rows : (i + 1) * v_rows]
            out_ref[j * repeat + i, v_rows:] = u_sum[j * u_rows : (j + 1) * u_rows]


def close_sum_kernel(arrived_ref, out_ref):
    total = arrived_ref[0].astype(jnp.float32)
    for i in range(1, arrived_ref.shape[0]):
        total = total + arrived_ref[i].astype(jnp.float32)
    for i in range(out_ref.shape[0]):
        out_ref[i] = total.astype(out_ref.dtype)


def far_sum_kernel(arrived_ref, v_ref, u_ref):
    n_yh = 2
    v_rows = v_ref.shape[0] // n_yh
    u_rows = u_ref.shape[1] // n_yh
    for h in range(n_yh):
        total = arrived_ref[h].astype(jnp.float32)
        for i in range(h + n_yh, arrived_ref.shape[0], n_yh):
            total = total + arrived_ref[i].astype(jnp.float32)
        v_ref[h * v_rows : (h + 1) * v_rows] = total[:v_rows]
        for i in range(u_ref.shape[0]):
            u_ref[i, h * u_rows : (h + 1) * u_rows] = total[v_rows:]


def place_kernel(order_ref, *refs):
    *piece_refs, out_ref = refs
    n_yh = 2
    rows = piece_refs[0].shape[0] // n_yh
    half = out_ref.shape[0] // n_yh
    for k, piece in enumerate(piece_refs):
        for h in range(n_yh):
            start = pl.multiple_of(h * half + order_ref[k] * rows, rows)
            out_ref[pl.ds(start, rows)] = piece[h * rows : (h + 1) * rows]


def kernel_call(kernel, out, name, operands, scalars=0):
    return pl.pallas_call(
        kernel,
        out_shape=out,
        in_specs=[IN_SMEM] * scalars + [IN_VMEM] * (len(operands) - scalars),
        out_specs=jax.tree.map(lambda _: IN_VMEM, out),
        compiler_params=PARAMS,
        name=name,
    )(*operands)


def shards(hidden, target, base_weight, v_factor, u_factor, sigma, bits, v_exps, u_exps):
    n_x, n_z0, n_near = lax.axis_size("x"), lax.axis_size("z0"), lax.axis_size(NEAR)
    tok, _ = hidden.shape
    kvw, rank = u_factor.shape
    rows = v_factor.shape[0]
    me = lax.axis_index(NEAR)
    swap = [(0, 1), (1, 0)]

    v_quant = fake_quantize(v_factor, bits, v_exps).astype(jnp.bfloat16)
    own = jnp.concatenate([base_weight, v_quant], axis=1)
    across = lax.ppermute(own, "yl", swap)
    pieces = [own, lax.ppermute(own, "core", swap), across, lax.ppermute(across, "core", swap)]
    wide = n_near * rows
    columns = jnp.stack([hidden[:, i * wide : (i + 1) * wide] for i in range(n_x)])
    tokens = exchange(columns, "x").reshape(n_x * tok, wide)
    u_quant = fake_quantize(u_factor, bits, u_exps).astype(jnp.bfloat16)

    f32, bf16 = jnp.float32, jnp.bfloat16
    shape = jax.ShapeDtypeStruct
    order = jnp.bitwise_xor(me, jnp.arange(n_near, dtype=jnp.int32))
    part = kernel_call(
        partial_kernel,
        shape((n_x, tok, kvw + rank), f32),
        "partial_products",
        (order, tokens, *pieces),
        scalars=1,
    )
    scale = 1.0 / math.sqrt(tok * math.prod(lax.axis_size(a) for a in AXES))
    ranks = kernel_call(
        functools.partial(middle_kernel, scale),
        shape((n_x, tok + kvw // n_x, rank), f32),
        "residual_and_grad_u",
        (exchange(part, "x"), target, u_quant, sigma.reshape(1, rank)),
    )
    n_close, n_far = lax.axis_size(CLOSE), lax.axis_size(FAR)
    v_rows, u_rows = wide // n_close, kvw * n_z0 // (n_x * n_close)
    parts = kernel_call(
        grads_kernel,
        shape((n_close, v_rows + u_rows, rank), bf16),
        "grads_packed",
        (tokens, exchange(ranks, "x")),
    )
    mine = kernel_call(
        close_sum_kernel,
        shape((n_far, v_rows + u_rows, rank), bf16),
        "close_sum",
        (exchange(parts, CLOSE),),
    )
    v_mine, u_mine = kernel_call(
        far_sum_kernel,
        (shape((2 * v_rows, rank), f32), shape((lax.axis_size(FSDP), 2 * u_rows, rank), f32)),
        "far_sum",
        (exchange(mine, FAR),),
    )
    grad_u = exchange(u_mine, FSDP).reshape(kvw, rank)
    v_pieces = [v_mine]
    for k in range(1, n_z0):
        v_pieces.append(lax.ppermute(v_mine, "z0", [(j, (j + k) % n_z0) for j in range(n_z0)]))
    order = jnp.remainder(lax.axis_index("z0") - jnp.arange(n_z0, dtype=jnp.int32), n_z0)
    grad_v = kernel_call(
        place_kernel, shape((rows, rank), f32), "grad_v", (order, *v_pieces), scalars=1
    )
    return (grad_v, grad_u)


def solution(mesh):
    fine = Mesh(mesh.devices.reshape(tuple(AXES.values())), tuple(AXES))
    in_specs = (
        P((*DP, *FSDP), None),
        P((*DP, *FSDP), None),
        P(FSDP, None),
        P(FSDP, None),
        P(),
        P(),
        P(),
        P(),
        P(),
    )
    out_specs = (P(FSDP, None), P())
    return jax.shard_map(shards, mesh=fine, in_specs=in_specs, out_specs=out_specs, check_vma=False)
```

time: 156 us -> 149 us (0.955)
  blocking collectives: 97.1 us -> 88.2 us
  starting transfers between devices: 33.5 us -> 38.6 us
  waiting for transfers between devices: 12.1 us -> 8.31 us
  Pallas kernels: 4.32 us -> 6.42 us
    all_to_all x5 -> x4, blocking collectives: 97.1 us -> 88.2 us  [exchange(): return lax.all_to_all(parts, axes, 0, 0, tiled=True)]
    ppermute x1 -> x3, starting transfers between devices: 2.72 us -> 9.74 us  [shards(): lax.ppermute(v_mine, 'z0', [(j, (j + k) % n_z0) for j in range(n_z0)])]
    all_to_all x2, waiting for transfers between devices: 6.7 us -> 0.01 us  [exchange(): return lax.all_to_all(parts, axes, 0, 0, tiled=True)]
    ppermute x1 -> x3, waiting for transfers between devices: 0.01 us -> 2.89 us  [shards(): lax.ppermute(v_mine, 'z0', [(j, (j + k) % n_z0) for j in range(n_z0)])]
    pallas_call x3 -> x6, Pallas kernels: 4.32 us -> 6.42 us  [kernel_call(): pl.pallas_call(kernel, out_shape=out, in_specs=[IN_SMEM] * scalars + [IN_...]
    all_to_all x2, starting transfers between devices: 13.4 us -> 11.6 us  [exchange(): return lax.all_to_all(parts, axes, 0, 0, tiled=True)]
  transfers between devices with their start and end apart: 6 -> 8, of which waited for: 3 -> 4; matrix products, arithmetic and copies ran while one was open for 2% -> 1% of each run, Pallas kernels for 0% -> 1%
where the time goes in v5:
time: 149 us; the launch traced here: 148 us
  blocking collectives  88.2 us (59%)
  starting transfers between devices  38.6 us (26%)
  waiting for transfers between devices  8.31 us (6%)
  Pallas kernels  6.42 us (4%)
  other arithmetic  3.56 us (2%)
  local copies, waits for them, and re-layouts  2.4 us (2%)
    all_to_all x4, blocking collectives, exchange(): return lax.all_to_all(parts, axes, 0, 0, tiled=True)  88.2 us
    all_to_all x2, starting transfers between devices, exchange(): return lax.all_to_all(parts, axes, 0, 0, tiled=True)  11.6 us
    ppermute x3, starting transfers between devices, shards(): lax.ppermute(v_mine, 'z0', [(j, (j + k) % n_z0) for j in range(n_z0)])  9.74 us
    ppermute x1, starting transfers between devices, shards(): lax.ppermute(across, 'core', swap)  7.83 us
    pallas_call x6, Pallas kernels, kernel_call(): pl.pallas_call(kernel, out_shape=out, in_specs=[IN_SMEM] * scalars + [IN_...  6.42 us
    ppermute x1, starting transfers between devices, shards(): lax.ppermute(own, 'core', swap)  6.29 us
    ppermute x1, waiting for transfers between devices, shards(): across = lax.ppermute(own, 'yl', swap)  3.6 us
    ppermute x1, starting transfers between devices, shards(): across = lax.ppermute(own, 'yl', swap)  3.2 us
  transfers between devices with their start and end apart: 8, of which 4 were waited for; matrix products, arithmetic and copies ran while one was open for 1% of the time, Pallas kernels for 1%

profile of v5, /device:TPU:1, one launch (start us, length us, event | category | flops | bytes accessed | tf_op | source)
XLA Modules:
  0.0 148.4 jit_solution(18170300529147814735)
XLA Ops:
  0.6 1.7 %slice_bitcast_fusion.3 = (bf16[1,128,2048]{2,1,0:T(8,128)(2,1)S(1)}, bf16[1,128,2048]{2,1,0:T(8,128)(2,1)S(1)}, bf16[1,128,2048]{2,1,0:T(8,128)(2,1)S(1)}, bf16[1,128,2048]{2,1,0:T(8,128)(2,1)S(1)}) fusion(bf16[128,8192]{1,0:T(8,128)(2,1)} %param.9), kind=kLoop, calls=%fused_computation.5 | loop fusion | bytes 4194304 | tf_op jit(solution)/shard_map/stack | solution.py:146
  2.3 1.6 %pad_maximum_fusion = bf16[4,128,2048]{2,1,0:T(8,128)(2,1)} fusion(bf16[1,128,2048]{2,1,0:T(8,128)(2,1)S(1)} %get-tuple-element.8, bf16[1,128,2048]{2,1,0:T(8,128)(2,1)S(1)} %get-tuple-element.9, bf16[1,128,2048]{2,1,0:T(8,128)(2,1)S(1)} %get-tuple-element.7, bf16[1,128,2048]{2,1,0:T(8,128)(2,1)S(1)} %get-tuple-element.6), kind=kLoop, calls=%fused_computation | loop fusion | flops 3145728 | bytes 4194304 | tf_op jit(solution)/shard_map/stack | solution.py:146
  3.9 0.0 copy-start.7
  3.9 0.0 copy-start.5
  3.9 0.0 copy-start.6
  3.9 0.0 copy-start.3
  3.9 0.0 copy-start.4
  3.9 0.0 copy-start.2
  3.9 5.0 %all-to-all-start = ((bf16[4,128,2048]{2,1,0:T(8,128)(2,1)}), bf16[4,128,2048]{2,1,0:T(8,128)(2,1)S(1)}, u32[]{:S(2)}, u32[]{:S(2)}) async-start(bf16[4,128,2048]{2,1,0:T(8,128)(2,1)} %pad_maximum_fusion), calls=%async_computation | async-start | bytes 4194304 | tf_op jit(solution)/shard_map/all_to_all | solution.py:25
  8.9 0.0 copy-done.7
  8.9 0.0 copy-done.5
  8.9 0.0 copy-done.6
  9.0 0.0 copy-done.3
  9.0 0.0 copy-done.4
  9.0 1.9 %multiply_convert_fusion = (bf16[512,128]{1,0:T(8,128)(2,1)S(1)}, bf16[512,128]{1,0:T(8,128)(2,1)S(1)}) fusion(f32[512,128]{1,0:T(8,128)S(1)} %copy-done.3, f32[128]{0:T(128)S(1)} %get-tuple-element.14, f32[128]{0:T(128)S(1)} %get-tuple-element.13, f32[128]{0:T(128)S(1)} %get-tuple-element.12, f32[512,128]{1,0:T(8,128)S(1)} %copy-done.4, ...), kind=kLoop, calls=%fused_computation.6 | loop fusion | flops 1048576 | bytes 788480 | tf_op jit(solution)/shard_map/convert_element_type | solution.py:148
  10.9 0.0 copy-done.2
  10.9 0.1 pad_maximum_fusion.1.refs_0_
  10.9 3.2 %collective-permute-start.1 = (bf16[512,640]{1,0:T(8,128)(2,1)S(1)}, bf16[512,640]{1,0:T(8,128)(2,1)S(1)}, u32[]{:S(2)}, u32[]{:S(2)}) collective-permute-start(bf16[512,640]{1,0:T(8,128)(2,1)S(1)} %pad_maximum_fusion.1.refs_0_), channel_id=1, source_target_pairs={{0,2},{2,0},{1,3},{3,1},{4,6},{6,4},{5,7},{7,5},{8,10},{10,8},{9,1... | collective-permute-start | bytes 1966088 | tf_op jit(solution)/shard_map/ppermute | solution.py:143
  14.1 6.3 %collective-permute-start = (bf16[512,640]{1,0:T(8,128)(2,1)S(1)}, bf16[512,640]{1,0:T(8,128)(2,1)}, u32[]{:S(2)}, u32[]{:S(2)}) collective-permute-start(bf16[512,640]{1,0:T(8,128)(2,1)S(1)} %pad_maximum_fusion.1.refs_0_), channel_id=1, source_target_pairs={{0,1},{1,0},{2,3},{3,2},{4,5},{5,4},{6,7},{7,6},{8,9},{9,8},{10,11... | collective-permute-start | bytes 1966088 | tf_op jit(solution)/shard_map/ppermute | solution.py:144
  20.4 3.6 %collective-permute-done.1.refs_2_ = bf16[512,640]{1,0:T(8,128)(2,1)S(1)} collective-permute-done((bf16[512,640]{1,0:T(8,128)(2,1)S(1)}, bf16[512,640]{1,0:T(8,128)(2,1)S(1)}, u32[]{:S(2)}, u32[]{:S(2)}) %collective-permute-start.1) | collective-permute-done | bytes 655392 | tf_op jit(solution)/shard_map/ppermute | solution.py:143
  24.0 7.8 %collective-permute-start.2 = (bf16[512,640]{1,0:T(8,128)(2,1)S(1)}, bf16[512,640]{1,0:T(8,128)(2,1)}, u32[]{:S(2)}, u32[]{:S(2)}) collective-permute-start(bf16[512,640]{1,0:T(8,128)(2,1)S(1)} %collective-permute-done.1.refs_2_), channel_id=1, source_target_pairs={{0,1},{1,0},{2,3},{3,2},{4,5},{5,4},{6,7},{7,6},{8,9},{9,8},{10,11... | collective-permute-start | bytes 1966088 | tf_op jit(solution)/shard_map/ppermute | solution.py:144
  31.9 0.0 collective-permute-done.refs_1_
  31.9 1.8 %collective-permute-done.2.refs_3_ = bf16[512,640]{1,0:T(8,128)(2,1)} collective-permute-done((bf16[512,640]{1,0:T(8,128)(2,1)S(1)}, bf16[512,640]{1,0:T(8,128)(2,1)}, u32[]{:S(2)}, u32[]{:S(2)}) %collective-permute-start.2) | collective-permute-done | bytes 655392 | tf_op jit(solution)/shard_map/ppermute | solution.py:144
  33.7 0.0 all-to-all-done
  33.7 3.1 %partial_products.1 = f32[4,128,640]{2,1,0:T(8,128)S(1)} custom-call(s32[4]{0:T(128)S(1)} %iota_xor_fusion.order_ref, bf16[512,2048]{1,0:T(8,128)(2,1)S(1)} %bitcast.11, bf16[512,640]{1,0:T(8,128)(2,1)S(1)} %pad_maximum_fusion.1.refs_0_, bf16[512,640]{1,0:T(8,128)(2,1)} %collective-permute-done.refs_1_, bf16[512,640]{1,0:T(8,128)(2,1)S(1)} %collective-permute-done.1.refs_2_, ...), custom_call_target="tpu_custom_call" | custom-call | tf_op jit(solution)/shard_map/partial_products/pallas_call | solution.py:123
  36.8 0.0 copy-start
  36.8 0.0 copy-start.1
  36.9 21.2 %all_to_all.30.parts_ref = f32[4,128,640]{2,1,0:T(8,128)S(1)} all-to-all(f32[4,128,640]{2,1,0:T(8,128)S(1)} %partial_products.1), channel_id=1, replica_groups=mesh['z1'=4,'z0'=4,'yh'=2,'x'=4,'yl'=2,'core'=2] {'x'}, dimensions={0} | all-to-all | bytes 2621440 | tf_op jit(solution)/shard_map/all_to_all | solution.py:25
  58.1 0.0 copy-done
  58.1 0.0 copy-done.1
  58.1 0.4 residual_and_grad_u.1
  58.5 10.1 %all_to_all.31.arrived_ref = f32[4,256,128]{2,1,0:T(8,128)S(1)} all-to-all(f32[4,256,128]{2,1,0:T(8,128)S(1)} %residual_and_grad_u.1), channel_id=1, replica_groups=mesh['z1'=4,'z0'=4,'yh'=2,'x'=4,'yl'=2,'core'=2] {'x'}, dimensions={0} | all-to-all | bytes 1048576 | tf_op jit(solution)/shard_map/all_to_all | solution.py:25
  68.5 0.8 grads_packed.1
  69.4 30.1 %all_to_all.32.arrived_ref = bf16[32,80,128]{2,1,0:T(8,128)(2,1)S(1)} all-to-all(bf16[32,80,128]{2,1,0:T(8,128)(2,1)S(1)} %grads_packed.1), channel_id=1, replica_groups=mesh['z1'=4,'z0'=4,'yh'=2,'x'=4,'yl'=2,'core'=2] {'yl','core','yh','z0'}, dimensions={0} | all-to-all | bytes 1310720 | tf_op jit(solution)/shard_map/all_to_all | solution.py:25
  99.5 0.1 close_sum.1
  99.6 26.8 %all_to_all.33.arrived_ref = bf16[8,80,128]{2,1,0:T(8,128)(2,1)S(1)} all-to-all(bf16[8,80,128]{2,1,0:T(8,128)(2,1)S(1)} %close_sum.1), channel_id=1, replica_groups=mesh['z1'=4,'z0'=4,'yh'=2,'x'=4,'yl'=2,'core'=2] {'z1','yh'}, dimensions={0} | all-to-all | bytes 327680 | tf_op jit(solution)/shard_map/all_to_all | solution.py:25
  126.4 0.7 far_sum.1
  127.1 6.6 %all-to-all-start.5 = ((f32[16,32,128]{2,1,0:T(8,128)}), f32[16,32,128]{2,1,0:T(8,128)S(1)}, u32[]{:S(2)}, u32[]{:S(2)}) async-start(f32[16,32,128]{2,1,0:T(8,128)} %get-tuple-element.5), calls=%async_computation.5 | async-start | bytes 524288 | tf_op jit(solution)/shard_map/all_to_all | solution.py:25
  133.7 3.5 %collective-permute-start.3 = (f32[128,128]{1,0:T(8,128)S(1)}, f32[128,128]{1,0:T(8,128)S(1)}, u32[]{:S(2)}, u32[]{:S(2)}) collective-permute-start(f32[128,128]{1,0:T(8,128)S(1)} %get-tuple-element.4.refs_0_), channel_id=1, source_target_pairs={{0,32},{32,64},{64,96},{96,0},{1,33},{33,65},{65,97},{97,1},{2,34}... | collective-permute-start | bytes 196616 | tf_op jit(solution)/shard_map/ppermute | solution.py:190
  137.3 2.0 %collective-permute-start.4 = (f32[128,128]{1,0:T(8,128)S(1)}, f32[128,128]{1,0:T(8,128)S(1)}, u32[]{:S(2)}, u32[]{:S(2)}) collective-permute-start(f32[128,128]{1,0:T(8,128)S(1)} %get-tuple-element.4.refs_0_), channel_id=1, source_target_pairs={{0,64},{32,96},{64,0},{96,32},{1,65},{33,97},{65,1},{97,33},{2,66}... | collective-permute-start | bytes 196616 | tf_op jit(solution)/shard_map/ppermute | solution.py:190
  139.2 4.3 %collective-permute-start.5 = (f32[128,128]{1,0:T(8,128)S(1)}, f32[128,128]{1,0:T(8,128)S(1)}, u32[]{:S(2)}, u32[]{:S(2)}) collective-permute-start(f32[128,128]{1,0:T(8,128)S(1)} %get-tuple-element.4.refs_0_), channel_id=1, source_target_pairs={{0,96},{32,0},{64,32},{96,64},{1,97},{33,1},{65,33},{97,65},{2,98}... | collective-permute-start | bytes 196616 | tf_op jit(solution)/shard_map/ppermute | solution.py:190
  143.5 0.0 collective-permute-done.3.refs_1_
  143.5 1.8 %collective-permute-done.4.refs_2_ = f32[128,128]{1,0:T(8,128)S(1)} collective-permute-done((f32[128,128]{1,0:T(8,128)S(1)}, f32[128,128]{1,0:T(8,128)S(1)}, u32[]{:S(2)}, u32[]{:S(2)}) %collective-permute-start.4) | collective-permute-done | bytes 65568 | tf_op jit(solution)/shard_map/ppermute | solution.py:190
  145.3 1.1 collective-permute-done.5.refs_3_
  146.4 1.3 grad_v.1
  147.7 0.0 all-to-all-done.5
  147.7 0.7 copy.12
  (4 shorter events, 0.0 us)
Async XLA Ops:
  3.9 5.0 %copy-start.7 = (s32[128]{0:T(128)S(1)}, s32[128]{0:T(128)}, u32[]{:S(2)}) copy-start(s32[128]{0:T(128)} %param.15) | copy-start | bytes 1540
  3.9 5.0 %copy-start.5 = (s32[128]{0:T(128)S(1)}, s32[128]{0:T(128)}, u32[]{:S(2)}) copy-start(s32[128]{0:T(128)} %param.17) | copy-start | bytes 1540
  3.9 5.0 %copy-start.6 = (s32[128]{0:T(128)S(1)}, s32[128]{0:T(128)}, u32[]{:S(2)}) copy-start(s32[128]{0:T(128)} %param.16) | copy-start | bytes 1540
  3.9 5.1 %copy-start.3 = (f32[512,128]{1,0:T(8,128)S(1)}, f32[512,128]{1,0:T(8,128)}, u32[]{:S(2)}) copy-start(f32[512,128]{1,0:T(8,128)} %param.13) | copy-start | bytes 786436
  3.9 5.1 %copy-start.4 = (f32[512,128]{1,0:T(8,128)S(1)}, f32[512,128]{1,0:T(8,128)}, u32[]{:S(2)}) copy-start(f32[512,128]{1,0:T(8,128)} %param.12) | copy-start | bytes 786436
  3.9 7.0 %copy-start.2 = (bf16[512,512]{1,0:T(8,128)(2,1)S(1)}, bf16[512,512]{1,0:T(8,128)(2,1)}, u32[]{:S(2)}) copy-start(bf16[512,512]{1,0:T(8,128)(2,1)} %param.11) | copy-start | bytes 1572868
  3.9 29.8 %all-to-all-start = ((bf16[4,128,2048]{2,1,0:T(8,128)(2,1)}), bf16[4,128,2048]{2,1,0:T(8,128)(2,1)S(1)}, u32[]{:S(2)}, u32[]{:S(2)}) async-start(bf16[4,128,2048]{2,1,0:T(8,128)(2,1)} %pad_maximum_fusion), calls=%async_computation | async-start | bytes 4194304 | tf_op jit(solution)/shard_map/all_to_all | solution.py:25
  10.9 13.1 %collective-permute-start.1 = (bf16[512,640]{1,0:T(8,128)(2,1)S(1)}, bf16[512,640]{1,0:T(8,128)(2,1)S(1)}, u32[]{:S(2)}, u32[]{:S(2)}) collective-permute-start(bf16[512,640]{1,0:T(8,128)(2,1)S(1)} %pad_maximum_fusion.1.refs_0_), channel_id=1, source_target_pairs={{0,2},{2,0},{1,3},{3,1},{4,6},{6,4},{5,7},{7,5},{8,10},{10,8},{9,1... | collective-permute-start | bytes 1966088 | tf_op jit(solution)/shard_map/ppermute | solution.py:143
  14.1 17.8 %collective-permute-start = (bf16[512,640]{1,0:T(8,128)(2,1)S(1)}, bf16[512,640]{1,0:T(8,128)(2,1)}, u32[]{:S(2)}, u32[]{:S(2)}) collective-permute-start(bf16[512,640]{1,0:T(8,128)(2,1)S(1)} %pad_maximum_fusion.1.refs_0_), channel_id=1, source_target_pairs={{0,1},{1,0},{2,3},{3,2},{4,5},{5,4},{6,7},{7,6},{8,9},{9,8},{10,11... | collective-permute-start | bytes 1966088 | tf_op jit(solution)/shard_map/ppermute | solution.py:144
  24.0 9.7 %collective-permute-start.2 = (bf16[512,640]{1,0:T(8,128)(2,1)S(1)}, bf16[512,640]{1,0:T(8,128)(2,1)}, u32[]{:S(2)}, u32[]{:S(2)}) collective-permute-start(bf16[512,640]{1,0:T(8,128)(2,1)S(1)} %collective-permute-done.1.refs_2_), channel_id=1, source_target_pairs={{0,1},{1,0},{2,3},{3,2},{4,5},{5,4},{6,7},{7,6},{8,9},{9,8},{10,11... | collective-permute-start | bytes 1966088 | tf_op jit(solution)/shard_map/ppermute | solution.py:144
  36.8 21.2 %copy-start = (bf16[128,512]{1,0:T(8,128)(2,1)S(1)}, bf16[128,512]{1,0:T(8,128)(2,1)}, u32[]{:S(2)}) copy-start(bf16[128,512]{1,0:T(8,128)(2,1)} %target_ref.1) | copy-start | bytes 393220
  36.8 21.2 %copy-start.1 = (f32[128]{0:T(128)S(1)}, f32[128]{0:T(128)}, u32[]{:S(2)}) copy-start(f32[128]{0:T(128)} %param.14) | copy-start | bytes 1540
  127.1 20.5 %all-to-all-start.5 = ((f32[16,32,128]{2,1,0:T(8,128)}), f32[16,32,128]{2,1,0:T(8,128)S(1)}, u32[]{:S(2)}, u32[]{:S(2)}) async-start(f32[16,32,128]{2,1,0:T(8,128)} %get-tuple-element.5), calls=%async_computation.5 | async-start | bytes 524288 | tf_op jit(solution)/shard_map/all_to_all | solution.py:25
  133.7 9.8 %collective-permute-start.3 = (f32[128,128]{1,0:T(8,128)S(1)}, f32[128,128]{1,0:T(8,128)S(1)}, u32[]{:S(2)}, u32[]{:S(2)}) collective-permute-start(f32[128,128]{1,0:T(8,128)S(1)} %get-tuple-element.4.refs_0_), channel_id=1, source_target_pairs={{0,32},{32,64},{64,96},{96,0},{1,33},{33,65},{65,97},{97,1},{2,34}... | collective-permute-start | bytes 196616 | tf_op jit(solution)/shard_map/ppermute | solution.py:190
  137.3 8.0 %collective-permute-start.4 = (f32[128,128]{1,0:T(8,128)S(1)}, f32[128,128]{1,0:T(8,128)S(1)}, u32[]{:S(2)}, u32[]{:S(2)}) collective-permute-start(f32[128,128]{1,0:T(8,128)S(1)} %get-tuple-element.4.refs_0_), channel_id=1, source_target_pairs={{0,64},{32,96},{64,0},{96,32},{1,65},{33,97},{65,1},{97,33},{2,66}... | collective-permute-start | bytes 196616 | tf_op jit(solution)/shard_map/ppermute | solution.py:190
  139.2 7.2 %collective-permute-start.5 = (f32[128,128]{1,0:T(8,128)S(1)}, f32[128,128]{1,0:T(8,128)S(1)}, u32[]{:S(2)}, u32[]{:S(2)}) collective-permute-start(f32[128,128]{1,0:T(8,128)S(1)} %get-tuple-element.4.refs_0_), channel_id=1, source_target_pairs={{0,96},{32,0},{64,32},{96,64},{1,97},{33,1},{65,33},{97,65},{2,98}... | collective-permute-start | bytes 196616 | tf_op jit(solution)/shard_map/ppermute | solution.py:190

commit v6 on v5

--- a/solution.py
+++ b/solution.py
@@ -19,6 +19,10 @@
     ratio = factor / step
     smooth = ratio - jnp.sin(2.0 * math.pi * ratio) / (2.0 * math.pi)
     return step * jnp.clip(smooth, -upper, upper - 1.0)
+
+
+def flips(n, step):
+    return [(j, j ^ step) for j in range(n)]
 
 
 def exchange(parts, axes):
@@ -110,13 +114,13 @@
 
 def place_kernel(order_ref, *refs):
     *piece_refs, out_ref = refs
-    n_yh = 2
-    rows = piece_refs[0].shape[0] // n_yh
+    n_yh, n_z0 = 2, order_ref.shape[0]
     half = out_ref.shape[0] // n_yh
-    for k, piece in enumerate(piece_refs):
-        for h in range(n_yh):
-            start = pl.multiple_of(h * half + order_ref[k] * rows, rows)
-            out_ref[pl.ds(start, rows)] = piece[h * rows : (h + 1) * rows]
+    rows = half // n_z0
+    pieces = [p[i : i + rows] for p in piece_refs for i in range(0, p.shape[0], rows)]
+    for i, piece in enumerate(pieces):
+        start = pl.multiple_of(i % n_yh * half + order_ref[i // n_yh] * rows, rows)
+        out_ref[pl.ds(start, rows)] = piece
 
 
 def kernel_call(kernel, out, name, operands, scalars=0):
@@ -185,10 +189,9 @@
         (exchange(mine, FAR),),
     )
     grad_u = exchange(u_mine, FSDP).reshape(kvw, rank)
-    v_pieces = [v_mine]
-    for k in range(1, n_z0):
-        v_pieces.append(lax.ppermute(v_mine, "z0", [(j, (j + k) % n_z0) for j in range(n_z0)]))
-    order = jnp.remainder(lax.axis_index("z0") - jnp.arange(n_z0, dtype=jnp.int32), n_z0)
+    v_two = jnp.concatenate([v_mine, lax.ppermute(v_mine, "z0", flips(n_z0, 2))], axis=0)
+    v_pieces = [v_two, lax.ppermute(v_two, "z0", flips(n_z0, 1))]
+    order = jnp.bitwise_xor(lax.axis_index("z0"), jnp.array([0, 2, 1, 3], jnp.int32))
     grad_v = kernel_call(
         place_kernel, shape((rows, rank), f32), "grad_v", (order, *v_pieces), scalars=1
     )

time: 149 us -> 148 us (level)
  blocking collectives: 88.2 us -> 61.4 us
  waiting for transfers between devices: 8.31 us -> 24.5 us
  starting transfers between devices: 38.6 us -> 47.5 us
    all_to_all x4 -> x3, blocking collectives: 88.2 us -> 61.4 us  [exchange(): return lax.all_to_all(parts, axes, 0, 0, tiled=True)]
    all_to_all x2 -> x3, starting transfers between devices: 11.6 us -> 26.1 us  [exchange(): return lax.all_to_all(parts, axes, 0, 0, tiled=True)]
    all_to_all x2 -> x3, waiting for transfers between devices: 0.01 us -> 14.2 us  [exchange(): return lax.all_to_all(parts, axes, 0, 0, tiled=True)]
    ppermute x3 -> x2, starting transfers between devices: 9.74 us -> 4.03 us  [the longest x1 2.11 us: shards(): lax.ppermute(v_mine, 'z0', flips(n_z0, 2))]
    ppermute x3 -> x2, waiting for transfers between devices: 2.89 us -> 4.82 us  [the longest x1 4.82 us: shards(): v_pieces = [v_two, lax.ppermute(v_two, 'z0', flips(n_z0, 1))]]
where the time goes in v6:
time: 148 us; the launch traced here: 147 us
  blocking collectives  61.4 us (41%)
  starting transfers between devices  47.5 us (32%)
  waiting for transfers between devices  24.5 us (17%)
  Pallas kernels  7.08 us (5%)
  other arithmetic  3.56 us (2%)
  local copies, waits for them, and re-layouts  2.42 us (2%)
    all_to_all x3, blocking collectives, exchange(): return lax.all_to_all(parts, axes, 0, 0, tiled=True)  61.4 us
    all_to_all x3, starting transfers between devices, exchange(): return lax.all_to_all(parts, axes, 0, 0, tiled=True)  26.1 us
    all_to_all x3, waiting for transfers between devices, exchange(): return lax.all_to_all(parts, axes, 0, 0, tiled=True)  14.2 us
    ppermute x1, starting transfers between devices, shards(): lax.ppermute(across, 'core', swap)  7.83 us
    pallas_call x6, Pallas kernels, kernel_call(): pl.pallas_call(kernel, out_shape=out, in_specs=[IN_SMEM] * scalars + [IN_...  7.08 us
    ppermute x1, starting transfers between devices, shards(): lax.ppermute(own, 'core', swap)  6.29 us
    ppermute x1, waiting for transfers between devices, shards(): v_pieces = [v_two, lax.ppermute(v_two, 'z0', flips(n_z0, 1))]  4.82 us
    ppermute x1, waiting for transfers between devices, shards(): across = lax.ppermute(own, 'yl', swap)  3.6 us
  transfers between devices with their start and end apart: 8, of which 4 were waited for; matrix products, arithmetic and copies ran while one was open for 1% of the time, Pallas kernels for 1%

profile of v6, /device:TPU:1, one launch (start us, length us, event | category | flops | bytes accessed | tf_op | source)
XLA Modules:
  0.0 147.2 jit_solution(11686249881297413015)
XLA Ops:
  0.6 1.7 %slice_bitcast_fusion.3 = (bf16[1,128,2048]{2,1,0:T(8,128)(2,1)S(1)}, bf16[1,128,2048]{2,1,0:T(8,128)(2,1)S(1)}, bf16[1,128,2048]{2,1,0:T(8,128)(2,1)S(1)}, bf16[1,128,2048]{2,1,0:T(8,128)(2,1)S(1)}) fusion(bf16[128,8192]{1,0:T(8,128)(2,1)} %param.10), kind=kLoop, calls=%fused_computation.5 | loop fusion | bytes 4194304 | tf_op jit(solution)/shard_map/stack | solution.py:150
  2.3 1.6 %pad_maximum_fusion = bf16[4,128,2048]{2,1,0:T(8,128)(2,1)} fusion(bf16[1,128,2048]{2,1,0:T(8,128)(2,1)S(1)} %get-tuple-element.8, bf16[1,128,2048]{2,1,0:T(8,128)(2,1)S(1)} %get-tuple-element.9, bf16[1,128,2048]{2,1,0:T(8,128)(2,1)S(1)} %get-tuple-element.7, bf16[1,128,2048]{2,1,0:T(8,128)(2,1)S(1)} %get-tuple-element.6), kind=kLoop, calls=%fused_computation | loop fusion | flops 3145728 | bytes 4194304 | tf_op jit(solution)/shard_map/stack | solution.py:150
  3.9 0.0 copy-start.7
  3.9 0.0 copy-start.5
  3.9 0.0 copy-start.6
  3.9 0.0 copy-start.3
  3.9 0.0 copy-start.4
  3.9 0.0 copy-start.2
  3.9 5.0 %all-to-all-start = ((bf16[4,128,2048]{2,1,0:T(8,128)(2,1)}), bf16[4,128,2048]{2,1,0:T(8,128)(2,1)S(1)}, u32[]{:S(2)}, u32[]{:S(2)}) async-start(bf16[4,128,2048]{2,1,0:T(8,128)(2,1)} %pad_maximum_fusion), calls=%async_computation | async-start | bytes 4194304 | tf_op jit(solution)/shard_map/all_to_all | solution.py:29
  8.9 0.0 copy-done.7
  8.9 0.0 copy-done.5
  8.9 0.0 copy-done.6
  9.0 0.0 copy-done.3
  9.0 0.0 copy-done.4
  9.0 1.9 %multiply_convert_fusion = (bf16[512,128]{1,0:T(8,128)(2,1)S(1)}, bf16[512,128]{1,0:T(8,128)(2,1)S(1)}) fusion(f32[512,128]{1,0:T(8,128)S(1)} %copy-done.3, f32[128]{0:T(128)S(1)} %get-tuple-element.14, f32[128]{0:T(128)S(1)} %get-tuple-element.13, f32[128]{0:T(128)S(1)} %get-tuple-element.12, f32[512,128]{1,0:T(8,128)S(1)} %copy-done.4, ...), kind=kLoop, calls=%fused_computation.6 | loop fusion | flops 1048576 | bytes 788480 | tf_op jit(solution)/shard_map/convert_element_type | solution.py:152
  10.9 0.0 copy-done.2
  10.9 0.1 pad_maximum_fusion.1.refs_0_
  10.9 3.2 %collective-permute-start.1 = (bf16[512,640]{1,0:T(8,128)(2,1)S(1)}, bf16[512,640]{1,0:T(8,128)(2,1)S(1)}, u32[]{:S(2)}, u32[]{:S(2)}) collective-permute-start(bf16[512,640]{1,0:T(8,128)(2,1)S(1)} %pad_maximum_fusion.1.refs_0_), channel_id=1, source_target_pairs={{0,2},{2,0},{1,3},{3,1},{4,6},{6,4},{5,7},{7,5},{8,10},{10,8},{9,1... | collective-permute-start | bytes 1966088 | tf_op jit(solution)/shard_map/ppermute | solution.py:147
  14.2 6.3 %collective-permute-start = (bf16[512,640]{1,0:T(8,128)(2,1)S(1)}, bf16[512,640]{1,0:T(8,128)(2,1)}, u32[]{:S(2)}, u32[]{:S(2)}) collective-permute-start(bf16[512,640]{1,0:T(8,128)(2,1)S(1)} %pad_maximum_fusion.1.refs_0_), channel_id=1, source_target_pairs={{0,1},{1,0},{2,3},{3,2},{4,5},{5,4},{6,7},{7,6},{8,9},{9,8},{10,11... | collective-permute-start | bytes 1966088 | tf_op jit(solution)/shard_map/ppermute | solution.py:148
  20.5 3.6 %collective-permute-done.1.refs_2_ = bf16[512,640]{1,0:T(8,128)(2,1)S(1)} collective-permute-done((bf16[512,640]{1,0:T(8,128)(2,1)S(1)}, bf16[512,640]{1,0:T(8,128)(2,1)S(1)}, u32[]{:S(2)}, u32[]{:S(2)}) %collective-permute-start.1) | collective-permute-done | bytes 655392 | tf_op jit(solution)/shard_map/ppermute | solution.py:147
  24.1 7.8 %collective-permute-start.2 = (bf16[512,640]{1,0:T(8,128)(2,1)S(1)}, bf16[512,640]{1,0:T(8,128)(2,1)}, u32[]{:S(2)}, u32[]{:S(2)}) collective-permute-start(bf16[512,640]{1,0:T(8,128)(2,1)S(1)} %collective-permute-done.1.refs_2_), channel_id=1, source_target_pairs={{0,1},{1,0},{2,3},{3,2},{4,5},{5,4},{6,7},{7,6},{8,9},{9,8},{10,11... | collective-permute-start | bytes 1966088 | tf_op jit(solution)/shard_map/ppermute | solution.py:148
  31.9 0.0 collective-permute-done.refs_1_
  31.9 1.8 %collective-permute-done.2.refs_3_ = bf16[512,640]{1,0:T(8,128)(2,1)} collective-permute-done((bf16[512,640]{1,0:T(8,128)(2,1)S(1)}, bf16[512,640]{1,0:T(8,128)(2,1)}, u32[]{:S(2)}, u32[]{:S(2)}) %collective-permute-start.2) | collective-permute-done | bytes 655392 | tf_op jit(solution)/shard_map/ppermute | solution.py:148
  33.7 0.0 all-to-all-done
  33.7 3.1 %partial_products.1 = f32[4,128,640]{2,1,0:T(8,128)S(1)} custom-call(s32[4]{0:T(128)S(1)} %iota_xor_fusion.order_ref, bf16[512,2048]{1,0:T(8,128)(2,1)S(1)} %bitcast.11, bf16[512,640]{1,0:T(8,128)(2,1)S(1)} %pad_maximum_fusion.1.refs_0_, bf16[512,640]{1,0:T(8,128)(2,1)} %collective-permute-done.refs_1_, bf16[512,640]{1,0:T(8,128)(2,1)S(1)} %collective-permute-done.1.refs_2_, ...), custom_call_target="tpu_custom_call" | custom-call | tf_op jit(solution)/shard_map/partial_products/pallas_call | solution.py:127
  36.8 0.0 copy-start
  36.9 0.0 copy-start.1
  36.9 21.2 %all_to_all.30.parts_ref = f32[4,128,640]{2,1,0:T(8,128)S(1)} all-to-all(f32[4,128,640]{2,1,0:T(8,128)S(1)} %partial_products.1), channel_id=1, replica_groups=mesh['z1'=4,'z0'=4,'yh'=2,'x'=4,'yl'=2,'core'=2] {'x'}, dimensions={0} | all-to-all | bytes 2621440 | tf_op jit(solution)/shard_map/all_to_all | solution.py:29
  58.1 0.0 copy-done
  58.1 0.0 copy-done.1
  58.1 0.4 residual_and_grad_u.1
  58.5 10.1 %all_to_all.31.arrived_ref = f32[4,256,128]{2,1,0:T(8,128)S(1)} all-to-all(f32[4,256,128]{2,1,0:T(8,128)S(1)} %residual_and_grad_u.1), channel_id=1, replica_groups=mesh['z1'=4,'z0'=4,'yh'=2,'x'=4,'yl'=2,'core'=2] {'x'}, dimensions={0} | all-to-all | bytes 1048576 | tf_op jit(solution)/shard_map/all_to_all | solution.py:29
  68.6 0.8 grads_packed.1
  69.4 0.0 copy-start.8
  69.4 30.1 %all_to_all.32.arrived_ref = bf16[32,80,128]{2,1,0:T(8,128)(2,1)S(1)} all-to-all(bf16[32,80,128]{2,1,0:T(8,128)(2,1)S(1)} %grads_packed.1), channel_id=1, replica_groups=mesh['z1'=4,'z0'=4,'yh'=2,'x'=4,'yl'=2,'core'=2] {'yl','core','yh','z0'}, dimensions={0} | all-to-all | bytes 1310720 | tf_op jit(solution)/shard_map/all_to_all | solution.py:29
  99.5 0.8 close_sum.1
  100.3 12.8 %all-to-all-start.4 = ((bf16[8,80,128]{2,1,0:T(8,128)(2,1)}), bf16[8,80,128]{2,1,0:T(8,128)(2,1)S(1)}, u32[]{:S(2)}, u32[]{:S(2)}) async-start(bf16[8,80,128]{2,1,0:T(8,128)(2,1)} %close_sum.1), calls=%async_computation.4 | async-start | bytes 327680 | tf_op jit(solution)/shard_map/all_to_all | solution.py:29
  113.1 14.2 %all-to-all-done.4.arrived_ref = bf16[8,80,128]{2,1,0:T(8,128)(2,1)S(1)} async-done(((bf16[8,80,128]{2,1,0:T(8,128)(2,1)}), bf16[8,80,128]{2,1,0:T(8,128)(2,1)S(1)}, u32[]{:S(2)}, u32[]{:S(2)}) %all-to-all-start.4) | async-done | bytes 163872 | tf_op jit(solution)/shard_map/all_to_all | solution.py:29
  127.3 0.7 far_sum.1
  128.0 2.1 %collective-permute-start.3 = (f32[128,128]{1,0:T(8,128)S(1)}, f32[128,128]{1,0:T(8,128)S(1)}, u32[]{:S(2)}, u32[]{:S(2)}) collective-permute-start(f32[128,128]{1,0:T(8,128)S(1)} %get-tuple-element.4), channel_id=1, source_target_pairs={{0,64},{32,96},{64,0},{96,32},{1,65},{33,97},{65,1},{97,33},{2,66}... | collective-permute-start | bytes 196616 | tf_op jit(solution)/shard_map/ppermute | solution.py:192
  130.2 8.3 %all-to-all-start.5 = ((f32[16,32,128]{2,1,0:T(8,128)}), f32[16,32,128]{2,1,0:T(8,128)S(1)}, u32[]{:S(2)}, u32[]{:S(2)}) async-start(f32[16,32,128]{2,1,0:T(8,128)} %get-tuple-element.5), calls=%async_computation.5 | async-start | bytes 524288 | tf_op jit(solution)/shard_map/all_to_all | solution.py:29
  138.5 0.0 collective-permute-done.3
  138.5 1.9 %collective-permute-start.4 = (f32[256,128]{1,0:T(8,128)S(1)}, f32[256,128]{1,0:T(8,128)S(1)}, u32[]{:S(2)}, u32[]{:S(2)}) collective-permute-start(f32[256,128]{1,0:T(8,128)S(1)} %constant_dynamic-update-slice_fusion.refs_0_), channel_id=1, source_target_pairs={{0,32},{32,0},{64,96},{96,64},{1,33},{33,1},{65,97},{97,65},{2,34}... | collective-permute-start | bytes 393224 | tf_op jit(solution)/shard_map/ppermute | solution.py:193
  140.4 0.0 copy-done.8
  140.5 4.8 %collective-permute-done.4.refs_1_ = f32[256,128]{1,0:T(8,128)S(1)} collective-permute-done((f32[256,128]{1,0:T(8,128)S(1)}, f32[256,128]{1,0:T(8,128)S(1)}, u32[]{:S(2)}, u32[]{:S(2)}) %collective-permute-start.4) | collective-permute-done | bytes 131104 | tf_op jit(solution)/shard_map/ppermute | solution.py:193
  145.3 1.3 grad_v.1
  146.5 0.0 all-to-all-done.5
  146.5 0.7 copy.14
  (6 shorter events, 0.0 us)
Async XLA Ops:
  3.9 5.0 %copy-start.7 = (s32[128]{0:T(128)S(1)}, s32[128]{0:T(128)}, u32[]{:S(2)}) copy-start(s32[128]{0:T(128)} %param.16) | copy-start | bytes 1540
  3.9 5.0 %copy-start.5 = (s32[128]{0:T(128)S(1)}, s32[128]{0:T(128)}, u32[]{:S(2)}) copy-start(s32[128]{0:T(128)} %param.18) | copy-start | bytes 1540
  3.9 5.0 %copy-start.6 = (s32[128]{0:T(128)S(1)}, s32[128]{0:T(128)}, u32[]{:S(2)}) copy-start(s32[128]{0:T(128)} %param.17) | copy-start | bytes 1540
  3.9 5.1 %copy-start.3 = (f32[512,128]{1,0:T(8,128)S(1)}, f32[512,128]{1,0:T(8,128)}, u32[]{:S(2)}) copy-start(f32[512,128]{1,0:T(8,128)} %param.14) | copy-start | bytes 786436
  3.9 5.1 %copy-start.4 = (f32[512,128]{1,0:T(8,128)S(1)}, f32[512,128]{1,0:T(8,128)}, u32[]{:S(2)}) copy-start(f32[512,128]{1,0:T(8,128)} %param.13) | copy-start | bytes 786436
  3.9 7.0 %copy-start.2 = (bf16[512,512]{1,0:T(8,128)(2,1)S(1)}, bf16[512,512]{1,0:T(8,128)(2,1)}, u32[]{:S(2)}) copy-start(bf16[512,512]{1,0:T(8,128)(2,1)} %param.12) | copy-start | bytes 1572868
  3.9 29.8 %all-to-all-start = ((bf16[4,128,2048]{2,1,0:T(8,128)(2,1)}), bf16[4,128,2048]{2,1,0:T(8,128)(2,1)S(1)}, u32[]{:S(2)}, u32[]{:S(2)}) async-start(bf16[4,128,2048]{2,1,0:T(8,128)(2,1)} %pad_maximum_fusion), calls=%async_computation | async-start | bytes 4194304 | tf_op jit(solution)/shard_map/all_to_all | solution.py:29
  10.9 13.1 %collective-permute-start.1 = (bf16[512,640]{1,0:T(8,128)(2,1)S(1)}, bf16[512,640]{1,0:T(8,128)(2,1)S(1)}, u32[]{:S(2)}, u32[]{:S(2)}) collective-permute-start(bf16[512,640]{1,0:T(8,128)(2,1)S(1)} %pad_maximum_fusion.1.refs_0_), channel_id=1, source_target_pairs={{0,2},{2,0},{1,3},{3,1},{4,6},{6,4},{5,7},{7,5},{8,10},{10,8},{9,1... | collective-permute-start | bytes 1966088 | tf_op jit(solution)/shard_map/ppermute | solution.py:147
  14.2 17.8 %collective-permute-start = (bf16[512,640]{1,0:T(8,128)(2,1)S(1)}, bf16[512,640]{1,0:T(8,128)(2,1)}, u32[]{:S(2)}, u32[]{:S(2)}) collective-permute-start(bf16[512,640]{1,0:T(8,128)(2,1)S(1)} %pad_maximum_fusion.1.refs_0_), channel_id=1, source_target_pairs={{0,1},{1,0},{2,3},{3,2},{4,5},{5,4},{6,7},{7,6},{8,9},{9,8},{10,11... | collective-permute-start | bytes 1966088 | tf_op jit(solution)/shard_map/ppermute | solution.py:148
  24.1 9.7 %collective-permute-start.2 = (bf16[512,640]{1,0:T(8,128)(2,1)S(1)}, bf16[512,640]{1,0:T(8,128)(2,1)}, u32[]{:S(2)}, u32[]{:S(2)}) collective-permute-start(bf16[512,640]{1,0:T(8,128)(2,1)S(1)} %collective-permute-done.1.refs_2_), channel_id=1, source_target_pairs={{0,1},{1,0},{2,3},{3,2},{4,5},{5,4},{6,7},{7,6},{8,9},{9,8},{10,11... | collective-permute-start | bytes 1966088 | tf_op jit(solution)/shard_map/ppermute | solution.py:148
  36.8 21.2 %copy-start = (bf16[128,512]{1,0:T(8,128)(2,1)S(1)}, bf16[128,512]{1,0:T(8,128)(2,1)}, u32[]{:S(2)}) copy-start(bf16[128,512]{1,0:T(8,128)(2,1)} %target_ref.1) | copy-start | bytes 393220
  36.9 21.2 %copy-start.1 = (f32[128]{0:T(128)S(1)}, f32[128]{0:T(128)}, u32[]{:S(2)}) copy-start(f32[128]{0:T(128)} %param.15) | copy-start | bytes 1540
  69.4 71.1 %copy-start.8 = (s32[4]{0:T(128)S(1)}, s32[4]{0:T(128)}, u32[]{:S(2)}) copy-start(s32[4]{0:T(128)} %constant.27.clone) | copy-start | bytes 52
  100.3 27.0 %all-to-all-start.4 = ((bf16[8,80,128]{2,1,0:T(8,128)(2,1)}), bf16[8,80,128]{2,1,0:T(8,128)(2,1)S(1)}, u32[]{:S(2)}, u32[]{:S(2)}) async-start(bf16[8,80,128]{2,1,0:T(8,128)(2,1)} %close_sum.1), calls=%async_computation.4 | async-start | bytes 327680 | tf_op jit(solution)/shard_map/all_to_all | solution.py:29
  128.0 10.5 %collective-permute-start.3 = (f32[128,128]{1,0:T(8,128)S(1)}, f32[128,128]{1,0:T(8,128)S(1)}, u32[]{:S(2)}, u32[]{:S(2)}) collective-permute-start(f32[128,128]{1,0:T(8,128)S(1)} %get-tuple-element.4), channel_id=1, source_target_pairs={{0,64},{32,96},{64,0},{96,32},{1,65},{33,97},{65,1},{97,33},{2,66}... | collective-permute-start | bytes 196616 | tf_op jit(solution)/shard_map/ppermute | solution.py:192
  130.2 16.4 %all-to-all-start.5 = ((f32[16,32,128]{2,1,0:T(8,128)}), f32[16,32,128]{2,1,0:T(8,128)S(1)}, u32[]{:S(2)}, u32[]{:S(2)}) async-start(f32[16,32,128]{2,1,0:T(8,128)} %get-tuple-element.5), calls=%async_computation.5 | async-start | bytes 524288 | tf_op jit(solution)/shard_map/all_to_all | solution.py:29
  138.5 6.8 %collective-permute-start.4 = (f32[256,128]{1,0:T(8,128)S(1)}, f32[256,128]{1,0:T(8,128)S(1)}, u32[]{:S(2)}, u32[]{:S(2)}) collective-permute-start(f32[256,128]{1,0:T(8,128)S(1)} %constant_dynamic-update-slice_fusion.refs_0_), channel_id=1, source_target_pairs={{0,32},{32,0},{64,96},{96,64},{1,33},{33,1},{65,97},{97,65},{2,34}... | collective-permute-start | bytes 393224 | tf_op jit(solution)/shard_map/ppermute | solution.py:193

commit v7 on v6

--- a/solution.py
+++ b/solution.py
@@ -10,7 +10,8 @@
 
 AXES = {"z1": 4, "z0": 4, "yh": 2, "x": 4, "yl": 2, "core": 2}
 DP, FSDP, NEAR = ("z1", "z0", "yh"), ("x", "yl", "core"), ("yl", "core")
-CLOSE, FAR = (*NEAR, "yh", "z0"), ("z1", "yh")
+CLOSE, FAR = ("yl", "yh", "z0"), ("z1", "yh")
+SPLIT = ("x", "core", "yl")
 
 
 def fake_quantize(factor, bits, scale_exps):
@@ -62,33 +63,47 @@
     scaled = (out[:, kvw:] * sigma).astype(jnp.bfloat16)
     residual = out[:, :kvw] + dot32(scaled, u_quant, ((1,), (1,))) - target_ref[...].astype(jnp.float32)
     out_grad = (residual * scale).astype(jnp.bfloat16)
-    rank_grad = (dot32(out_grad, u_quant) * sigma).astype(jnp.bfloat16).astype(jnp.float32)
-    each = kvw // n_x
-    for i in range(n_x):
+    rank_grad = (dot32(out_grad, u_quant) * sigma).astype(jnp.bfloat16)
+    grad_u = dot32(out_grad, scaled, ((0,), (0,)))
+    high = grad_u.astype(jnp.bfloat16)
+    low = (grad_u - high.astype(jnp.float32)).astype(jnp.bfloat16)
+    n_to = out_ref.shape[0]
+    each = kvw // n_to
+    for i in range(n_to):
         out_ref[i, :tok] = rank_grad
-        out_ref[i, tok:] = dot32(out_grad[:, i * each : (i + 1) * each], scaled, ((0,), (0,)))
-
-
-def grads_kernel(tokens_ref, arrived_ref, out_ref):
-    n_x, _, rank = arrived_ref.shape
+        out_ref[i, tok : tok + each] = high[i * each : (i + 1) * each]
+        out_ref[i, tok + each :] = low[i * each : (i + 1) * each]
+
+
+def grads_kernel(core_ref, tokens_ref, others_ref, arrived_ref, out_ref):
+    core = core_ref[0]
+    n_from, both, rank = arrived_ref.shape
     n_to, packed, _ = out_ref.shape
+    n_x, n_yl = n_from // 2, 2
+    rows = others_ref.shape[1] // n_yl
     tok = tokens_ref.shape[0] // n_x
-    v_rows = tokens_ref.shape[1] // n_to
+    each = (both - tok) // 2
+    per_yl = n_to // n_yl
+    v_rows = rows // per_yl
     u_rows = packed - v_rows
-    rank_all = jnp.concatenate([arrived_ref[i, :tok] for i in range(n_x)], axis=0)
-    rank_all = rank_all.astype(jnp.bfloat16)
-    u_sum = arrived_ref[0, tok:]
-    for i in range(1, n_x):
-        u_sum = u_sum + arrived_ref[i, tok:]
+    mine = jnp.concatenate([arrived_ref[2 * x + core, :tok] for x in range(n_x)], axis=0)
+    other = jnp.concatenate([arrived_ref[2 * x + 1 - core, :tok] for x in range(n_x)], axis=0)
+    u_sum = jnp.zeros((each, rank), jnp.float32)
+    for i in range(n_from):
+        u_sum = u_sum + arrived_ref[i, tok : tok + each].astype(jnp.float32)
+        u_sum = u_sum + arrived_ref[i, tok + each :].astype(jnp.float32)
     u_sum = u_sum.astype(jnp.bfloat16)
-    repeat = n_to * u_rows // u_sum.shape[0]
-    wide = repeat * v_rows
-    for j in range(n_to // repeat):
-        v_part = dot32(tokens_ref[:, j * wide : (j + 1) * wide], rank_all, ((0,), (0,)))
+    repeat = n_to * u_rows // each
+    for j in range(n_yl):
+        start = pl.multiple_of((2 * j + core) * rows, rows)
+        v_part = dot32(tokens_ref[:, pl.ds(start, rows)], mine, ((0,), (0,)))
+        v_part = v_part + dot32(others_ref[:, j * rows : (j + 1) * rows], other, ((0,), (0,)))
         v_part = v_part.astype(jnp.bfloat16)
-        for i in range(repeat):
-            out_ref[j * repeat + i, :v_rows] = v_part[i * v_rows : (i + 1) * v_rows]
-            out_ref[j * repeat + i, v_rows:] = u_sum[j * u_rows : (j + 1) * u_rows]
+        for r in range(per_yl):
+            i = j * per_yl + r
+            u_at = i // repeat * u_rows
+            out_ref[i, :v_rows] = v_part[r * v_rows : (r + 1) * v_rows]
+            out_ref[i, v_rows:] = u_sum[u_at : u_at + u_rows]
 
 
 def close_sum_kernel(arrived_ref, out_ref):
@@ -161,20 +176,27 @@
         (order, tokens, *pieces),
         scalars=1,
     )
+    core = lax.axis_index("core")
+    others = [
+        lax.dynamic_slice_in_dim(tokens, (2 * i + 1 - core) * rows, rows, 1)
+        for i in range(n_near // 2)
+    ]
+    others = lax.ppermute(jnp.concatenate(others, axis=1), "core", swap)
     scale = 1.0 / math.sqrt(tok * math.prod(lax.axis_size(a) for a in AXES))
     ranks = kernel_call(
         functools.partial(middle_kernel, scale),
-        shape((n_x, tok + kvw // n_x, rank), f32),
+        shape((2 * n_x, tok + kvw // n_x, rank), bf16),
         "residual_and_grad_u",
         (exchange(part, "x"), target, u_quant, sigma.reshape(1, rank)),
     )
     n_close, n_far = lax.axis_size(CLOSE), lax.axis_size(FAR)
-    v_rows, u_rows = wide // n_close, kvw * n_z0 // (n_x * n_close)
+    v_rows, u_rows = wide // (2 * n_close), kvw * n_z0 // (2 * n_x * n_close)
     parts = kernel_call(
         grads_kernel,
         shape((n_close, v_rows + u_rows, rank), bf16),
         "grads_packed",
-        (tokens, exchange(ranks, "x")),
+        (core.reshape(1), tokens, others, exchange(ranks, ("x", "core"))),
+        scalars=1,
     )
     mine = kernel_call(
         close_sum_kernel,
@@ -184,11 +206,11 @@
     )
     v_mine, u_mine = kernel_call(
         far_sum_kernel,
-        (shape((2 * v_rows, rank), f32), shape((lax.axis_size(FSDP), 2 * u_rows, rank), f32)),
+        (shape((2 * v_rows, rank), f32), shape((lax.axis_size(SPLIT), 2 * u_rows, rank), f32)),
         "far_sum",
         (exchange(mine, FAR),),
     )
-    grad_u = exchange(u_mine, FSDP).reshape(kvw, rank)
+    grad_u = exchange(u_mine, SPLIT).reshape(kvw, rank)
     v_two = jnp.concatenate([v_mine, lax.ppermute(v_mine, "z0", flips(n_z0, 2))], axis=0)
     v_pieces = [v_two, lax.ppermute(v_two, "z0", flips(n_z0, 1))]
     order = jnp.bitwise_xor(lax.axis_index("z0"), jnp.array([0, 2, 1, 3], jnp.int32))

time: 148 us -> 150 us (1.014)
  blocking collectives: 61.4 us -> 19.6 us
  waiting for transfers between devices: 24.5 us -> 50.2 us
  starting transfers between devices: 47.5 us -> 60.2 us
  local copies, waits for them, and re-layouts: 2.42 us -> 5.4 us
    all_to_all x3 -> x1, blocking collectives: 61.4 us -> 19.6 us  [exchange(): return lax.all_to_all(parts, axes, 0, 0, tiled=True)]
    all_to_all x3 -> x5, waiting for transfers between devices: 14.2 us -> 34.8 us  [exchange(): return lax.all_to_all(parts, axes, 0, 0, tiled=True)]
    all_to_all x3 -> x5, starting transfers between devices: 26.1 us -> 35.1 us  [exchange(): return lax.all_to_all(parts, axes, 0, 0, tiled=True)]
    ppermute x1, waiting for transfers between devices: 0.01 us -> 5.37 us  [shards(): lax.ppermute(v_mine, 'z0', flips(n_z0, 2))]
    ppermute x0 -> x1, starting transfers between devices: none -> 3.71 us  [shards(): others = lax.ppermute(jnp.concatenate(others, axis=1), 'core', swap)]
    unnamed x20 -> x24, local copies, waits for them, and re-layouts: 0.76 us -> 3.53 us
  transfers between devices with their start and end apart: 8 -> 11, of which waited for: 4 -> 7; matrix products, arithmetic and copies ran while one was open for 1% -> 2% of each run, Pallas kernels for 1% -> 1%
where the time goes in v7:
time: 150 us; the launch traced here: 149 us
  starting transfers between devices  60.2 us (40%)
  waiting for transfers between devices  50.2 us (33%)
  blocking collectives  19.6 us (13%)
  Pallas kernels  8.27 us (6%)
  local copies, waits for them, and re-layouts  5.4 us (4%)
  other arithmetic  4.69 us (3%)
    all_to_all x5, starting transfers between devices, exchange(): return lax.all_to_all(parts, axes, 0, 0, tiled=True)  35.1 us
    all_to_all x5, waiting for transfers between devices, exchange(): return lax.all_to_all(parts, axes, 0, 0, tiled=True)  34.8 us
    all_to_all x1, blocking collectives, exchange(): return lax.all_to_all(parts, axes, 0, 0, tiled=True)  19.6 us
    pallas_call x6, Pallas kernels, kernel_call(): pl.pallas_call(kernel, out_shape=out, in_specs=[IN_SMEM] * scalars + [IN_...  8.27 us
    ppermute x1, starting transfers between devices, shards(): lax.ppermute(across, 'core', swap)  7.83 us
    ppermute x1, starting transfers between devices, shards(): lax.ppermute(own, 'core', swap)  6.29 us
    ppermute x1, waiting for transfers between devices, shards(): lax.ppermute(v_mine, 'z0', flips(n_z0, 2))  5.37 us
    ppermute x1, waiting for transfers between devices, shards(): v_pieces = [v_two, lax.ppermute(v_two, 'z0', flips(n_z0, 1))]  4.57 us
  transfers between devices with their start and end apart: 11, of which 7 were waited for; matrix products, arithmetic and copies ran while one was open for 2% of the time, Pallas kernels for 1%

profile of v7, /device:TPU:1, one launch (start us, length us, event | category | flops | bytes accessed | tf_op | source)
XLA Modules:
  0.0 149.2 jit_solution(6456330644806773092)
XLA Ops:
  0.6 1.8 %slice_bitcast_fusion.3 = (bf16[1,128,2048]{2,1,0:T(8,128)(2,1)S(1)}, bf16[1,128,2048]{2,1,0:T(8,128)(2,1)S(1)}, bf16[1,128,2048]{2,1,0:T(8,128)(2,1)S(1)}, bf16[1,128,2048]{2,1,0:T(8,128)(2,1)S(1)}) fusion(bf16[128,8192]{1,0:T(8,128)(2,1)} %param.10), kind=kLoop, calls=%fused_computation.6 | loop fusion | bytes 4194304 | tf_op jit(solution)/shard_map/stack | solution.py:165
  2.4 1.6 %pad_maximum_fusion = bf16[4,128,2048]{2,1,0:T(8,128)(2,1)} fusion(bf16[1,128,2048]{2,1,0:T(8,128)(2,1)S(1)} %get-tuple-element.10, bf16[1,128,2048]{2,1,0:T(8,128)(2,1)S(1)} %get-tuple-element.11, bf16[1,128,2048]{2,1,0:T(8,128)(2,1)S(1)} %get-tuple-element.9, bf16[1,128,2048]{2,1,0:T(8,128)(2,1)S(1)} %get-tuple-element.8), kind=kLoop, calls=%fused_computation | loop fusion | flops 3145728 | bytes 4194304 | tf_op jit(solution)/shard_map/stack | solution.py:165
  4.0 0.0 copy-start.9
  4.0 0.0 copy-start.7
  4.0 0.0 copy-start.8
  4.0 0.0 copy-start.5
  4.0 0.0 copy-start.6
  4.0 0.0 copy-start.4
  4.1 5.0 %all-to-all-start = ((bf16[4,128,2048]{2,1,0:T(8,128)(2,1)}), bf16[4,128,2048]{2,1,0:T(8,128)(2,1)S(1)}, u32[]{:S(2)}, u32[]{:S(2)}) async-start(bf16[4,128,2048]{2,1,0:T(8,128)(2,1)} %pad_maximum_fusion), calls=%async_computation | async-start | bytes 4194304 | tf_op jit(solution)/shard_map/all_to_all | solution.py:30
  9.0 0.0 copy-done.9
  9.1 0.0 copy-done.7
  9.1 0.0 copy-done.8
  9.1 0.0 copy-done.5
  9.1 0.0 copy-done.6
  9.1 1.9 %multiply_convert_fusion = (bf16[512,128]{1,0:T(8,128)(2,1)S(1)}, bf16[512,128]{1,0:T(8,128)(2,1)S(1)}) fusion(f32[512,128]{1,0:T(8,128)S(1)} %copy-done.5, f32[128]{0:T(128)S(1)} %get-tuple-element.16, f32[128]{0:T(128)S(1)} %get-tuple-element.15, f32[128]{0:T(128)S(1)} %get-tuple-element.14, f32[512,128]{1,0:T(8,128)S(1)} %copy-done.6, ...), kind=kLoop, calls=%fused_computation.7 | loop fusion | flops 1048576 | bytes 788480 | tf_op jit(solution)/shard_map/convert_element_type | solution.py:167
  11.0 0.0 copy-done.4
  11.0 0.1 pad_maximum_fusion.2.refs_0_
  11.1 3.2 %collective-permute-start.2 = (bf16[512,640]{1,0:T(8,128)(2,1)S(1)}, bf16[512,640]{1,0:T(8,128)(2,1)S(1)}, u32[]{:S(2)}, u32[]{:S(2)}) collective-permute-start(bf16[512,640]{1,0:T(8,128)(2,1)S(1)} %pad_maximum_fusion.2.refs_0_), channel_id=1, source_target_pairs={{0,2},{2,0},{1,3},{3,1},{4,6},{6,4},{5,7},{7,5},{8,10},{10,8},{9,1... | collective-permute-start | bytes 1966088 | tf_op jit(solution)/shard_map/ppermute | solution.py:162
  14.3 6.3 %collective-permute-start.1 = (bf16[512,640]{1,0:T(8,128)(2,1)S(1)}, bf16[512,640]{1,0:T(8,128)(2,1)}, u32[]{:S(2)}, u32[]{:S(2)}) collective-permute-start(bf16[512,640]{1,0:T(8,128)(2,1)S(1)} %pad_maximum_fusion.2.refs_0_), channel_id=1, source_target_pairs={{0,1},{1,0},{2,3},{3,2},{4,5},{5,4},{6,7},{7,6},{8,9},{9,8},{10,11... | collective-permute-start | bytes 1966088 | tf_op jit(solution)/shard_map/ppermute | solution.py:163
  20.6 3.6 %collective-permute-done.2.refs_2_ = bf16[512,640]{1,0:T(8,128)(2,1)S(1)} collective-permute-done((bf16[512,640]{1,0:T(8,128)(2,1)S(1)}, bf16[512,640]{1,0:T(8,128)(2,1)S(1)}, u32[]{:S(2)}, u32[]{:S(2)}) %collective-permute-start.2) | collective-permute-done | bytes 655392 | tf_op jit(solution)/shard_map/ppermute | solution.py:162
  24.2 7.8 %collective-permute-start.3 = (bf16[512,640]{1,0:T(8,128)(2,1)S(1)}, bf16[512,640]{1,0:T(8,128)(2,1)}, u32[]{:S(2)}, u32[]{:S(2)}) collective-permute-start(bf16[512,640]{1,0:T(8,128)(2,1)S(1)} %collective-permute-done.2.refs_2_), channel_id=1, source_target_pairs={{0,1},{1,0},{2,3},{3,2},{4,5},{5,4},{6,7},{7,6},{8,9},{9,8},{10,11... | collective-permute-start | bytes 1966088 | tf_op jit(solution)/shard_map/ppermute | solution.py:163
  32.0 0.0 collective-permute-done.1.refs_1_
  32.0 1.8 %collective-permute-done.3.refs_3_ = bf16[512,640]{1,0:T(8,128)(2,1)} collective-permute-done((bf16[512,640]{1,0:T(8,128)(2,1)S(1)}, bf16[512,640]{1,0:T(8,128)(2,1)}, u32[]{:S(2)}, u32[]{:S(2)}) %collective-permute-start.3) | collective-permute-done | bytes 655392 | tf_op jit(solution)/shard_map/ppermute | solution.py:163
  33.9 0.0 all-to-all-done
  33.9 3.1 %partial_products.1 = f32[4,128,640]{2,1,0:T(8,128)S(1)} custom-call(s32[4]{0:T(128)S(1)} %iota_xor_fusion.order_ref, bf16[512,2048]{1,0:T(8,128)(2,1)S(1)} %bitcast.12, bf16[512,640]{1,0:T(8,128)(2,1)S(1)} %pad_maximum_fusion.2.refs_0_, bf16[512,640]{1,0:T(8,128)(2,1)} %collective-permute-done.1.refs_1_, ...), custom_call_target="tpu_custom_call" | custom-call | tf_op jit(solution)/shard_map/partial_products/pallas_call | solution.py:142
  37.0 0.0 copy-start
  37.0 1.1 copy-done
  38.1 4.2 %all-to-all-start.1 = ((f32[4,128,640]{2,1,0:T(8,128)}), f32[4,128,640]{2,1,0:T(8,128)S(1)}, u32[]{:S(2)}, u32[]{:S(2)}) async-start(f32[4,128,640]{2,1,0:T(8,128)} %copy-done), calls=%async_computation.1 | async-start | bytes 2621440 | tf_op jit(solution)/shard_map/all_to_all | solution.py:30
  42.3 0.0 copy-start.3
  42.3 0.1 constant_dynamic-slice_fusion.1
  42.4 1.1 pad_maximum_fusion.1
  43.5 3.7 %collective-permute-start = (bf16[512,1024]{1,0:T(8,128)(2,1)}, bf16[512,1024]{1,0:T(8,128)(2,1)}, u32[]{:S(2)}, u32[]{:S(2)}) collective-permute-start(bf16[512,1024]{1,0:T(8,128)(2,1)} %pad_maximum_fusion.1), channel_id=1, source_target_pairs={{0,1},{1,0},{2,3},{3,2},{4,5},{5,4},{6,7},{7,6},{8,9},{9,8},{10,11... | collective-permute-start | bytes 3145736 | tf_op jit(solution)/shard_map/ppermute | solution.py:184
  47.2 11.3 %all-to-all-done.1.parts_ref = f32[4,128,640]{2,1,0:T(8,128)S(1)} async-done(((f32[4,128,640]{2,1,0:T(8,128)}), f32[4,128,640]{2,1,0:T(8,128)S(1)}, u32[]{:S(2)}, u32[]{:S(2)}) %all-to-all-start.1) | async-done | bytes 1310752 | tf_op jit(solution)/shard_map/all_to_all | solution.py:30
  58.5 0.0 copy-done.3
  58.5 0.0 copy-start.2
  58.5 0.9 copy-done.2
  59.4 0.4 residual_and_grad_u.1
  59.8 0.0 copy-start.1
  59.8 0.8 copy-done.1
  60.6 6.1 %all-to-all-start.2 = ((bf16[8,256,128]{2,1,0:T(8,128)(2,1)}), bf16[8,256,128]{2,1,0:T(8,128)(2,1)S(1)}, u32[]{:S(2)}, u32[]{:S(2)}) async-start(bf16[8,256,128]{2,1,0:T(8,128)(2,1)} %copy-done.1), calls=%async_computation.2 | async-start | bytes 1048576 | tf_op jit(solution)/shard_map/all_to_all | solution.py:30
  66.7 0.0 collective-permute-done.others_ref
  66.7 9.5 %all-to-all-done.2.arrived_ref = bf16[8,256,128]{2,1,0:T(8,128)(2,1)S(1)} async-done(((bf16[8,256,128]{2,1,0:T(8,128)(2,1)}), bf16[8,256,128]{2,1,0:T(8,128)(2,1)S(1)}, u32[]{:S(2)}, u32[]{:S(2)}) %all-to-all-start.2) | async-done | bytes 524320 | tf_op jit(solution)/shard_map/all_to_all | solution.py:30
  76.2 2.0 %grads_packed.1 = bf16[16,80,128]{2,1,0:T(8,128)(2,1)S(1)} custom-call(s32[1]{0:T(128)} %bitcast.core_ref, bf16[512,2048]{1,0:T(8,128)(2,1)S(1)} %bitcast.14, bf16[512,1024]{1,0:T(8,128)(2,1)} %collective-permute-done.others_ref, bf16[8,256,128]{2,1,0:T(8,128)(2,1)S(1)} %all-to-all-done.2.arrived_ref), custom_call_target="tpu_custom_call" | custom-call | tf_op jit(solution)/shard_map/grads_packed/pallas_call | solution.py:142
  78.2 0.0 copy-start.10
  78.2 19.6 %all_to_all.30.arrived_ref = bf16[16,80,128]{2,1,0:T(8,128)(2,1)S(1)} all-to-all(bf16[16,80,128]{2,1,0:T(8,128)(2,1)S(1)} %grads_packed.1), channel_id=1, replica_groups=mesh['z1'=4,'z0'=4,'yh'=2,'x'=4,'yl'=2,'core'=2] {'yl','yh','z0'}, dimensions={0} | all-to-all | bytes 655360 | tf_op jit(solution)/shard_map/all_to_all | solution.py:30
  97.8 0.7 close_sum.1
  98.5 12.3 %all-to-all-start.4 = ((bf16[8,80,128]{2,1,0:T(8,128)(2,1)}), bf16[8,80,128]{2,1,0:T(8,128)(2,1)S(1)}, u32[]{:S(2)}, u32[]{:S(2)}) async-start(bf16[8,80,128]{2,1,0:T(8,128)(2,1)} %close_sum.1), calls=%async_computation.4 | async-start | bytes 327680 | tf_op jit(solution)/shard_map/all_to_all | solution.py:30
  110.8 14.1 %all-to-all-done.4.arrived_ref = bf16[8,80,128]{2,1,0:T(8,128)(2,1)S(1)} async-done(((bf16[8,80,128]{2,1,0:T(8,128)(2,1)}), bf16[8,80,128]{2,1,0:T(8,128)(2,1)S(1)}, u32[]{:S(2)}, u32[]{:S(2)}) %all-to-all-start.4) | async-done | bytes 163872 | tf_op jit(solution)/shard_map/all_to_all | solution.py:30
  124.9 0.7 far_sum.1
  125.6 7.5 %all-to-all-start.5 = ((f32[16,32,128]{2,1,0:T(8,128)}), f32[16,32,128]{2,1,0:T(8,128)S(1)}, u32[]{:S(2)}, u32[]{:S(2)}) async-start(f32[16,32,128]{2,1,0:T(8,128)} %get-tuple-element.5), calls=%async_computation.5 | async-start | bytes 524288 | tf_op jit(solution)/shard_map/all_to_all | solution.py:30
  133.1 2.2 %collective-permute-start.4 = (f32[128,128]{1,0:T(8,128)S(1)}, f32[128,128]{1,0:T(8,128)S(1)}, u32[]{:S(2)}, u32[]{:S(2)}) collective-permute-start(f32[128,128]{1,0:T(8,128)S(1)} %get-tuple-element.4), channel_id=1, source_target_pairs={{0,64},{32,96},{64,0},{96,32},{1,65},{33,97},{65,1},{97,33},{2,66}... | collective-permute-start | bytes 196616 | tf_op jit(solution)/shard_map/ppermute | solution.py:214
  135.3 5.4 %collective-permute-done.4 = f32[128,128]{1,0:T(8,128)S(1)} collective-permute-done((f32[128,128]{1,0:T(8,128)S(1)}, f32[128,128]{1,0:T(8,128)S(1)}, u32[]{:S(2)}, u32[]{:S(2)}) %collective-permute-start.4) | collective-permute-done | bytes 65568 | tf_op jit(solution)/shard_map/ppermute | solution.py:214
  140.7 1.9 %collective-permute-start.5 = (f32[256,128]{1,0:T(8,128)S(1)}, f32[256,128]{1,0:T(8,128)S(1)}, u32[]{:S(2)}, u32[]{:S(2)}) collective-permute-start(f32[256,128]{1,0:T(8,128)S(1)} %constant_dynamic-update-slice_fusion.refs_0_), channel_id=1, source_target_pairs={{0,32},{32,0},{64,96},{96,64},{1,33},{33,1},{65,97},{97,65},{2,34}... | collective-permute-start | bytes 393224 | tf_op jit(solution)/shard_map/ppermute | solution.py:215
  142.6 0.0 copy-done.10
  142.6 4.6 %collective-permute-done.5.refs_1_ = f32[256,128]{1,0:T(8,128)S(1)} collective-permute-done((f32[256,128]{1,0:T(8,128)S(1)}, f32[256,128]{1,0:T(8,128)S(1)}, u32[]{:S(2)}, u32[]{:S(2)}) %collective-permute-start.5) | collective-permute-done | bytes 131104 | tf_op jit(solution)/shard_map/ppermute | solution.py:215
  147.2 1.3 grad_v.1
  148.5 0.0 all-to-all-done.5
  148.5 0.7 copy.14
  (6 shorter events, 0.0 us)
Async XLA Ops:
  4.0 5.0 %copy-start.9 = (s32[128]{0:T(128)S(1)}, s32[128]{0:T(128)}, u32[]{:S(2)}) copy-start(s32[128]{0:T(128)} %param.16) | copy-start | bytes 1540
  4.0 5.0 %copy-start.7 = (s32[128]{0:T(128)S(1)}, s32[128]{0:T(128)}, u32[]{:S(2)}) copy-start(s32[128]{0:T(128)} %param.18) | copy-start | bytes 1540
  4.0 5.0 %copy-start.8 = (s32[128]{0:T(128)S(1)}, s32[128]{0:T(128)}, u32[]{:S(2)}) copy-start(s32[128]{0:T(128)} %param.17) | copy-start | bytes 1540
  4.0 5.1 %copy-start.5 = (f32[512,128]{1,0:T(8,128)S(1)}, f32[512,128]{1,0:T(8,128)}, u32[]{:S(2)}) copy-start(f32[512,128]{1,0:T(8,128)} %param.14) | copy-start | bytes 786436
  4.0 5.1 %copy-start.6 = (f32[512,128]{1,0:T(8,128)S(1)}, f32[512,128]{1,0:T(8,128)}, u32[]{:S(2)}) copy-start(f32[512,128]{1,0:T(8,128)} %param.13) | copy-start | bytes 786436
  4.0 7.0 %copy-start.4 = (bf16[512,512]{1,0:T(8,128)(2,1)S(1)}, bf16[512,512]{1,0:T(8,128)(2,1)}, u32[]{:S(2)}) copy-start(bf16[512,512]{1,0:T(8,128)(2,1)} %param.12) | copy-start | bytes 1572868
  4.1 29.8 %all-to-all-start = ((bf16[4,128,2048]{2,1,0:T(8,128)(2,1)}), bf16[4,128,2048]{2,1,0:T(8,128)(2,1)S(1)}, u32[]{:S(2)}, u32[]{:S(2)}) async-start(bf16[4,128,2048]{2,1,0:T(8,128)(2,1)} %pad_maximum_fusion), calls=%async_computation | async-start | bytes 4194304 | tf_op jit(solution)/shard_map/all_to_all | solution.py:30
  11.1 13.1 %collective-permute-start.2 = (bf16[512,640]{1,0:T(8,128)(2,1)S(1)}, bf16[512,640]{1,0:T(8,128)(2,1)S(1)}, u32[]{:S(2)}, u32[]{:S(2)}) collective-permute-start(bf16[512,640]{1,0:T(8,128)(2,1)S(1)} %pad_maximum_fusion.2.refs_0_), channel_id=1, source_target_pairs={{0,2},{2,0},{1,3},{3,1},{4,6},{6,4},{5,7},{7,5},{8,10},{10,8},{9,1... | collective-permute-start | bytes 1966088 | tf_op jit(solution)/shard_map/ppermute | solution.py:162
  14.3 17.8 %collective-permute-start.1 = (bf16[512,640]{1,0:T(8,128)(2,1)S(1)}, bf16[512,640]{1,0:T(8,128)(2,1)}, u32[]{:S(2)}, u32[]{:S(2)}) collective-permute-start(bf16[512,640]{1,0:T(8,128)(2,1)S(1)} %pad_maximum_fusion.2.refs_0_), channel_id=1, source_target_pairs={{0,1},{1,0},{2,3},{3,2},{4,5},{5,4},{6,7},{7,6},{8,9},{9,8},{10,11... | collective-permute-start | bytes 1966088 | tf_op jit(solution)/shard_map/ppermute | solution.py:163
  24.2 9.7 %collective-permute-start.3 = (bf16[512,640]{1,0:T(8,128)(2,1)S(1)}, bf16[512,640]{1,0:T(8,128)(2,1)}, u32[]{:S(2)}, u32[]{:S(2)}) collective-permute-start(bf16[512,640]{1,0:T(8,128)(2,1)S(1)} %collective-permute-done.2.refs_2_), channel_id=1, source_target_pairs={{0,1},{1,0},{2,3},{3,2},{4,5},{5,4},{6,7},{7,6},{8,9},{9,8},{10,11... | collective-permute-start | bytes 1966088 | tf_op jit(solution)/shard_map/ppermute | solution.py:163
  37.0 1.1 copy-start
  38.1 20.4 %all-to-all-start.1 = ((f32[4,128,640]{2,1,0:T(8,128)}), f32[4,128,640]{2,1,0:T(8,128)S(1)}, u32[]{:S(2)}, u32[]{:S(2)}) async-start(f32[4,128,640]{2,1,0:T(8,128)} %copy-done), calls=%async_computation.1 | async-start | bytes 2621440 | tf_op jit(solution)/shard_map/all_to_all | solution.py:30
  42.3 16.2 %copy-start.3 = (f32[128]{0:T(128)S(1)}, f32[128]{0:T(128)}, u32[]{:S(2)}) copy-start(f32[128]{0:T(128)} %param.15) | copy-start | bytes 1540
  43.5 23.2 %collective-permute-start = (bf16[512,1024]{1,0:T(8,128)(2,1)}, bf16[512,1024]{1,0:T(8,128)(2,1)}, u32[]{:S(2)}, u32[]{:S(2)}) collective-permute-start(bf16[512,1024]{1,0:T(8,128)(2,1)} %pad_maximum_fusion.1), channel_id=1, source_target_pairs={{0,1},{1,0},{2,3},{3,2},{4,5},{5,4},{6,7},{7,6},{8,9},{9,8},{10,11... | collective-permute-start | bytes 3145736 | tf_op jit(solution)/shard_map/ppermute | solution.py:184
  58.5 0.9 copy-start.2
  59.8 0.8 copy-start.1
  60.6 15.6 %all-to-all-start.2 = ((bf16[8,256,128]{2,1,0:T(8,128)(2,1)}), bf16[8,256,128]{2,1,0:T(8,128)(2,1)S(1)}, u32[]{:S(2)}, u32[]{:S(2)}) async-start(bf16[8,256,128]{2,1,0:T(8,128)(2,1)} %copy-done.1), calls=%async_computation.2 | async-start | bytes 1048576 | tf_op jit(solution)/shard_map/all_to_all | solution.py:30
  78.2 64.4 %copy-start.10 = (s32[4]{0:T(128)S(1)}, s32[4]{0:T(128)}, u32[]{:S(2)}) copy-start(s32[4]{0:T(128)} %constant.37.clone) | copy-start | bytes 52
  98.5 26.3 %all-to-all-start.4 = ((bf16[8,80,128]{2,1,0:T(8,128)(2,1)}), bf16[8,80,128]{2,1,0:T(8,128)(2,1)S(1)}, u32[]{:S(2)}, u32[]{:S(2)}) async-start(bf16[8,80,128]{2,1,0:T(8,128)(2,1)} %close_sum.1), calls=%async_computation.4 | async-start | bytes 327680 | tf_op jit(solution)/shard_map/all_to_all | solution.py:30
  125.6 22.9 %all-to-all-start.5 = ((f32[16,32,128]{2,1,0:T(8,128)}), f32[16,32,128]{2,1,0:T(8,128)S(1)}, u32[]{:S(2)}, u32[]{:S(2)}) async-start(f32[16,32,128]{2,1,0:T(8,128)} %get-tuple-element.5), calls=%async_computation.5 | async-start | bytes 524288 | tf_op jit(solution)/shard_map/all_to_all | solution.py:30
  133.1 7.6 %collective-permute-start.4 = (f32[128,128]{1,0:T(8,128)S(1)}, f32[128,128]{1,0:T(8,128)S(1)}, u32[]{:S(2)}, u32[]{:S(2)}) collective-permute-start(f32[128,128]{1,0:T(8,128)S(1)} %get-tuple-element.4), channel_id=1, source_target_pairs={{0,64},{32,96},{64,0},{96,32},{1,65},{33,97},{65,1},{97,33},{2,66}... | collective-permute-start | bytes 196616 | tf_op jit(solution)/shard_map/ppermute | solution.py:214
  140.7 6.5 %collective-permute-start.5 = (f32[256,128]{1,0:T(8,128)S(1)}, f32[256,128]{1,0:T(8,128)S(1)}, u32[]{:S(2)}, u32[]{:S(2)}) collective-permute-start(f32[256,128]{1,0:T(8,128)S(1)} %constant_dynamic-update-slice_fusion.refs_0_), channel_id=1, source_target_pairs={{0,32},{32,0},{64,96},{96,64},{1,33},{33,1},{65,97},{97,65},{2,34}... | collective-permute-start | bytes 393224 | tf_op jit(solution)/shard_map/ppermute | solution.py:215

commit v8 on v7

--- a/solution.py
+++ b/solution.py
@@ -114,17 +114,26 @@
         out_ref[i] = total.astype(out_ref.dtype)
 
 
-def far_sum_kernel(arrived_ref, v_ref, u_ref):
+def far_v_kernel(arrived_ref, v_ref):
+    n_yh = 2
+    rows = v_ref.shape[0] // n_yh
+    for h in range(n_yh):
+        total = arrived_ref[h, :rows].astype(jnp.float32)
+        for i in range(h + n_yh, arrived_ref.shape[0], n_yh):
+            total = total + arrived_ref[i, :rows].astype(jnp.float32)
+        v_ref[h * rows : (h + 1) * rows] = total
+
+
+def far_u_kernel(arrived_ref, v_ref, u_ref):
     n_yh = 2
     v_rows = v_ref.shape[0] // n_yh
-    u_rows = u_ref.shape[1] // n_yh
+    rows = u_ref.shape[1] // n_yh
     for h in range(n_yh):
-        total = arrived_ref[h].astype(jnp.float32)
+        total = arrived_ref[h, v_rows:].astype(jnp.float32)
         for i in range(h + n_yh, arrived_ref.shape[0], n_yh):
-            total = total + arrived_ref[i].astype(jnp.float32)
-        v_ref[h * v_rows : (h + 1) * v_rows] = total[:v_rows]
+            total = total + arrived_ref[i, v_rows:].astype(jnp.float32)
         for i in range(u_ref.shape[0]):
-            u_ref[i, h * u_rows : (h + 1) * u_rows] = total[v_rows:]
+            u_ref[i, h * rows : (h + 1) * rows] = total
 
 
 def place_kernel(order_ref, *refs):
@@ -182,12 +191,13 @@
         for i in range(n_near // 2)
     ]
     others = lax.ppermute(jnp.concatenate(others, axis=1), "core", swap)
+    out_parts, others = lax.optimization_barrier((exchange(part, "x"), others))
     scale = 1.0 / math.sqrt(tok * math.prod(lax.axis_size(a) for a in AXES))
     ranks = kernel_call(
         functools.partial(middle_kernel, scale),
         shape((2 * n_x, tok + kvw // n_x, rank), bf16),
         "residual_and_grad_u",
-        (exchange(part, "x"), target, u_quant, sigma.reshape(1, rank)),
+        (out_parts, target, u_quant, sigma.reshape(1, rank)),
     )
     n_close, n_far = lax.axis_size(CLOSE), lax.axis_size(FAR)
     v_rows, u_rows = wide // (2 * n_close), kvw * n_z0 // (2 * n_x * n_close)
@@ -204,11 +214,13 @@
         "close_sum",
         (exchange(parts, CLOSE),),
     )
-    v_mine, u_mine = kernel_call(
-        far_sum_kernel,
-        (shape((2 * v_rows, rank), f32), shape((lax.axis_size(SPLIT), 2 * u_rows, rank), f32)),
-        "far_sum",
-        (exchange(mine, FAR),),
+    arrived = exchange(mine, FAR)
+    v_mine = kernel_call(far_v_kernel, shape((2 * v_rows, rank), f32), "far_v", (arrived,))
+    u_mine = kernel_call(
+        far_u_kernel,
+        shape((lax.axis_size(SPLIT), 2 * u_rows, rank), f32),
+        "far_u",
+        (arrived, v_mine),
     )
     grad_u = exchange(u_mine, SPLIT).reshape(kvw, rank)
     v_two = jnp.concatenate([v_mine, lax.ppermute(v_mine, "z0", flips(n_z0, 2))], axis=0)

time: 150 us -> 143 us (0.953)
  blocking collectives: 19.6 us -> 78.9 us
  waiting for transfers between devices: 50.2 us -> 8.25 us
  starting transfers between devices: 60.2 us -> 40.7 us
  local copies, waits for them, and re-layouts: 5.4 us -> 2.62 us
  Pallas kernels: 8.27 us -> 6.38 us
    all_to_all x1 -> x4, blocking collectives: 19.6 us -> 78.9 us  [exchange(): return lax.all_to_all(parts, axes, 0, 0, tiled=True)]
    all_to_all x5 -> x2, waiting for transfers between devices: 34.8 us -> 0.01 us  [exchange(): return lax.all_to_all(parts, axes, 0, 0, tiled=True)]
    all_to_all x5 -> x2, starting transfers between devices: 35.1 us -> 12.1 us  [exchange(): return lax.all_to_all(parts, axes, 0, 0, tiled=True)]
    ppermute x1, waiting for transfers between devices: 5.37 us -> 0.01 us  [shards(): lax.ppermute(v_mine, 'z0', flips(n_z0, 2))]
    unnamed x24 -> x19, local copies, waits for them, and re-layouts: 3.53 us -> 0.75 us
    ppermute x1, starting transfers between devices: 3.71 us -> 6.19 us  [shards(): others = lax.ppermute(jnp.concatenate(others, axis=1), 'core', swap)]
    pallas_call x6 -> x7, Pallas kernels: 8.27 us -> 6.38 us  [kernel_call(): pl.pallas_call(kernel, out_shape=out, in_specs=[IN_SMEM] * scalars + [IN_...]
    ppermute x1, waiting for transfers between devices: 1.8 us -> 0.01 us  [shards(): lax.ppermute(across, 'core', swap)]
  transfers between devices with their start and end apart: 11 -> 8, of which waited for: 7 -> 2; matrix products, arithmetic and copies ran while one was open for 2% -> 2% of each run, Pallas kernels for 1% -> 4%
where the time goes in v8:
time: 143 us; the launch traced here: 141 us
  blocking collectives  78.9 us (55%)
  starting transfers between devices  40.7 us (28%)
  waiting for transfers between devices  8.25 us (6%)
  Pallas kernels  6.38 us (4%)
  other arithmetic  3.7 us (3%)
  local copies, waits for them, and re-layouts  2.62 us (2%)
    all_to_all x4, blocking collectives, exchange(): return lax.all_to_all(parts, axes, 0, 0, tiled=True)  78.9 us
    all_to_all x2, starting transfers between devices, exchange(): return lax.all_to_all(parts, axes, 0, 0, tiled=True)  12.1 us
    ppermute x1, starting transfers between devices, shards(): lax.ppermute(across, 'core', swap)  7.83 us
    pallas_call x7, Pallas kernels, kernel_call(): pl.pallas_call(kernel, out_shape=out, in_specs=[IN_SMEM] * scalars + [IN_...  6.38 us
    ppermute x1, starting transfers between devices, shards(): lax.ppermute(own, 'core', swap)  6.29 us
    ppermute x1, starting transfers between devices, shards(): others = lax.ppermute(jnp.concatenate(others, axis=1), 'core', swap)  6.19 us
    ppermute x1, waiting for transfers between devices, shards(): v_pieces = [v_two, lax.ppermute(v_two, 'z0', flips(n_z0, 1))]  4.63 us
    ppermute x1, waiting for transfers between devices, shards(): across = lax.ppermute(own, 'yl', swap)  3.6 us
  transfers between devices with their start and end apart: 8, of which 2 were waited for; matrix products, arithmetic and copies ran while one was open for 2% of the time, Pallas kernels for 4%

profile of v8, /device:TPU:1, one launch (start us, length us, event | category | flops | bytes accessed | tf_op | source)
XLA Modules:
  0.0 141.5 jit_solution(9747853869147893909)
XLA Ops:
  0.6 1.8 %slice_bitcast_fusion.3 = (bf16[1,128,2048]{2,1,0:T(8,128)(2,1)S(1)}, bf16[1,128,2048]{2,1,0:T(8,128)(2,1)S(1)}, bf16[1,128,2048]{2,1,0:T(8,128)(2,1)S(1)}, bf16[1,128,2048]{2,1,0:T(8,128)(2,1)S(1)}) fusion(bf16[128,8192]{1,0:T(8,128)(2,1)} %param.10), kind=kLoop, calls=%fused_computation.6 | loop fusion | bytes 4194304 | tf_op jit(solution)/shard_map/stack | solution.py:174
  2.4 1.6 %pad_maximum_fusion = bf16[4,128,2048]{2,1,0:T(8,128)(2,1)} fusion(bf16[1,128,2048]{2,1,0:T(8,128)(2,1)S(1)} %get-tuple-element.10, bf16[1,128,2048]{2,1,0:T(8,128)(2,1)S(1)} %get-tuple-element.11, bf16[1,128,2048]{2,1,0:T(8,128)(2,1)S(1)} %get-tuple-element.9, bf16[1,128,2048]{2,1,0:T(8,128)(2,1)S(1)} %get-tuple-element.8), kind=kLoop, calls=%fused_computation | loop fusion | flops 3145728 | bytes 4194304 | tf_op jit(solution)/shard_map/stack | solution.py:174
  4.0 0.0 copy-start.7
  4.0 0.0 copy-start.5
  4.0 0.0 copy-start.6
  4.0 0.0 copy-start.3
  4.0 0.0 copy-start.4
  4.0 0.0 copy-start.2
  4.0 5.0 %all-to-all-start = ((bf16[4,128,2048]{2,1,0:T(8,128)(2,1)}), bf16[4,128,2048]{2,1,0:T(8,128)(2,1)S(1)}, u32[]{:S(2)}, u32[]{:S(2)}) async-start(bf16[4,128,2048]{2,1,0:T(8,128)(2,1)} %pad_maximum_fusion), calls=%async_computation | async-start | bytes 4194304 | tf_op jit(solution)/shard_map/all_to_all | solution.py:30
  9.0 0.0 copy-done.7
  9.0 0.0 copy-done.5
  9.0 0.0 copy-done.6
  9.1 0.0 copy-done.3
  9.1 0.0 copy-done.4
  9.1 1.9 %multiply_convert_fusion = (bf16[512,128]{1,0:T(8,128)(2,1)S(1)}, bf16[512,128]{1,0:T(8,128)(2,1)S(1)}) fusion(f32[512,128]{1,0:T(8,128)S(1)} %copy-done.3, f32[128]{0:T(128)S(1)} %get-tuple-element.16, f32[128]{0:T(128)S(1)} %get-tuple-element.15, f32[128]{0:T(128)S(1)} %get-tuple-element.14, f32[512,128]{1,0:T(8,128)S(1)} %copy-done.4, ...), kind=kLoop, calls=%fused_computation.7 | loop fusion | flops 1048576 | bytes 788480 | tf_op jit(solution)/shard_map/convert_element_type | solution.py:176
  11.0 0.0 copy-done.2
  11.0 0.1 pad_maximum_fusion.2.refs_0_
  11.0 3.2 %collective-permute-start.1 = (bf16[512,640]{1,0:T(8,128)(2,1)S(1)}, bf16[512,640]{1,0:T(8,128)(2,1)S(1)}, u32[]{:S(2)}, u32[]{:S(2)}) collective-permute-start(bf16[512,640]{1,0:T(8,128)(2,1)S(1)} %pad_maximum_fusion.2.refs_0_), channel_id=1, source_target_pairs={{0,2},{2,0},{1,3},{3,1},{4,6},{6,4},{5,7},{7,5},{8,10},{10,8},{9,1... | collective-permute-start | bytes 1966088 | tf_op jit(solution)/shard_map/ppermute | solution.py:171
  14.2 6.3 %collective-permute-start = (bf16[512,640]{1,0:T(8,128)(2,1)S(1)}, bf16[512,640]{1,0:T(8,128)(2,1)}, u32[]{:S(2)}, u32[]{:S(2)}) collective-permute-start(bf16[512,640]{1,0:T(8,128)(2,1)S(1)} %pad_maximum_fusion.2.refs_0_), channel_id=1, source_target_pairs={{0,1},{1,0},{2,3},{3,2},{4,5},{5,4},{6,7},{7,6},{8,9},{9,8},{10,11... | collective-permute-start | bytes 1966088 | tf_op jit(solution)/shard_map/ppermute | solution.py:172
  20.5 3.6 %collective-permute-done.1.refs_2_ = bf16[512,640]{1,0:T(8,128)(2,1)S(1)} collective-permute-done((bf16[512,640]{1,0:T(8,128)(2,1)S(1)}, bf16[512,640]{1,0:T(8,128)(2,1)S(1)}, u32[]{:S(2)}, u32[]{:S(2)}) %collective-permute-start.1) | collective-permute-done | bytes 655392 | tf_op jit(solution)/shard_map/ppermute | solution.py:171
  24.1 7.8 %collective-permute-start.2 = (bf16[512,640]{1,0:T(8,128)(2,1)S(1)}, bf16[512,640]{1,0:T(8,128)(2,1)}, u32[]{:S(2)}, u32[]{:S(2)}) collective-permute-start(bf16[512,640]{1,0:T(8,128)(2,1)S(1)} %collective-permute-done.1.refs_2_), channel_id=1, source_target_pairs={{0,1},{1,0},{2,3},{3,2},{4,5},{5,4},{6,7},{7,6},{8,9},{9,8},{10,11... | collective-permute-start | bytes 1966088 | tf_op jit(solution)/shard_map/ppermute | solution.py:172
  32.0 0.0 all-to-all-done
  32.0 0.1 constant_dynamic-slice_fusion.1
  32.1 0.1 pad_maximum_fusion.1
  32.3 6.2 %collective-permute-start.3 = (bf16[512,1024]{1,0:T(8,128)(2,1)S(1)}, bf16[512,1024]{1,0:T(8,128)(2,1)S(1)}, u32[]{:S(2)}, u32[]{:S(2)}) collective-permute-start(bf16[512,1024]{1,0:T(8,128)(2,1)S(1)} %pad_maximum_fusion.1), channel_id=1, source_target_pairs={{0,1},{1,0},{2,3},{3,2},{4,5},{5,4},{6,7},{7,6},{8,9},{9,8},{10,11... | collective-permute-start | bytes 3145736 | tf_op jit(solution)/shard_map/ppermute | solution.py:193
  38.5 0.0 collective-permute-done.refs_1_
  38.5 0.0 collective-permute-done.2.refs_3_
  38.5 3.1 %partial_products.1 = f32[4,128,640]{2,1,0:T(8,128)S(1)} custom-call(s32[4]{0:T(128)S(1)} %iota_xor_fusion.order_ref, bf16[512,2048]{1,0:T(8,128)(2,1)S(1)} %bitcast.13, bf16[512,640]{1,0:T(8,128)(2,1)S(1)} %pad_maximum_fusion.2.refs_0_, bf16[512,640]{1,0:T(8,128)(2,1)} %collective-permute-done.refs_1_, bf16[512,640]{1,0:T(8,128)(2,1)S(1)} %collective-permute-done.1.refs_2_, ...), custom_call_target="tpu_custom_call" | custom-call | tf_op jit(solution)/shard_map/partial_products/pallas_call | solution.py:151
  41.6 0.0 copy-start
  41.6 0.0 copy-start.1
  41.6 20.3 %all_to_all.30.parts_ref = f32[4,128,640]{2,1,0:T(8,128)S(1)} all-to-all(f32[4,128,640]{2,1,0:T(8,128)S(1)} %partial_products.1), channel_id=1, replica_groups=mesh['z1'=4,'z0'=4,'yh'=2,'x'=4,'yl'=2,'core'=2] {'x'}, dimensions={0} | all-to-all | bytes 2621440 | tf_op jit(solution)/shard_map/all_to_all | solution.py:30
  62.0 0.0 collective-permute-done.3.others_ref
  62.0 0.0 copy-done
  62.0 0.0 copy-done.1
  62.0 0.4 residual_and_grad_u.1
  62.4 12.8 %all_to_all.31.arrived_ref = bf16[8,256,128]{2,1,0:T(8,128)(2,1)S(1)} all-to-all(bf16[8,256,128]{2,1,0:T(8,128)(2,1)S(1)} %residual_and_grad_u.1), channel_id=1, replica_groups=mesh['z1'=4,'z0'=4,'yh'=2,'x'=4,'yl'=2,'core'=2] {'x','core'}, dimensions={0} | all-to-all | bytes 1048576 | tf_op jit(solution)/shard_map/all_to_all | solution.py:30
  75.3 0.8 grads_packed.1
  76.0 0.0 copy-start.8
  76.1 19.6 %all_to_all.32.arrived_ref = bf16[16,80,128]{2,1,0:T(8,128)(2,1)S(1)} all-to-all(bf16[16,80,128]{2,1,0:T(8,128)(2,1)S(1)} %grads_packed.1), channel_id=1, replica_groups=mesh['z1'=4,'z0'=4,'yh'=2,'x'=4,'yl'=2,'core'=2] {'yl','yh','z0'}, dimensions={0} | all-to-all | bytes 655360 | tf_op jit(solution)/shard_map/all_to_all | solution.py:30
  95.6 0.1 close_sum.1
  95.7 26.2 %all_to_all.33.arrived_ref = bf16[8,80,128]{2,1,0:T(8,128)(2,1)S(1)} all-to-all(bf16[8,80,128]{2,1,0:T(8,128)(2,1)S(1)} %close_sum.1), channel_id=1, replica_groups=mesh['z1'=4,'z0'=4,'yh'=2,'x'=4,'yl'=2,'core'=2] {'z1','yh'}, dimensions={0} | all-to-all | bytes 327680 | tf_op jit(solution)/shard_map/all_to_all | solution.py:30
  121.8 3.0 %collective-permute-start.4 = (f32[128,128]{1,0:T(8,128)S(1)}, f32[128,128]{1,0:T(8,128)S(1)}, u32[]{:S(2)}, u32[]{:S(2)}) collective-permute-start(f32[128,128]{1,0:T(8,128)S(1)} %far_v.1.v_ref), channel_id=1, source_target_pairs={{0,64},{32,96},{64,0},{96,32},{1,65},{33,97},{65,1},{97,33},{2,66}... | collective-permute-start | bytes 196616 | tf_op jit(solution)/shard_map/ppermute | solution.py:226
  124.9 0.7 far_u.1
  125.6 7.1 %all-to-all-start.5 = ((f32[16,32,128]{2,1,0:T(8,128)}), f32[16,32,128]{2,1,0:T(8,128)S(1)}, u32[]{:S(2)}, u32[]{:S(2)}) async-start(f32[16,32,128]{2,1,0:T(8,128)} %far_u.1), calls=%async_computation.5 | async-start | bytes 524288 | tf_op jit(solution)/shard_map/all_to_all | solution.py:30
  132.7 0.0 collective-permute-done.4
  132.7 2.1 %collective-permute-start.5 = (f32[256,128]{1,0:T(8,128)S(1)}, f32[256,128]{1,0:T(8,128)S(1)}, u32[]{:S(2)}, u32[]{:S(2)}) collective-permute-start(f32[256,128]{1,0:T(8,128)S(1)} %pad_maximum_fusion.3.refs_0_), channel_id=1, source_target_pairs={{0,32},{32,0},{64,96},{96,64},{1,33},{33,1},{65,97},{97,65},{2,34}... | collective-permute-start | bytes 393224 | tf_op jit(solution)/shard_map/ppermute | solution.py:227
  134.8 0.0 copy-done.8
  134.9 4.6 %collective-permute-done.5.refs_1_ = f32[256,128]{1,0:T(8,128)S(1)} collective-permute-done((f32[256,128]{1,0:T(8,128)S(1)}, f32[256,128]{1,0:T(8,128)S(1)}, u32[]{:S(2)}, u32[]{:S(2)}) %collective-permute-start.5) | collective-permute-done | bytes 131104 | tf_op jit(solution)/shard_map/ppermute | solution.py:227
  139.5 1.3 grad_v.1
  140.8 0.0 all-to-all-done.5
  140.8 0.7 copy.13
  (6 shorter events, 0.1 us)
Async XLA Ops:
  4.0 5.0 %copy-start.7 = (s32[128]{0:T(128)S(1)}, s32[128]{0:T(128)}, u32[]{:S(2)}) copy-start(s32[128]{0:T(128)} %param.16) | copy-start | bytes 1540
  4.0 5.0 %copy-start.5 = (s32[128]{0:T(128)S(1)}, s32[128]{0:T(128)}, u32[]{:S(2)}) copy-start(s32[128]{0:T(128)} %param.18) | copy-start | bytes 1540
  4.0 5.0 %copy-start.6 = (s32[128]{0:T(128)S(1)}, s32[128]{0:T(128)}, u32[]{:S(2)}) copy-start(s32[128]{0:T(128)} %param.17) | copy-start | bytes 1540
  4.0 5.1 %copy-start.3 = (f32[512,128]{1,0:T(8,128)S(1)}, f32[512,128]{1,0:T(8,128)}, u32[]{:S(2)}) copy-start(f32[512,128]{1,0:T(8,128)} %param.14) | copy-start | bytes 786436
  4.0 5.1 %copy-start.4 = (f32[512,128]{1,0:T(8,128)S(1)}, f32[512,128]{1,0:T(8,128)}, u32[]{:S(2)}) copy-start(f32[512,128]{1,0:T(8,128)} %param.13) | copy-start | bytes 786436
  4.0 7.0 %copy-start.2 = (bf16[512,512]{1,0:T(8,128)(2,1)S(1)}, bf16[512,512]{1,0:T(8,128)(2,1)}, u32[]{:S(2)}) copy-start(bf16[512,512]{1,0:T(8,128)(2,1)} %param.12) | copy-start | bytes 1572868
  4.0 28.0 %all-to-all-start = ((bf16[4,128,2048]{2,1,0:T(8,128)(2,1)}), bf16[4,128,2048]{2,1,0:T(8,128)(2,1)S(1)}, u32[]{:S(2)}, u32[]{:S(2)}) async-start(bf16[4,128,2048]{2,1,0:T(8,128)(2,1)} %pad_maximum_fusion), calls=%async_computation | async-start | bytes 4194304 | tf_op jit(solution)/shard_map/all_to_all | solution.py:30
  11.0 13.1 %collective-permute-start.1 = (bf16[512,640]{1,0:T(8,128)(2,1)S(1)}, bf16[512,640]{1,0:T(8,128)(2,1)S(1)}, u32[]{:S(2)}, u32[]{:S(2)}) collective-permute-start(bf16[512,640]{1,0:T(8,128)(2,1)S(1)} %pad_maximum_fusion.2.refs_0_), channel_id=1, source_target_pairs={{0,2},{2,0},{1,3},{3,1},{4,6},{6,4},{5,7},{7,5},{8,10},{10,8},{9,1... | collective-permute-start | bytes 1966088 | tf_op jit(solution)/shard_map/ppermute | solution.py:171
  14.2 24.2 %collective-permute-start = (bf16[512,640]{1,0:T(8,128)(2,1)S(1)}, bf16[512,640]{1,0:T(8,128)(2,1)}, u32[]{:S(2)}, u32[]{:S(2)}) collective-permute-start(bf16[512,640]{1,0:T(8,128)(2,1)S(1)} %pad_maximum_fusion.2.refs_0_), channel_id=1, source_target_pairs={{0,1},{1,0},{2,3},{3,2},{4,5},{5,4},{6,7},{7,6},{8,9},{9,8},{10,11... | collective-permute-start | bytes 1966088 | tf_op jit(solution)/shard_map/ppermute | solution.py:172
  24.1 14.3 %collective-permute-start.2 = (bf16[512,640]{1,0:T(8,128)(2,1)S(1)}, bf16[512,640]{1,0:T(8,128)(2,1)}, u32[]{:S(2)}, u32[]{:S(2)}) collective-permute-start(bf16[512,640]{1,0:T(8,128)(2,1)S(1)} %collective-permute-done.1.refs_2_), channel_id=1, source_target_pairs={{0,1},{1,0},{2,3},{3,2},{4,5},{5,4},{6,7},{7,6},{8,9},{9,8},{10,11... | collective-permute-start | bytes 1966088 | tf_op jit(solution)/shard_map/ppermute | solution.py:172
  32.3 29.7 %collective-permute-start.3 = (bf16[512,1024]{1,0:T(8,128)(2,1)S(1)}, bf16[512,1024]{1,0:T(8,128)(2,1)S(1)}, u32[]{:S(2)}, u32[]{:S(2)}) collective-permute-start(bf16[512,1024]{1,0:T(8,128)(2,1)S(1)} %pad_maximum_fusion.1), channel_id=1, source_target_pairs={{0,1},{1,0},{2,3},{3,2},{4,5},{5,4},{6,7},{7,6},{8,9},{9,8},{10,11... | collective-permute-start | bytes 3145736 | tf_op jit(solution)/shard_map/ppermute | solution.py:193
  41.6 20.4 %copy-start = (bf16[128,512]{1,0:T(8,128)(2,1)S(1)}, bf16[128,512]{1,0:T(8,128)(2,1)}, u32[]{:S(2)}) copy-start(bf16[128,512]{1,0:T(8,128)(2,1)} %target_ref.1) | copy-start | bytes 393220
  41.6 20.4 %copy-start.1 = (f32[128]{0:T(128)S(1)}, f32[128]{0:T(128)}, u32[]{:S(2)}) copy-start(f32[128]{0:T(128)} %param.15) | copy-start | bytes 1540
  76.0 58.8 %copy-start.8 = (s32[4]{0:T(128)S(1)}, s32[4]{0:T(128)}, u32[]{:S(2)}) copy-start(s32[4]{0:T(128)} %constant.37.clone) | copy-start | bytes 52
  121.8 10.8 %collective-permute-start.4 = (f32[128,128]{1,0:T(8,128)S(1)}, f32[128,128]{1,0:T(8,128)S(1)}, u32[]{:S(2)}, u32[]{:S(2)}) collective-permute-start(f32[128,128]{1,0:T(8,128)S(1)} %far_v.1.v_ref), channel_id=1, source_target_pairs={{0,64},{32,96},{64,0},{96,32},{1,65},{33,97},{65,1},{97,33},{2,66}... | collective-permute-start | bytes 196616 | tf_op jit(solution)/shard_map/ppermute | solution.py:226
  125.6 15.2 %all-to-all-start.5 = ((f32[16,32,128]{2,1,0:T(8,128)}), f32[16,32,128]{2,1,0:T(8,128)S(1)}, u32[]{:S(2)}, u32[]{:S(2)}) async-start(f32[16,32,128]{2,1,0:T(8,128)} %far_u.1), calls=%async_computation.5 | async-start | bytes 524288 | tf_op jit(solution)/shard_map/all_to_all | solution.py:30
  132.7 6.8 %collective-permute-start.5 = (f32[256,128]{1,0:T(8,128)S(1)}, f32[256,128]{1,0:T(8,128)S(1)}, u32[]{:S(2)}, u32[]{:S(2)}) collective-permute-start(f32[256,128]{1,0:T(8,128)S(1)} %pad_maximum_fusion.3.refs_0_), channel_id=1, source_target_pairs={{0,32},{32,0},{64,96},{96,64},{1,33},{33,1},{65,97},{97,65},{2,34}... | collective-permute-start | bytes 393224 | tf_op jit(solution)/shard_map/ppermute | solution.py:227

commit v9 on v8

--- a/solution.py
+++ b/solution.py
@@ -136,15 +136,16 @@
             u_ref[i, h * rows : (h + 1) * rows] = total
 
 
-def place_kernel(order_ref, *refs):
-    *piece_refs, out_ref = refs
+def place_kernel(order_ref, u_ref, *refs):
+    *piece_refs, v_ref, out_u_ref = refs
     n_yh, n_z0 = 2, order_ref.shape[0]
-    half = out_ref.shape[0] // n_yh
+    half = v_ref.shape[0] // n_yh
     rows = half // n_z0
     pieces = [p[i : i + rows] for p in piece_refs for i in range(0, p.shape[0], rows)]
     for i, piece in enumerate(pieces):
         start = pl.multiple_of(i % n_yh * half + order_ref[i // n_yh] * rows, rows)
-        out_ref[pl.ds(start, rows)] = piece
+        v_ref[pl.ds(start, rows)] = piece
+    out_u_ref[...] = u_ref[...]
 
 
 def kernel_call(kernel, out, name, operands, scalars=0):
@@ -171,8 +172,8 @@
     across = lax.ppermute(own, "yl", swap)
     pieces = [own, lax.ppermute(own, "core", swap), across, lax.ppermute(across, "core", swap)]
     wide = n_near * rows
-    columns = jnp.stack([hidden[:, i * wide : (i + 1) * wide] for i in range(n_x)])
-    tokens = exchange(columns, "x").reshape(n_x * tok, wide)
+    columns = lax.all_to_all(hidden.reshape(tok, n_x, wide), "x", 1, 1, tiled=True)
+    tokens = columns.transpose(1, 0, 2).reshape(n_x * tok, wide)
     u_quant = fake_quantize(u_factor, bits, u_exps).astype(jnp.bfloat16)
 
     f32, bf16 = jnp.float32, jnp.bfloat16
@@ -191,14 +192,14 @@
         for i in range(n_near // 2)
     ]
     others = lax.ppermute(jnp.concatenate(others, axis=1), "core", swap)
-    out_parts, others = lax.optimization_barrier((exchange(part, "x"), others))
     scale = 1.0 / math.sqrt(tok * math.prod(lax.axis_size(a) for a in AXES))
     ranks = kernel_call(
         functools.partial(middle_kernel, scale),
         shape((2 * n_x, tok + kvw // n_x, rank), bf16),
         "residual_and_grad_u",
-        (out_parts, target, u_quant, sigma.reshape(1, rank)),
-    )
+        (exchange(part, "x"), target, u_quant, sigma.reshape(1, rank)),
+    )
+    ranks, others = lax.optimization_barrier((ranks, others))
     n_close, n_far = lax.axis_size(CLOSE), lax.axis_size(FAR)
     v_rows, u_rows = wide // (2 * n_close), kvw * n_z0 // (2 * n_x * n_close)
     parts = kernel_call(
@@ -226,10 +227,13 @@
     v_two = jnp.concatenate([v_mine, lax.ppermute(v_mine, "z0", flips(n_z0, 2))], axis=0)
     v_pieces = [v_two, lax.ppermute(v_two, "z0", flips(n_z0, 1))]
     order = jnp.bitwise_xor(lax.axis_index("z0"), jnp.array([0, 2, 1, 3], jnp.int32))
-    grad_v = kernel_call(
-        place_kernel, shape((rows, rank), f32), "grad_v", (order, *v_pieces), scalars=1
-    )
-    return (grad_v, grad_u)
+    return kernel_call(
+        place_kernel,
+        (shape((rows, rank), f32), shape((kvw, rank), f32)),
+        "grads",
+        (order, grad_u, *v_pieces),
+        scalars=1,
+    )
 
 
 def solution(mesh):

time: 143 us -> 142 us (level)
  other arithmetic: 3.7 us -> 2.11 us
    all_to_all x0 -> x1, starting transfers between devices: none -> 4.99 us  [shards(): lax.all_to_all(hidden.reshape(tok, n_x, wide), 'x', 1, 1, tiled=True)]
    all_to_all x2 -> x1, starting transfers between devices: 12.1 us -> 7.1 us  [exchange(): return lax.all_to_all(parts, axes, 0, 0, tiled=True)]
    reshape x0 -> x1, local copies, waits for them, and re-layouts: none -> 3.17 us  [shards(): hidden.reshape(tok, n_x, wide)]
    another operation x1 -> x0, local copies, waits for them, and re-layouts: 1.76 us -> none  [shards(): jnp.stack([hidden[:, i * wide:(i + 1) * wide] for i in range(n_x)])]
    another operation x1 -> x0, other arithmetic: 1.59 us -> none  [shards(): jnp.stack([hidden[:, i * wide:(i + 1) * wide] for i in range(n_x)])]
  transfers between devices with their start and end apart: 8 -> 8, of which waited for: 2 -> 3; matrix products, arithmetic and copies ran while one was open for 2% -> 2% of each run, Pallas kernels for 4% -> 3%
where the time goes in v9:
time: 142 us
  blocking collectives  78.9 us (56%)
  starting transfers between devices  40.7 us (29%)
  waiting for transfers between devices  9.35 us (7%)
  Pallas kernels  6.47 us (5%)
  local copies, waits for them, and re-layouts  3.32 us (2%)
  other arithmetic  2.11 us (1%)
    all_to_all x4, blocking collectives, exchange(): return lax.all_to_all(parts, axes, 0, 0, tiled=True)  78.9 us
    ppermute x1, starting transfers between devices, shards(): lax.ppermute(across, 'core', swap)  7.83 us
    all_to_all x1, starting transfers between devices, exchange(): return lax.all_to_all(parts, axes, 0, 0, tiled=True)  7.1 us
    pallas_call x7, Pallas kernels, kernel_call(): pl.pallas_call(kernel, out_shape=out, in_specs=[IN_SMEM] * scalars + [IN_...  6.47 us
    ppermute x1, starting transfers between devices, shards(): lax.ppermute(own, 'core', swap)  6.29 us
    ppermute x1, starting transfers between devices, shards(): others = lax.ppermute(jnp.concatenate(others, axis=1), 'core', swap)  6.19 us
    all_to_all x1, starting transfers between devices, shards(): lax.all_to_all(hidden.reshape(tok, n_x, wide), 'x', 1, 1, tiled=True)  4.99 us
    ppermute x1, waiting for transfers between devices, shards(): v_pieces = [v_two, lax.ppermute(v_two, 'z0', flips(n_z0, 1))]  4.63 us
  transfers between devices with their start and end apart: 8, of which 3 were waited for; matrix products, arithmetic and copies ran while one was open for 2% of the time, Pallas kernels for 3%

profile of v9, /device:TPU:1, one launch (start us, length us, event | category | flops | bytes accessed | tf_op | source)
XLA Modules:
  0.0 141.8 jit_solution(1808193789587351173)
XLA Ops:
  0.6 3.2 %copy.15 = bf16[16,4,8,2048]{3,2,0,1:T(8,128)(2,1)} copy(bf16[16,4,8,2048]{3,2,1,0:T(8,128)(2,1)} %bitcast.16) | data formatting | bytes 4194304 | tf_op jit(solution)/shard_map/reshape | solution.py:175
  3.8 0.0 copy-start.7
  3.8 0.0 copy-start.5
  3.8 0.0 copy-start.6
  3.8 0.0 copy-start.3
  3.8 0.0 copy-start.4
  3.8 0.0 copy-start.2
  3.8 5.0 %all-to-all-start = ((bf16[128,4,2048]{2,0,1:T(8,128)(2,1)}), bf16[128,4,2048]{2,0,1:T(8,128)(2,1)S(1)}, u32[]{:S(2)}, u32[]{:S(2)}) async-start(bf16[128,4,2048]{2,0,1:T(8,128)(2,1)} %bitcast.15), calls=%async_computation | async-start | bytes 4194304 | tf_op jit(solution)/shard_map/all_to_all | solution.py:175
  8.8 0.0 copy-done.7
  8.8 0.0 copy-done.5
  8.8 0.0 copy-done.6
  8.9 0.0 copy-done.3
  8.9 0.0 copy-done.4
  8.9 1.9 %multiply_convert_fusion = (bf16[512,128]{1,0:T(8,128)(2,1)S(1)}, bf16[512,128]{1,0:T(8,128)(2,1)S(1)}) fusion(f32[512,128]{1,0:T(8,128)S(1)} %copy-done.3, f32[128]{0:T(128)S(1)} %get-tuple-element.12, f32[128]{0:T(128)S(1)} %get-tuple-element.11, f32[128]{0:T(128)S(1)} %get-tuple-element.10, f32[512,128]{1,0:T(8,128)S(1)} %copy-done.4, ...), kind=kLoop, calls=%fused_computation.3 | loop fusion | flops 1048576 | bytes 788480 | tf_op jit(solution)/shard_map/convert_element_type | solution.py:177
  10.8 0.0 copy-done.2
  10.8 0.1 pad_maximum_fusion.1.refs_0_
  10.8 3.2 %collective-permute-start.1 = (bf16[512,640]{1,0:T(8,128)(2,1)S(1)}, bf16[512,640]{1,0:T(8,128)(2,1)S(1)}, u32[]{:S(2)}, u32[]{:S(2)}) collective-permute-start(bf16[512,640]{1,0:T(8,128)(2,1)S(1)} %pad_maximum_fusion.1.refs_0_), channel_id=1, source_target_pairs={{0,2},{2,0},{1,3},{3,1},{4,6},{6,4},{5,7},{7,5},{8,10},{10,8},{9,1... | collective-permute-start | bytes 1966088 | tf_op jit(solution)/shard_map/ppermute | solution.py:172
  14.1 6.3 %collective-permute-start = (bf16[512,640]{1,0:T(8,128)(2,1)S(1)}, bf16[512,640]{1,0:T(8,128)(2,1)}, u32[]{:S(2)}, u32[]{:S(2)}) collective-permute-start(bf16[512,640]{1,0:T(8,128)(2,1)S(1)} %pad_maximum_fusion.1.refs_0_), channel_id=1, source_target_pairs={{0,1},{1,0},{2,3},{3,2},{4,5},{5,4},{6,7},{7,6},{8,9},{9,8},{10,11... | collective-permute-start | bytes 1966088 | tf_op jit(solution)/shard_map/ppermute | solution.py:173
  20.4 3.6 %collective-permute-done.1.refs_2_ = bf16[512,640]{1,0:T(8,128)(2,1)S(1)} collective-permute-done((bf16[512,640]{1,0:T(8,128)(2,1)S(1)}, bf16[512,640]{1,0:T(8,128)(2,1)S(1)}, u32[]{:S(2)}, u32[]{:S(2)}) %collective-permute-start.1) | collective-permute-done | bytes 655392 | tf_op jit(solution)/shard_map/ppermute | solution.py:172
  24.0 7.8 %collective-permute-start.2 = (bf16[512,640]{1,0:T(8,128)(2,1)S(1)}, bf16[512,640]{1,0:T(8,128)(2,1)}, u32[]{:S(2)}, u32[]{:S(2)}) collective-permute-start(bf16[512,640]{1,0:T(8,128)(2,1)S(1)} %collective-permute-done.1.refs_2_), channel_id=1, source_target_pairs={{0,1},{1,0},{2,3},{3,2},{4,5},{5,4},{6,7},{7,6},{8,9},{9,8},{10,11... | collective-permute-start | bytes 1966088 | tf_op jit(solution)/shard_map/ppermute | solution.py:173
  31.8 0.0 all-to-all-done
  31.8 0.1 constant_dynamic-slice_fusion.1
  31.9 0.1 pad_maximum_fusion
  32.1 6.2 %collective-permute-start.3 = (bf16[512,1024]{1,0:T(8,128)(2,1)S(1)}, bf16[512,1024]{1,0:T(8,128)(2,1)S(1)}, u32[]{:S(2)}, u32[]{:S(2)}) collective-permute-start(bf16[512,1024]{1,0:T(8,128)(2,1)S(1)} %pad_maximum_fusion), channel_id=1, source_target_pairs={{0,1},{1,0},{2,3},{3,2},{4,5},{5,4},{6,7},{7,6},{8,9},{9,8},{10,11... | collective-permute-start | bytes 3145736 | tf_op jit(solution)/shard_map/ppermute | solution.py:194
  38.3 0.0 collective-permute-done.refs_1_
  38.3 0.0 collective-permute-done.2.refs_3_
  38.3 3.1 %partial_products.1 = f32[4,128,640]{2,1,0:T(8,128)S(1)} custom-call(s32[4]{0:T(128)S(1)} %iota_xor_fusion.order_ref, bf16[512,2048]{1,0:T(8,128)(2,1)S(1)} %bitcast.11, bf16[512,640]{1,0:T(8,128)(2,1)S(1)} %pad_maximum_fusion.1.refs_0_, bf16[512,640]{1,0:T(8,128)(2,1)} %collective-permute-done.refs_1_, bf16[512,640]{1,0:T(8,128)(2,1)S(1)} %collective-permute-done.1.refs_2_, ...), custom_call_target="tpu_custom_call" | custom-call | tf_op jit(solution)/shard_map/partial_products/pallas_call | solution.py:152
  41.4 0.0 copy-start
  41.4 0.0 copy-start.1
  41.4 20.3 %all_to_all.30.parts_ref = f32[4,128,640]{2,1,0:T(8,128)S(1)} all-to-all(f32[4,128,640]{2,1,0:T(8,128)S(1)} %partial_products.1), channel_id=1, replica_groups=mesh['z1'=4,'z0'=4,'yh'=2,'x'=4,'yl'=2,'core'=2] {'x'}, dimensions={0} | all-to-all | bytes 2621440 | tf_op jit(solution)/shard_map/all_to_all | solution.py:30
  61.8 0.0 copy-done
  61.8 0.0 copy-done.1
  61.8 0.4 residual_and_grad_u.1
  62.2 0.0 collective-permute-done.3.others_ref
  62.2 12.9 %all_to_all.31.arrived_ref = bf16[8,256,128]{2,1,0:T(8,128)(2,1)S(1)} all-to-all(bf16[8,256,128]{2,1,0:T(8,128)(2,1)S(1)} %residual_and_grad_u.1), channel_id=1, replica_groups=mesh['z1'=4,'z0'=4,'yh'=2,'x'=4,'yl'=2,'core'=2] {'x','core'}, dimensions={0} | all-to-all | bytes 1048576 | tf_op jit(solution)/shard_map/all_to_all | solution.py:30
  75.1 0.8 grads_packed.1
  75.9 0.0 copy-start.8
  75.9 19.6 %all_to_all.32.arrived_ref = bf16[16,80,128]{2,1,0:T(8,128)(2,1)S(1)} all-to-all(bf16[16,80,128]{2,1,0:T(8,128)(2,1)S(1)} %grads_packed.1), channel_id=1, replica_groups=mesh['z1'=4,'z0'=4,'yh'=2,'x'=4,'yl'=2,'core'=2] {'yl','yh','z0'}, dimensions={0} | all-to-all | bytes 655360 | tf_op jit(solution)/shard_map/all_to_all | solution.py:30
  95.4 0.1 close_sum.1
  95.5 26.1 %all_to_all.33.arrived_ref = bf16[8,80,128]{2,1,0:T(8,128)(2,1)S(1)} all-to-all(bf16[8,80,128]{2,1,0:T(8,128)(2,1)S(1)} %close_sum.1), channel_id=1, replica_groups=mesh['z1'=4,'z0'=4,'yh'=2,'x'=4,'yl'=2,'core'=2] {'z1','yh'}, dimensions={0} | all-to-all | bytes 327680 | tf_op jit(solution)/shard_map/all_to_all | solution.py:30
  121.7 3.0 %collective-permute-start.4 = (f32[128,128]{1,0:T(8,128)S(1)}, f32[128,128]{1,0:T(8,128)S(1)}, u32[]{:S(2)}, u32[]{:S(2)}) collective-permute-start(f32[128,128]{1,0:T(8,128)S(1)} %far_v.1.v_ref), channel_id=1, source_target_pairs={{0,64},{32,96},{64,0},{96,32},{1,65},{33,97},{65,1},{97,33},{2,66}... | collective-permute-start | bytes 196616 | tf_op jit(solution)/shard_map/ppermute | solution.py:227
  124.7 0.7 far_u.1
  125.4 7.1 %all-to-all-start.5 = ((f32[16,32,128]{2,1,0:T(8,128)}), f32[16,32,128]{2,1,0:T(8,128)S(1)}, u32[]{:S(2)}, u32[]{:S(2)}) async-start(f32[16,32,128]{2,1,0:T(8,128)} %far_u.1), calls=%async_computation.5 | async-start | bytes 524288 | tf_op jit(solution)/shard_map/all_to_all | solution.py:30
  132.5 0.0 collective-permute-done.4
  132.5 2.1 %collective-permute-start.5 = (f32[256,128]{1,0:T(8,128)S(1)}, f32[256,128]{1,0:T(8,128)S(1)}, u32[]{:S(2)}, u32[]{:S(2)}) collective-permute-start(f32[256,128]{1,0:T(8,128)S(1)} %pad_maximum_fusion.2.refs_0_), channel_id=1, source_target_pairs={{0,32},{32,0},{64,96},{96,64},{1,33},{33,1},{65,97},{97,65},{2,34}... | collective-permute-start | bytes 393224 | tf_op jit(solution)/shard_map/ppermute | solution.py:228
  134.7 0.0 copy-done.8
  134.7 4.6 %collective-permute-done.5.refs_1_ = f32[256,128]{1,0:T(8,128)S(1)} collective-permute-done((f32[256,128]{1,0:T(8,128)S(1)}, f32[256,128]{1,0:T(8,128)S(1)}, u32[]{:S(2)}, u32[]{:S(2)}) %collective-permute-start.5) | collective-permute-done | bytes 131104 | tf_op jit(solution)/shard_map/ppermute | solution.py:228
  139.3 1.1 all-to-all-done.5
  140.4 1.4 grads.1
  (6 shorter events, 0.1 us)
Async XLA Ops:
  3.8 5.0 %copy-start.7 = (s32[128]{0:T(128)S(1)}, s32[128]{0:T(128)}, u32[]{:S(2)}) copy-start(s32[128]{0:T(128)} %param.16) | copy-start | bytes 1540
  3.8 5.0 %copy-start.5 = (s32[128]{0:T(128)S(1)}, s32[128]{0:T(128)}, u32[]{:S(2)}) copy-start(s32[128]{0:T(128)} %param.18) | copy-start | bytes 1540
  3.8 5.0 %copy-start.6 = (s32[128]{0:T(128)S(1)}, s32[128]{0:T(128)}, u32[]{:S(2)}) copy-start(s32[128]{0:T(128)} %param.17) | copy-start | bytes 1540
  3.8 5.1 %copy-start.3 = (f32[512,128]{1,0:T(8,128)S(1)}, f32[512,128]{1,0:T(8,128)}, u32[]{:S(2)}) copy-start(f32[512,128]{1,0:T(8,128)} %param.14) | copy-start | bytes 786436
  3.8 5.1 %copy-start.4 = (f32[512,128]{1,0:T(8,128)S(1)}, f32[512,128]{1,0:T(8,128)}, u32[]{:S(2)}) copy-start(f32[512,128]{1,0:T(8,128)} %param.13) | copy-start | bytes 786436
  3.8 7.0 %copy-start.2 = (bf16[512,512]{1,0:T(8,128)(2,1)S(1)}, bf16[512,512]{1,0:T(8,128)(2,1)}, u32[]{:S(2)}) copy-start(bf16[512,512]{1,0:T(8,128)(2,1)} %param.12) | copy-start | bytes 1572868
  3.8 28.0 %all-to-all-start = ((bf16[128,4,2048]{2,0,1:T(8,128)(2,1)}), bf16[128,4,2048]{2,0,1:T(8,128)(2,1)S(1)}, u32[]{:S(2)}, u32[]{:S(2)}) async-start(bf16[128,4,2048]{2,0,1:T(8,128)(2,1)} %bitcast.15), calls=%async_computation | async-start | bytes 4194304 | tf_op jit(solution)/shard_map/all_to_all | solution.py:175
  10.8 13.1 %collective-permute-start.1 = (bf16[512,640]{1,0:T(8,128)(2,1)S(1)}, bf16[512,640]{1,0:T(8,128)(2,1)S(1)}, u32[]{:S(2)}, u32[]{:S(2)}) collective-permute-start(bf16[512,640]{1,0:T(8,128)(2,1)S(1)} %pad_maximum_fusion.1.refs_0_), channel_id=1, source_target_pairs={{0,2},{2,0},{1,3},{3,1},{4,6},{6,4},{5,7},{7,5},{8,10},{10,8},{9,1... | collective-permute-start | bytes 1966088 | tf_op jit(solution)/shard_map/ppermute | solution.py:172
  14.1 24.2 %collective-permute-start = (bf16[512,640]{1,0:T(8,128)(2,1)S(1)}, bf16[512,640]{1,0:T(8,128)(2,1)}, u32[]{:S(2)}, u32[]{:S(2)}) collective-permute-start(bf16[512,640]{1,0:T(8,128)(2,1)S(1)} %pad_maximum_fusion.1.refs_0_), channel_id=1, source_target_pairs={{0,1},{1,0},{2,3},{3,2},{4,5},{5,4},{6,7},{7,6},{8,9},{9,8},{10,11... | collective-permute-start | bytes 1966088 | tf_op jit(solution)/shard_map/ppermute | solution.py:173
  24.0 14.3 %collective-permute-start.2 = (bf16[512,640]{1,0:T(8,128)(2,1)S(1)}, bf16[512,640]{1,0:T(8,128)(2,1)}, u32[]{:S(2)}, u32[]{:S(2)}) collective-permute-start(bf16[512,640]{1,0:T(8,128)(2,1)S(1)} %collective-permute-done.1.refs_2_), channel_id=1, source_target_pairs={{0,1},{1,0},{2,3},{3,2},{4,5},{5,4},{6,7},{7,6},{8,9},{9,8},{10,11... | collective-permute-start | bytes 1966088 | tf_op jit(solution)/shard_map/ppermute | solution.py:173
  32.1 30.1 %collective-permute-start.3 = (bf16[512,1024]{1,0:T(8,128)(2,1)S(1)}, bf16[512,1024]{1,0:T(8,128)(2,1)S(1)}, u32[]{:S(2)}, u32[]{:S(2)}) collective-permute-start(bf16[512,1024]{1,0:T(8,128)(2,1)S(1)} %pad_maximum_fusion), channel_id=1, source_target_pairs={{0,1},{1,0},{2,3},{3,2},{4,5},{5,4},{6,7},{7,6},{8,9},{9,8},{10,11... | collective-permute-start | bytes 3145736 | tf_op jit(solution)/shard_map/ppermute | solution.py:194
  41.4 20.4 %copy-start = (bf16[128,512]{1,0:T(8,128)(2,1)S(1)}, bf16[128,512]{1,0:T(8,128)(2,1)}, u32[]{:S(2)}) copy-start(bf16[128,512]{1,0:T(8,128)(2,1)} %target_ref.1) | copy-start | bytes 393220
  41.4 20.4 %copy-start.1 = (f32[128]{0:T(128)S(1)}, f32[128]{0:T(128)}, u32[]{:S(2)}) copy-start(f32[128]{0:T(128)} %param.15) | copy-start | bytes 1540
  75.9 58.8 %copy-start.8 = (s32[4]{0:T(128)S(1)}, s32[4]{0:T(128)}, u32[]{:S(2)}) copy-start(s32[4]{0:T(128)} %constant.37.clone) | copy-start | bytes 52
  121.7 10.8 %collective-permute-start.4 = (f32[128,128]{1,0:T(8,128)S(1)}, f32[128,128]{1,0:T(8,128)S(1)}, u32[]{:S(2)}, u32[]{:S(2)}) collective-permute-start(f32[128,128]{1,0:T(8,128)S(1)} %far_v.1.v_ref), channel_id=1, source_target_pairs={{0,64},{32,96},{64,0},{96,32},{1,65},{33,97},{65,1},{97,33},{2,66}... | collective-permute-start | bytes 196616 | tf_op jit(solution)/shard_map/ppermute | solution.py:227
  125.4 15.0 %all-to-all-start.5 = ((f32[16,32,128]{2,1,0:T(8,128)}), f32[16,32,128]{2,1,0:T(8,128)S(1)}, u32[]{:S(2)}, u32[]{:S(2)}) async-start(f32[16,32,128]{2,1,0:T(8,128)} %far_u.1), calls=%async_computation.5 | async-start | bytes 524288 | tf_op jit(solution)/shard_map/all_to_all | solution.py:30
  132.5 6.8 %collective-permute-start.5 = (f32[256,128]{1,0:T(8,128)S(1)}, f32[256,128]{1,0:T(8,128)S(1)}, u32[]{:S(2)}, u32[]{:S(2)}) collective-permute-start(f32[256,128]{1,0:T(8,128)S(1)} %pad_maximum_fusion.2.refs_0_), channel_id=1, source_target_pairs={{0,32},{32,0},{64,96},{96,64},{1,33},{33,1},{65,97},{97,65},{2,34}... | collective-permute-start | bytes 393224 | tf_op jit(solution)/shard_map/ppermute | solution.py:228

commit v10 on v9

--- a/solution.py
+++ b/solution.py
@@ -174,7 +174,8 @@
     wide = n_near * rows
     columns = lax.all_to_all(hidden.reshape(tok, n_x, wide), "x", 1, 1, tiled=True)
     tokens = columns.transpose(1, 0, 2).reshape(n_x * tok, wide)
-    u_quant = fake_quantize(u_factor, bits, u_exps).astype(jnp.bfloat16)
+    own, u_late = lax.optimization_barrier((own, u_factor))
+    u_quant = fake_quantize(u_late, bits, u_exps).astype(jnp.bfloat16)
 
     f32, bf16 = jnp.float32, jnp.bfloat16
     shape = jax.ShapeDtypeStruct

time: 142 us -> 148 us (1.042)
  blocking collectives: 78.9 us -> 58.3 us
  waiting for transfers between devices: 9.35 us -> 25.5 us
  starting transfers between devices: 40.7 us -> 45.4 us
  local copies, waits for them, and re-layouts: 3.32 us -> 5.28 us
  other arithmetic: 2.11 us -> 4.02 us
    all_to_all x4 -> x3, blocking collectives: 78.9 us -> 58.3 us  [exchange(): return lax.all_to_all(parts, axes, 0, 0, tiled=True)]
    all_to_all x1 -> x2, waiting for transfers between devices: 1.11 us -> 17.2 us  [exchange(): return lax.all_to_all(parts, axes, 0, 0, tiled=True)]
    all_to_all x1 -> x2, starting transfers between devices: 7.1 us -> 10.8 us  [exchange(): return lax.all_to_all(parts, axes, 0, 0, tiled=True)]
    unnamed x18, local copies, waits for them, and re-layouts: 0.05 us -> 2 us
  transfers between devices with their start and end apart: 8 -> 9, of which waited for: 3 -> 4; matrix products, arithmetic and copies ran while one was open for 2% -> 3% of each run, Pallas kernels for 3% -> 3%
where the time goes in v10:
time: 148 us; the launch traced here: 147 us
  blocking collectives  58.3 us (39%)
  starting transfers between devices  45.4 us (31%)
  waiting for transfers between devices  25.5 us (17%)
  Pallas kernels  7.72 us (5%)
  local copies, waits for them, and re-layouts  5.28 us (4%)
  other arithmetic  4.02 us (3%)
    all_to_all x3, blocking collectives, exchange(): return lax.all_to_all(parts, axes, 0, 0, tiled=True)  58.3 us
    all_to_all x2, waiting for transfers between devices, exchange(): return lax.all_to_all(parts, axes, 0, 0, tiled=True)  17.2 us
    all_to_all x2, starting transfers between devices, exchange(): return lax.all_to_all(parts, axes, 0, 0, tiled=True)  10.8 us
    ppermute x1, starting transfers between devices, shards(): lax.ppermute(across, 'core', swap)  7.83 us
    pallas_call x7, Pallas kernels, kernel_call(): pl.pallas_call(kernel, out_shape=out, in_specs=[IN_SMEM] * scalars + [IN_...  7.72 us
    ppermute x1, starting transfers between devices, shards(): others = lax.ppermute(jnp.concatenate(others, axis=1), 'core', swap)  7.17 us
    ppermute x1, starting transfers between devices, shards(): lax.ppermute(own, 'core', swap)  6.29 us
    all_to_all x1, starting transfers between devices, shards(): lax.all_to_all(hidden.reshape(tok, n_x, wide), 'x', 1, 1, tiled=True)  4.99 us
  transfers between devices with their start and end apart: 9, of which 4 were waited for; matrix products, arithmetic and copies ran while one was open for 3% of the time, Pallas kernels for 3%

profile of v10, /device:TPU:1, one launch (start us, length us, event | category | flops | bytes accessed | tf_op | source)
XLA Modules:
  0.0 147.0 jit_solution(2240319745629097687)
XLA Ops:
  0.6 3.2 %copy.15 = bf16[16,4,8,2048]{3,2,0,1:T(8,128)(2,1)} copy(bf16[16,4,8,2048]{3,2,1,0:T(8,128)(2,1)} %bitcast.16) | data formatting | bytes 4194304 | tf_op jit(solution)/shard_map/reshape | solution.py:175
  3.8 0.0 copy-start.5
  3.8 0.0 copy-start.6
  3.8 0.0 copy-start.4
  3.8 0.0 copy-start.3
  3.8 5.0 %all-to-all-start = ((bf16[128,4,2048]{2,0,1:T(8,128)(2,1)}), bf16[128,4,2048]{2,0,1:T(8,128)(2,1)S(1)}, u32[]{:S(2)}, u32[]{:S(2)}) async-start(bf16[128,4,2048]{2,0,1:T(8,128)(2,1)} %bitcast.15), calls=%async_computation | async-start | bytes 4194304 | tf_op jit(solution)/shard_map/all_to_all | solution.py:175
  8.8 0.0 copy-done.5
  8.8 0.0 copy-done.6
  8.8 0.0 copy-done.4
  8.8 0.9 multiply_convert_fusion.1
  9.7 0.0 copy-done.3
  9.8 0.1 pad_maximum_fusion.1.refs_0_
  9.8 3.2 %collective-permute-start.1 = (bf16[512,640]{1,0:T(8,128)(2,1)S(1)}, bf16[512,640]{1,0:T(8,128)(2,1)S(1)}, u32[]{:S(2)}, u32[]{:S(2)}) collective-permute-start(bf16[512,640]{1,0:T(8,128)(2,1)S(1)} %pad_maximum_fusion.1.refs_0_), channel_id=1, source_target_pairs={{0,2},{2,0},{1,3},{3,1},{4,6},{6,4},{5,7},{7,5},{8,10},{10,8},{9,1... | collective-permute-start | bytes 1966088 | tf_op jit(solution)/shard_map/ppermute | solution.py:172
  13.0 6.3 %collective-permute-start = (bf16[512,640]{1,0:T(8,128)(2,1)S(1)}, bf16[512,640]{1,0:T(8,128)(2,1)}, u32[]{:S(2)}, u32[]{:S(2)}) collective-permute-start(bf16[512,640]{1,0:T(8,128)(2,1)S(1)} %pad_maximum_fusion.1.refs_0_), channel_id=1, source_target_pairs={{0,1},{1,0},{2,3},{3,2},{4,5},{5,4},{6,7},{7,6},{8,9},{9,8},{10,11... | collective-permute-start | bytes 1966088 | tf_op jit(solution)/shard_map/ppermute | solution.py:173
  19.3 3.6 %collective-permute-done.1.refs_2_ = bf16[512,640]{1,0:T(8,128)(2,1)S(1)} collective-permute-done((bf16[512,640]{1,0:T(8,128)(2,1)S(1)}, bf16[512,640]{1,0:T(8,128)(2,1)S(1)}, u32[]{:S(2)}, u32[]{:S(2)}) %collective-permute-start.1) | collective-permute-done | bytes 655392 | tf_op jit(solution)/shard_map/ppermute | solution.py:172
  22.9 7.8 %collective-permute-start.2 = (bf16[512,640]{1,0:T(8,128)(2,1)S(1)}, bf16[512,640]{1,0:T(8,128)(2,1)}, u32[]{:S(2)}, u32[]{:S(2)}) collective-permute-start(bf16[512,640]{1,0:T(8,128)(2,1)S(1)} %collective-permute-done.1.refs_2_), channel_id=1, source_target_pairs={{0,1},{1,0},{2,3},{3,2},{4,5},{5,4},{6,7},{7,6},{8,9},{9,8},{10,11... | collective-permute-start | bytes 1966088 | tf_op jit(solution)/shard_map/ppermute | solution.py:173
  30.8 0.0 all-to-all-done
  30.8 0.1 constant_dynamic-slice_fusion.1
  30.9 1.1 pad_maximum_fusion
  32.0 7.2 %collective-permute-start.3 = (bf16[512,1024]{1,0:T(8,128)(2,1)}, bf16[512,1024]{1,0:T(8,128)(2,1)}, u32[]{:S(2)}, u32[]{:S(2)}) collective-permute-start(bf16[512,1024]{1,0:T(8,128)(2,1)} %pad_maximum_fusion), channel_id=1, source_target_pairs={{0,1},{1,0},{2,3},{3,2},{4,5},{5,4},{6,7},{7,6},{8,9},{9,8},{10,11... | collective-permute-start | bytes 3145736 | tf_op jit(solution)/shard_map/ppermute | solution.py:195
  39.2 0.0 collective-permute-done.refs_1_
  39.2 0.0 collective-permute-done.2.refs_3_
  39.3 3.1 %partial_products.1 = f32[4,128,640]{2,1,0:T(8,128)S(1)} custom-call(s32[4]{0:T(128)S(1)} %iota_xor_fusion.order_ref, bf16[512,2048]{1,0:T(8,128)(2,1)S(1)} %bitcast.11, bf16[512,640]{1,0:T(8,128)(2,1)S(1)} %pad_maximum_fusion.1.refs_0_, bf16[512,640]{1,0:T(8,128)(2,1)} %collective-permute-done.refs_1_, bf16[512,640]{1,0:T(8,128)(2,1)S(1)} %collective-permute-done.1.refs_2_, ...), custom_call_target="tpu_custom_call" | custom-call | tf_op jit(solution)/shard_map/partial_products/pallas_call | solution.py:152
  42.4 0.0 copy-start
  42.4 1.1 copy-done
  43.4 0.0 copy-start.7
  43.5 0.0 copy-start.2
  43.5 3.7 %all-to-all-start.1 = ((f32[4,128,640]{2,1,0:T(8,128)}), f32[4,128,640]{2,1,0:T(8,128)S(1)}, u32[]{:S(2)}, u32[]{:S(2)}) async-start(f32[4,128,640]{2,1,0:T(8,128)} %copy-done), calls=%async_computation.1 | async-start | bytes 2621440 | tf_op jit(solution)/shard_map/all_to_all | solution.py:30
  47.1 0.0 copy-done.7
  47.2 1.9 %multiply_convert_fusion.u_ref = bf16[512,128]{1,0:T(8,128)(2,1)S(1)} fusion(f32[512,128]{1,0:T(8,128)} %param.14, f32[128]{0:T(128)S(1)} %multiply_exponential_fusion, f32[128]{0:T(128)S(1)} %get-tuple-element.11, f32[128]{0:T(128)S(1)} %get-tuple-element.10), kind=kLoop, calls=%fused_computation.3 | loop fusion | flops 524288 | bytes 394752 | tf_op jit(solution)/shard_map/convert_element_type | solution.py:178
  49.0 16.1 %all-to-all-done.1.parts_ref = f32[4,128,640]{2,1,0:T(8,128)S(1)} async-done(((f32[4,128,640]{2,1,0:T(8,128)}), f32[4,128,640]{2,1,0:T(8,128)S(1)}, u32[]{:S(2)}, u32[]{:S(2)}) %all-to-all-start.1) | async-done | bytes 1310752 | tf_op jit(solution)/shard_map/all_to_all | solution.py:30
  65.2 0.0 copy-done.2
  65.2 0.0 copy-start.1
  65.2 0.9 copy-done.1
  66.1 0.4 residual_and_grad_u.1
  66.5 0.0 collective-permute-done.3.others_ref
  66.5 12.6 %all_to_all.30.arrived_ref = bf16[8,256,128]{2,1,0:T(8,128)(2,1)S(1)} all-to-all(bf16[8,256,128]{2,1,0:T(8,128)(2,1)S(1)} %residual_and_grad_u.1), channel_id=1, replica_groups=mesh['z1'=4,'z0'=4,'yh'=2,'x'=4,'yl'=2,'core'=2] {'x','core'}, dimensions={0} | all-to-all | bytes 1048576 | tf_op jit(solution)/shard_map/all_to_all | solution.py:30
  79.1 2.0 %grads_packed.1 = bf16[16,80,128]{2,1,0:T(8,128)(2,1)S(1)} custom-call(s32[1]{0:T(128)} %bitcast.core_ref, bf16[512,2048]{1,0:T(8,128)(2,1)S(1)} %bitcast.12, bf16[512,1024]{1,0:T(8,128)(2,1)} %collective-permute-done.3.others_ref, bf16[8,256,128]{2,1,0:T(8,128)(2,1)S(1)} %all_to_all.30.arrived_ref), custom_call_target="tpu_custom_call" | custom-call | tf_op jit(solution)/shard_map/grads_packed/pallas_call | solution.py:152
  81.1 0.0 copy-start.8
  81.1 19.6 %all_to_all.31.arrived_ref = bf16[16,80,128]{2,1,0:T(8,128)(2,1)S(1)} all-to-all(bf16[16,80,128]{2,1,0:T(8,128)(2,1)S(1)} %grads_packed.1), channel_id=1, replica_groups=mesh['z1'=4,'z0'=4,'yh'=2,'x'=4,'yl'=2,'core'=2] {'yl','yh','z0'}, dimensions={0} | all-to-all | bytes 655360 | tf_op jit(solution)/shard_map/all_to_all | solution.py:30
  100.7 0.1 close_sum.1
  100.7 26.2 %all_to_all.32.arrived_ref = bf16[8,80,128]{2,1,0:T(8,128)(2,1)S(1)} all-to-all(bf16[8,80,128]{2,1,0:T(8,128)(2,1)S(1)} %close_sum.1), channel_id=1, replica_groups=mesh['z1'=4,'z0'=4,'yh'=2,'x'=4,'yl'=2,'core'=2] {'z1','yh'}, dimensions={0} | all-to-all | bytes 327680 | tf_op jit(solution)/shard_map/all_to_all | solution.py:30
  126.9 3.0 %collective-permute-start.4 = (f32[128,128]{1,0:T(8,128)S(1)}, f32[128,128]{1,0:T(8,128)S(1)}, u32[]{:S(2)}, u32[]{:S(2)}) collective-permute-start(f32[128,128]{1,0:T(8,128)S(1)} %far_v.1.v_ref), channel_id=1, source_target_pairs={{0,64},{32,96},{64,0},{96,32},{1,65},{33,97},{65,1},{97,33},{2,66}... | collective-permute-start | bytes 196616 | tf_op jit(solution)/shard_map/ppermute | solution.py:228
  129.9 0.7 far_u.1
  130.6 7.1 %all-to-all-start.5 = ((f32[16,32,128]{2,1,0:T(8,128)}), f32[16,32,128]{2,1,0:T(8,128)S(1)}, u32[]{:S(2)}, u32[]{:S(2)}) async-start(f32[16,32,128]{2,1,0:T(8,128)} %far_u.1), calls=%async_computation.5 | async-start | bytes 524288 | tf_op jit(solution)/shard_map/all_to_all | solution.py:30
  137.7 0.0 collective-permute-done.4
  137.8 2.1 %collective-permute-start.5 = (f32[256,128]{1,0:T(8,128)S(1)}, f32[256,128]{1,0:T(8,128)S(1)}, u32[]{:S(2)}, u32[]{:S(2)}) collective-permute-start(f32[256,128]{1,0:T(8,128)S(1)} %pad_maximum_fusion.2.refs_0_), channel_id=1, source_target_pairs={{0,32},{32,0},{64,96},{96,64},{1,33},{33,1},{65,97},{97,65},{2,34}... | collective-permute-start | bytes 393224 | tf_op jit(solution)/shard_map/ppermute | solution.py:229
  139.9 0.0 copy-done.8
  139.9 4.6 %collective-permute-done.5.refs_1_ = f32[256,128]{1,0:T(8,128)S(1)} collective-permute-done((f32[256,128]{1,0:T(8,128)S(1)}, f32[256,128]{1,0:T(8,128)S(1)}, u32[]{:S(2)}, u32[]{:S(2)}) %collective-permute-start.5) | collective-permute-done | bytes 131104 | tf_op jit(solution)/shard_map/ppermute | solution.py:229
  144.5 1.1 all-to-all-done.5
  145.7 1.4 grads.1
  (6 shorter events, 0.1 us)
Async XLA Ops:
  3.8 5.0 %copy-start.5 = (s32[128]{0:T(128)S(1)}, s32[128]{0:T(128)}, u32[]{:S(2)}) copy-start(s32[128]{0:T(128)} %param.16) | copy-start | bytes 1540
  3.8 5.0 %copy-start.6 = (s32[128]{0:T(128)S(1)}, s32[128]{0:T(128)}, u32[]{:S(2)}) copy-start(s32[128]{0:T(128)} %param.17) | copy-start | bytes 1540
  3.8 5.0 %copy-start.4 = (f32[512,128]{1,0:T(8,128)S(1)}, f32[512,128]{1,0:T(8,128)}, u32[]{:S(2)}) copy-start(f32[512,128]{1,0:T(8,128)} %param.13) | copy-start | bytes 786436
  3.8 5.9 %copy-start.3 = (bf16[512,512]{1,0:T(8,128)(2,1)S(1)}, bf16[512,512]{1,0:T(8,128)(2,1)}, u32[]{:S(2)}) copy-start(bf16[512,512]{1,0:T(8,128)(2,1)} %param.12) | copy-start | bytes 1572868
  3.8 27.0 %all-to-all-start = ((bf16[128,4,2048]{2,0,1:T(8,128)(2,1)}), bf16[128,4,2048]{2,0,1:T(8,128)(2,1)S(1)}, u32[]{:S(2)}, u32[]{:S(2)}) async-start(bf16[128,4,2048]{2,0,1:T(8,128)(2,1)} %bitcast.15), calls=%async_computation | async-start | bytes 4194304 | tf_op jit(solution)/shard_map/all_to_all | solution.py:175
  9.8 13.1 %collective-permute-start.1 = (bf16[512,640]{1,0:T(8,128)(2,1)S(1)}, bf16[512,640]{1,0:T(8,128)(2,1)S(1)}, u32[]{:S(2)}, u32[]{:S(2)}) collective-permute-start(bf16[512,640]{1,0:T(8,128)(2,1)S(1)} %pad_maximum_fusion.1.refs_0_), channel_id=1, source_target_pairs={{0,2},{2,0},{1,3},{3,1},{4,6},{6,4},{5,7},{7,5},{8,10},{10,8},{9,1... | collective-permute-start | bytes 1966088 | tf_op jit(solution)/shard_map/ppermute | solution.py:172
  13.0 26.2 %collective-permute-start = (bf16[512,640]{1,0:T(8,128)(2,1)S(1)}, bf16[512,640]{1,0:T(8,128)(2,1)}, u32[]{:S(2)}, u32[]{:S(2)}) collective-permute-start(bf16[512,640]{1,0:T(8,128)(2,1)S(1)} %pad_maximum_fusion.1.refs_0_), channel_id=1, source_target_pairs={{0,1},{1,0},{2,3},{3,2},{4,5},{5,4},{6,7},{7,6},{8,9},{9,8},{10,11... | collective-permute-start | bytes 1966088 | tf_op jit(solution)/shard_map/ppermute | solution.py:173
  22.9 16.3 %collective-permute-start.2 = (bf16[512,640]{1,0:T(8,128)(2,1)S(1)}, bf16[512,640]{1,0:T(8,128)(2,1)}, u32[]{:S(2)}, u32[]{:S(2)}) collective-permute-start(bf16[512,640]{1,0:T(8,128)(2,1)S(1)} %collective-permute-done.1.refs_2_), channel_id=1, source_target_pairs={{0,1},{1,0},{2,3},{3,2},{4,5},{5,4},{6,7},{7,6},{8,9},{9,8},{10,11... | collective-permute-start | bytes 1966088 | tf_op jit(solution)/shard_map/ppermute | solution.py:173
  32.0 34.5 %collective-permute-start.3 = (bf16[512,1024]{1,0:T(8,128)(2,1)}, bf16[512,1024]{1,0:T(8,128)(2,1)}, u32[]{:S(2)}, u32[]{:S(2)}) collective-permute-start(bf16[512,1024]{1,0:T(8,128)(2,1)} %pad_maximum_fusion), channel_id=1, source_target_pairs={{0,1},{1,0},{2,3},{3,2},{4,5},{5,4},{6,7},{7,6},{8,9},{9,8},{10,11... | collective-permute-start | bytes 3145736 | tf_op jit(solution)/shard_map/ppermute | solution.py:195
  42.4 1.1 copy-start
  43.4 3.7 %copy-start.7 = (s32[128]{0:T(128)S(1)}, s32[128]{0:T(128)}, u32[]{:S(2)}) copy-start(s32[128]{0:T(128)} %param.18) | copy-start | bytes 1540
  43.5 21.7 %copy-start.2 = (f32[128]{0:T(128)S(1)}, f32[128]{0:T(128)}, u32[]{:S(2)}) copy-start(f32[128]{0:T(128)} %param.15) | copy-start | bytes 1540
  43.5 21.7 %all-to-all-start.1 = ((f32[4,128,640]{2,1,0:T(8,128)}), f32[4,128,640]{2,1,0:T(8,128)S(1)}, u32[]{:S(2)}, u32[]{:S(2)}) async-start(f32[4,128,640]{2,1,0:T(8,128)} %copy-done), calls=%async_computation.1 | async-start | bytes 2621440 | tf_op jit(solution)/shard_map/all_to_all | solution.py:30
  65.2 0.9 copy-start.1
  81.1 58.8 %copy-start.8 = (s32[4]{0:T(128)S(1)}, s32[4]{0:T(128)}, u32[]{:S(2)}) copy-start(s32[4]{0:T(128)} %constant.37.clone) | copy-start | bytes 52
  126.9 10.8 %collective-permute-start.4 = (f32[128,128]{1,0:T(8,128)S(1)}, f32[128,128]{1,0:T(8,128)S(1)}, u32[]{:S(2)}, u32[]{:S(2)}) collective-permute-start(f32[128,128]{1,0:T(8,128)S(1)} %far_v.1.v_ref), channel_id=1, source_target_pairs={{0,64},{32,96},{64,0},{96,32},{1,65},{33,97},{65,1},{97,33},{2,66}... | collective-permute-start | bytes 196616 | tf_op jit(solution)/shard_map/ppermute | solution.py:228
  130.6 15.0 %all-to-all-start.5 = ((f32[16,32,128]{2,1,0:T(8,128)}), f32[16,32,128]{2,1,0:T(8,128)S(1)}, u32[]{:S(2)}, u32[]{:S(2)}) async-start(f32[16,32,128]{2,1,0:T(8,128)} %far_u.1), calls=%async_computation.5 | async-start | bytes 524288 | tf_op jit(solution)/shard_map/all_to_all | solution.py:30
  137.8 6.8 %collective-permute-start.5 = (f32[256,128]{1,0:T(8,128)S(1)}, f32[256,128]{1,0:T(8,128)S(1)}, u32[]{:S(2)}, u32[]{:S(2)}) collective-permute-start(f32[256,128]{1,0:T(8,128)S(1)} %pad_maximum_fusion.2.refs_0_), channel_id=1, source_target_pairs={{0,32},{32,0},{64,96},{96,64},{1,33},{33,1},{65,97},{97,65},{2,34}... | collective-permute-start | bytes 393224 | tf_op jit(solution)/shard_map/ppermute | solution.py:229

commit v11 on v10

--- a/solution.py
+++ b/solution.py
@@ -180,6 +180,7 @@
     f32, bf16 = jnp.float32, jnp.bfloat16
     shape = jax.ShapeDtypeStruct
     order = jnp.bitwise_xor(me, jnp.arange(n_near, dtype=jnp.int32))
+    order, u_quant = lax.optimization_barrier((order, u_quant))
     part = kernel_call(
         partial_kernel,
         shape((n_x, tok, kvw + rank), f32),

time: 148 us -> 142 us (0.959)
  blocking collectives: 58.3 us -> 78.9 us
  waiting for transfers between devices: 25.5 us -> 9.34 us
  starting transfers between devices: 45.4 us -> 39.8 us
  local copies, waits for them, and re-layouts: 5.28 us -> 3.34 us
    all_to_all x3 -> x4, blocking collectives: 58.3 us -> 78.9 us  [exchange(): return lax.all_to_all(parts, axes, 0, 0, tiled=True)]
    all_to_all x2 -> x1, waiting for transfers between devices: 17.2 us -> 1.11 us  [exchange(): return lax.all_to_all(parts, axes, 0, 0, tiled=True)]
    all_to_all x2 -> x1, starting transfers between devices: 10.8 us -> 7.1 us  [exchange(): return lax.all_to_all(parts, axes, 0, 0, tiled=True)]
    unnamed x18 -> x16, local copies, waits for them, and re-layouts: 2 us -> 0.04 us
    ppermute x1, starting transfers between devices: 7.17 us -> 5.28 us  [shards(): others = lax.ppermute(jnp.concatenate(others, axis=1), 'core', swap)]
  transfers between devices with their start and end apart: 9 -> 8, of which waited for: 4 -> 3; matrix products, arithmetic and copies ran while one was open for 3% -> 2% of each run, Pallas kernels for 3% -> 3%
where the time goes in v11:
time: 142 us
  blocking collectives  78.9 us (56%)
  starting transfers between devices  39.8 us (28%)
  waiting for transfers between devices  9.34 us (7%)
  Pallas kernels  6.47 us (5%)
  local copies, waits for them, and re-layouts  3.34 us (2%)
  other arithmetic  3.03 us (2%)
    all_to_all x4, blocking collectives, exchange(): return lax.all_to_all(parts, axes, 0, 0, tiled=True)  78.9 us
    ppermute x1, starting transfers between devices, shards(): lax.ppermute(across, 'core', swap)  7.83 us
    all_to_all x1, starting transfers between devices, exchange(): return lax.all_to_all(parts, axes, 0, 0, tiled=True)  7.1 us
    pallas_call x7, Pallas kernels, kernel_call(): pl.pallas_call(kernel, out_shape=out, in_specs=[IN_SMEM] * scalars + [IN_...  6.47 us
    ppermute x1, starting transfers between devices, shards(): lax.ppermute(own, 'core', swap)  6.29 us
    ppermute x1, starting transfers between devices, shards(): others = lax.ppermute(jnp.concatenate(others, axis=1), 'core', swap)  5.28 us
    all_to_all x1, starting transfers between devices, shards(): lax.all_to_all(hidden.reshape(tok, n_x, wide), 'x', 1, 1, tiled=True)  4.99 us
    ppermute x1, waiting for transfers between devices, shards(): v_pieces = [v_two, lax.ppermute(v_two, 'z0', flips(n_z0, 1))]  4.63 us
  transfers between devices with their start and end apart: 8, of which 3 were waited for; matrix products, arithmetic and copies ran while one was open for 2% of the time, Pallas kernels for 3%

profile of v11, /device:TPU:1, one launch (start us, length us, event | category | flops | bytes accessed | tf_op | source)
XLA Modules:
  0.0 141.8 jit_solution(315231538894944245)
XLA Ops:
  0.6 3.2 %copy.15 = bf16[16,4,8,2048]{3,2,0,1:T(8,128)(2,1)} copy(bf16[16,4,8,2048]{3,2,1,0:T(8,128)(2,1)} %bitcast.16) | data formatting | bytes 4194304 | tf_op jit(solution)/shard_map/reshape | solution.py:175
  3.8 0.0 copy-start.4
  3.8 0.0 copy-start.5
  3.8 0.0 copy-start.3
  3.8 0.0 copy-start.2
  3.8 0.0 copy-start.6
  3.8 5.0 %all-to-all-start = ((bf16[128,4,2048]{2,0,1:T(8,128)(2,1)}), bf16[128,4,2048]{2,0,1:T(8,128)(2,1)S(1)}, u32[]{:S(2)}, u32[]{:S(2)}) async-start(bf16[128,4,2048]{2,0,1:T(8,128)(2,1)} %bitcast.15), calls=%async_computation | async-start | bytes 4194304 | tf_op jit(solution)/shard_map/all_to_all | solution.py:175
  8.8 0.0 copy-done.4
  8.8 0.0 copy-done.5
  8.8 0.0 copy-done.3
  8.8 0.9 multiply_convert_fusion.1
  9.8 0.0 copy-done.2
  9.8 0.1 pad_maximum_fusion.1.refs_0_
  9.9 3.2 %collective-permute-start.1 = (bf16[512,640]{1,0:T(8,128)(2,1)S(1)}, bf16[512,640]{1,0:T(8,128)(2,1)S(1)}, u32[]{:S(2)}, u32[]{:S(2)}) collective-permute-start(bf16[512,640]{1,0:T(8,128)(2,1)S(1)} %pad_maximum_fusion.1.refs_0_), channel_id=1, source_target_pairs={{0,2},{2,0},{1,3},{3,1},{4,6},{6,4},{5,7},{7,5},{8,10},{10,8},{9,1... | collective-permute-start | bytes 1966088 | tf_op jit(solution)/shard_map/ppermute | solution.py:172
  13.1 6.3 %collective-permute-start = (bf16[512,640]{1,0:T(8,128)(2,1)S(1)}, bf16[512,640]{1,0:T(8,128)(2,1)}, u32[]{:S(2)}, u32[]{:S(2)}) collective-permute-start(bf16[512,640]{1,0:T(8,128)(2,1)S(1)} %pad_maximum_fusion.1.refs_0_), channel_id=1, source_target_pairs={{0,1},{1,0},{2,3},{3,2},{4,5},{5,4},{6,7},{7,6},{8,9},{9,8},{10,11... | collective-permute-start | bytes 1966088 | tf_op jit(solution)/shard_map/ppermute | solution.py:173
  19.4 3.6 %collective-permute-done.1.refs_2_ = bf16[512,640]{1,0:T(8,128)(2,1)S(1)} collective-permute-done((bf16[512,640]{1,0:T(8,128)(2,1)S(1)}, bf16[512,640]{1,0:T(8,128)(2,1)S(1)}, u32[]{:S(2)}, u32[]{:S(2)}) %collective-permute-start.1) | collective-permute-done | bytes 655392 | tf_op jit(solution)/shard_map/ppermute | solution.py:172
  23.0 7.8 %collective-permute-start.2 = (bf16[512,640]{1,0:T(8,128)(2,1)S(1)}, bf16[512,640]{1,0:T(8,128)(2,1)}, u32[]{:S(2)}, u32[]{:S(2)}) collective-permute-start(bf16[512,640]{1,0:T(8,128)(2,1)S(1)} %collective-permute-done.1.refs_2_), channel_id=1, source_target_pairs={{0,1},{1,0},{2,3},{3,2},{4,5},{5,4},{6,7},{7,6},{8,9},{9,8},{10,11... | collective-permute-start | bytes 1966088 | tf_op jit(solution)/shard_map/ppermute | solution.py:173
  30.8 0.0 copy-done.6
  30.8 1.9 %multiply_convert_fusion.u_ref = bf16[512,128]{1,0:T(8,128)(2,1)S(1)} fusion(f32[512,128]{1,0:T(8,128)} %param.14, f32[128]{0:T(128)S(1)} %get-tuple-element.15, f32[128]{0:T(128)S(1)} %get-tuple-element.14, f32[128]{0:T(128)S(1)} %multiply_exponential_fusion.2), kind=kLoop, calls=%fused_computation.3 | loop fusion | flops 524288 | bytes 394752 | tf_op jit(solution)/shard_map/convert_element_type | solution.py:178
  32.7 0.0 all-to-all-done
  32.7 0.1 constant_dynamic-slice_fusion.1
  32.8 0.1 pad_maximum_fusion
  33.0 5.3 %collective-permute-start.3 = (bf16[512,1024]{1,0:T(8,128)(2,1)S(1)}, bf16[512,1024]{1,0:T(8,128)(2,1)S(1)}, u32[]{:S(2)}, u32[]{:S(2)}) collective-permute-start(bf16[512,1024]{1,0:T(8,128)(2,1)S(1)} %pad_maximum_fusion), channel_id=1, source_target_pairs={{0,1},{1,0},{2,3},{3,2},{4,5},{5,4},{6,7},{7,6},{8,9},{9,8},{10,11... | collective-permute-start | bytes 3145736 | tf_op jit(solution)/shard_map/ppermute | solution.py:196
  38.3 0.0 collective-permute-done.refs_1_
  38.3 0.0 collective-permute-done.2.refs_3_
  38.3 3.1 %partial_products.1 = f32[4,128,640]{2,1,0:T(8,128)S(1)} custom-call(s32[4]{0:T(128)S(1)} %iota_xor_fusion.order_ref, bf16[512,2048]{1,0:T(8,128)(2,1)S(1)} %bitcast.11, bf16[512,640]{1,0:T(8,128)(2,1)S(1)} %pad_maximum_fusion.1.refs_0_, bf16[512,640]{1,0:T(8,128)(2,1)} %collective-permute-done.refs_1_, bf16[512,640]{1,0:T(8,128)(2,1)S(1)} %collective-permute-done.1.refs_2_, ...), custom_call_target="tpu_custom_call" | custom-call | tf_op jit(solution)/shard_map/partial_products/pallas_call | solution.py:152
  41.4 0.0 copy-start
  41.4 0.0 copy-start.1
  41.5 20.3 %all_to_all.30.parts_ref = f32[4,128,640]{2,1,0:T(8,128)S(1)} all-to-all(f32[4,128,640]{2,1,0:T(8,128)S(1)} %partial_products.1), channel_id=1, replica_groups=mesh['z1'=4,'z0'=4,'yh'=2,'x'=4,'yl'=2,'core'=2] {'x'}, dimensions={0} | all-to-all | bytes 2621440 | tf_op jit(solution)/shard_map/all_to_all | solution.py:30
  61.8 0.0 copy-done
  61.8 0.0 copy-done.1
  61.8 0.4 residual_and_grad_u.1
  62.2 0.0 collective-permute-done.3.others_ref
  62.2 12.8 %all_to_all.31.arrived_ref = bf16[8,256,128]{2,1,0:T(8,128)(2,1)S(1)} all-to-all(bf16[8,256,128]{2,1,0:T(8,128)(2,1)S(1)} %residual_and_grad_u.1), channel_id=1, replica_groups=mesh['z1'=4,'z0'=4,'yh'=2,'x'=4,'yl'=2,'core'=2] {'x','core'}, dimensions={0} | all-to-all | bytes 1048576 | tf_op jit(solution)/shard_map/all_to_all | solution.py:30
  75.1 0.8 grads_packed.1
  75.9 0.0 copy-start.7
  75.9 19.6 %all_to_all.32.arrived_ref = bf16[16,80,128]{2,1,0:T(8,128)(2,1)S(1)} all-to-all(bf16[16,80,128]{2,1,0:T(8,128)(2,1)S(1)} %grads_packed.1), channel_id=1, replica_groups=mesh['z1'=4,'z0'=4,'yh'=2,'x'=4,'yl'=2,'core'=2] {'yl','yh','z0'}, dimensions={0} | all-to-all | bytes 655360 | tf_op jit(solution)/shard_map/all_to_all | solution.py:30
  95.4 0.1 close_sum.1
  95.5 26.2 %all_to_all.33.arrived_ref = bf16[8,80,128]{2,1,0:T(8,128)(2,1)S(1)} all-to-all(bf16[8,80,128]{2,1,0:T(8,128)(2,1)S(1)} %close_sum.1), channel_id=1, replica_groups=mesh['z1'=4,'z0'=4,'yh'=2,'x'=4,'yl'=2,'core'=2] {'z1','yh'}, dimensions={0} | all-to-all | bytes 327680 | tf_op jit(solution)/shard_map/all_to_all | solution.py:30
  121.7 3.0 %collective-permute-start.4 = (f32[128,128]{1,0:T(8,128)S(1)}, f32[128,128]{1,0:T(8,128)S(1)}, u32[]{:S(2)}, u32[]{:S(2)}) collective-permute-start(f32[128,128]{1,0:T(8,128)S(1)} %far_v.1.v_ref), channel_id=1, source_target_pairs={{0,64},{32,96},{64,0},{96,32},{1,65},{33,97},{65,1},{97,33},{2,66}... | collective-permute-start | bytes 196616 | tf_op jit(solution)/shard_map/ppermute | solution.py:229
  124.7 0.7 far_u.1
  125.4 7.1 %all-to-all-start.5 = ((f32[16,32,128]{2,1,0:T(8,128)}), f32[16,32,128]{2,1,0:T(8,128)S(1)}, u32[]{:S(2)}, u32[]{:S(2)}) async-start(f32[16,32,128]{2,1,0:T(8,128)} %far_u.1), calls=%async_computation.5 | async-start | bytes 524288 | tf_op jit(solution)/shard_map/all_to_all | solution.py:30
  132.5 0.0 collective-permute-done.4
  132.5 2.1 %collective-permute-start.5 = (f32[256,128]{1,0:T(8,128)S(1)}, f32[256,128]{1,0:T(8,128)S(1)}, u32[]{:S(2)}, u32[]{:S(2)}) collective-permute-start(f32[256,128]{1,0:T(8,128)S(1)} %pad_maximum_fusion.2.refs_0_), channel_id=1, source_target_pairs={{0,32},{32,0},{64,96},{96,64},{1,33},{33,1},{65,97},{97,65},{2,34}... | collective-permute-start | bytes 393224 | tf_op jit(solution)/shard_map/ppermute | solution.py:230
  134.7 0.0 copy-done.7
  134.7 4.6 %collective-permute-done.5.refs_1_ = f32[256,128]{1,0:T(8,128)S(1)} collective-permute-done((f32[256,128]{1,0:T(8,128)S(1)}, f32[256,128]{1,0:T(8,128)S(1)}, u32[]{:S(2)}, u32[]{:S(2)}) %collective-permute-start.5) | collective-permute-done | bytes 131104 | tf_op jit(solution)/shard_map/ppermute | solution.py:230
  139.3 1.1 all-to-all-done.5
  140.4 1.4 grads.1
  (6 shorter events, 0.1 us)
Async XLA Ops:
  3.8 5.0 %copy-start.4 = (s32[128]{0:T(128)S(1)}, s32[128]{0:T(128)}, u32[]{:S(2)}) copy-start(s32[128]{0:T(128)} %param.16) | copy-start | bytes 1540
  3.8 5.0 %copy-start.5 = (s32[128]{0:T(128)S(1)}, s32[128]{0:T(128)}, u32[]{:S(2)}) copy-start(s32[128]{0:T(128)} %param.17) | copy-start | bytes 1540
  3.8 5.0 %copy-start.3 = (f32[512,128]{1,0:T(8,128)S(1)}, f32[512,128]{1,0:T(8,128)}, u32[]{:S(2)}) copy-start(f32[512,128]{1,0:T(8,128)} %param.13) | copy-start | bytes 786436
  3.8 6.0 %copy-start.2 = (bf16[512,512]{1,0:T(8,128)(2,1)S(1)}, bf16[512,512]{1,0:T(8,128)(2,1)}, u32[]{:S(2)}) copy-start(bf16[512,512]{1,0:T(8,128)(2,1)} %param.12) | copy-start | bytes 1572868
  3.8 27.0 %copy-start.6 = (s32[128]{0:T(128)S(1)}, s32[128]{0:T(128)}, u32[]{:S(2)}) copy-start(s32[128]{0:T(128)} %param.18) | copy-start | bytes 1540
  3.8 28.9 %all-to-all-start = ((bf16[128,4,2048]{2,0,1:T(8,128)(2,1)}), bf16[128,4,2048]{2,0,1:T(8,128)(2,1)S(1)}, u32[]{:S(2)}, u32[]{:S(2)}) async-start(bf16[128,4,2048]{2,0,1:T(8,128)(2,1)} %bitcast.15), calls=%async_computation | async-start | bytes 4194304 | tf_op jit(solution)/shard_map/all_to_all | solution.py:175
  9.9 13.1 %collective-permute-start.1 = (bf16[512,640]{1,0:T(8,128)(2,1)S(1)}, bf16[512,640]{1,0:T(8,128)(2,1)S(1)}, u32[]{:S(2)}, u32[]{:S(2)}) collective-permute-start(bf16[512,640]{1,0:T(8,128)(2,1)S(1)} %pad_maximum_fusion.1.refs_0_), channel_id=1, source_target_pairs={{0,2},{2,0},{1,3},{3,1},{4,6},{6,4},{5,7},{7,5},{8,10},{10,8},{9,1... | collective-permute-start | bytes 1966088 | tf_op jit(solution)/shard_map/ppermute | solution.py:172
  13.1 25.2 %collective-permute-start = (bf16[512,640]{1,0:T(8,128)(2,1)S(1)}, bf16[512,640]{1,0:T(8,128)(2,1)}, u32[]{:S(2)}, u32[]{:S(2)}) collective-permute-start(bf16[512,640]{1,0:T(8,128)(2,1)S(1)} %pad_maximum_fusion.1.refs_0_), channel_id=1, source_target_pairs={{0,1},{1,0},{2,3},{3,2},{4,5},{5,4},{6,7},{7,6},{8,9},{9,8},{10,11... | collective-permute-start | bytes 1966088 | tf_op jit(solution)/shard_map/ppermute | solution.py:173
  23.0 15.3 %collective-permute-start.2 = (bf16[512,640]{1,0:T(8,128)(2,1)S(1)}, bf16[512,640]{1,0:T(8,128)(2,1)}, u32[]{:S(2)}, u32[]{:S(2)}) collective-permute-start(bf16[512,640]{1,0:T(8,128)(2,1)S(1)} %collective-permute-done.1.refs_2_), channel_id=1, source_target_pairs={{0,1},{1,0},{2,3},{3,2},{4,5},{5,4},{6,7},{7,6},{8,9},{9,8},{10,11... | collective-permute-start | bytes 1966088 | tf_op jit(solution)/shard_map/ppermute | solution.py:173
  33.0 29.2 %collective-permute-start.3 = (bf16[512,1024]{1,0:T(8,128)(2,1)S(1)}, bf16[512,1024]{1,0:T(8,128)(2,1)S(1)}, u32[]{:S(2)}, u32[]{:S(2)}) collective-permute-start(bf16[512,1024]{1,0:T(8,128)(2,1)S(1)} %pad_maximum_fusion), channel_id=1, source_target_pairs={{0,1},{1,0},{2,3},{3,2},{4,5},{5,4},{6,7},{7,6},{8,9},{9,8},{10,11... | collective-permute-start | bytes 3145736 | tf_op jit(solution)/shard_map/ppermute | solution.py:196
  41.4 20.4 %copy-start = (bf16[128,512]{1,0:T(8,128)(2,1)S(1)}, bf16[128,512]{1,0:T(8,128)(2,1)}, u32[]{:S(2)}) copy-start(bf16[128,512]{1,0:T(8,128)(2,1)} %target_ref.1) | copy-start | bytes 393220
  41.4 20.4 %copy-start.1 = (f32[128]{0:T(128)S(1)}, f32[128]{0:T(128)}, u32[]{:S(2)}) copy-start(f32[128]{0:T(128)} %param.15) | copy-start | bytes 1540
  75.9 58.8 %copy-start.7 = (s32[4]{0:T(128)S(1)}, s32[4]{0:T(128)}, u32[]{:S(2)}) copy-start(s32[4]{0:T(128)} %constant.37.clone) | copy-start | bytes 52
  121.7 10.8 %collective-permute-start.4 = (f32[128,128]{1,0:T(8,128)S(1)}, f32[128,128]{1,0:T(8,128)S(1)}, u32[]{:S(2)}, u32[]{:S(2)}) collective-permute-start(f32[128,128]{1,0:T(8,128)S(1)} %far_v.1.v_ref), channel_id=1, source_target_pairs={{0,64},{32,96},{64,0},{96,32},{1,65},{33,97},{65,1},{97,33},{2,66}... | collective-permute-start | bytes 196616 | tf_op jit(solution)/shard_map/ppermute | solution.py:229
  125.4 15.0 %all-to-all-start.5 = ((f32[16,32,128]{2,1,0:T(8,128)}), f32[16,32,128]{2,1,0:T(8,128)S(1)}, u32[]{:S(2)}, u32[]{:S(2)}) async-start(f32[16,32,128]{2,1,0:T(8,128)} %far_u.1), calls=%async_computation.5 | async-start | bytes 524288 | tf_op jit(solution)/shard_map/all_to_all | solution.py:30
  132.5 6.8 %collective-permute-start.5 = (f32[256,128]{1,0:T(8,128)S(1)}, f32[256,128]{1,0:T(8,128)S(1)}, u32[]{:S(2)}, u32[]{:S(2)}) collective-permute-start(f32[256,128]{1,0:T(8,128)S(1)} %pad_maximum_fusion.2.refs_0_), channel_id=1, source_target_pairs={{0,32},{32,0},{64,96},{96,64},{1,33},{33,1},{65,97},{97,65},{2,34}... | collective-permute-start | bytes 393224 | tf_op jit(solution)/shard_map/ppermute | solution.py:230
